TPU v7x, 32 devices: a whole 2x2x4 slice. The times are simulated.
32 devices in a mesh: grp: 4 (over x, core), dev: 8 (over z, y).
Axes of the slice: x: 2, y: 2, z: 4, core: 2. Of those that a mesh axis runs over, the one named last changes fastest.
Arguments:
- wavefield: float32 [32, 2, 128, 2048], P(('grp', 'dev')), may hold values from -6 to 6
- measured: float32 [32, 128, 2048], P(('grp', 'dev')), may hold values from 0.5 to 4
- leaf_map: float32 [32, 2, 128, 128], P(('grp', 'dev')), may hold values from -0.375 to 0.375
- factors: float32 [8, 32, 2, 128, 128], P(None, ('grp', 'dev')), may hold values from -0.375 to 0.375
- closing: float32 [32, 2, 128, 128], P(('grp', 'dev')), may hold values from -0.375 to 0.375
- box_perm: int32 [32, 2048], P(('grp', 'dev')), may hold values from 0 to 2047, each once within a row
- factor_order: int32 [8], replicated, may hold values from 0 to 7, each once
Outputs:
- projected: float32 [32, 2, 128, 2048], P(('grp', 'dev'))
Inputs may be any that keep to these rules, and one draw needn't show every extreme that they name: `box_perm`: each row is a permutation of 0 .. 2047. `factor_order`: a permutation of 0 .. 7.
All inputs are finite; a program needn't handle non-finite values.
Results may differ from a plain program's by a relative error of at most 0.00018.
Values sent between devices are 32-bit elements; how exact they have to be, the bound alone decides.
No kernel may reach another device: no remote copies, remote signals or barrier semaphores. Data moves between devices by JAX's collectives and lax.ppermute only.
A program may use at most 64 MiB of HBM per device.

v0:
```python
import functools

import jax
import jax.numpy as jnp
from jax import lax
from jax.experimental import pallas as pl
from jax.experimental.pallas import tpu as pltpu
from jax.sharding import PartitionSpec as P

BF = jnp.bfloat16
F32 = jnp.float32
FIRST_SIXTEENTHS = (1, 3, 4, 4, 4)
SECOND_SIXTEENTHS = (2, 4, 5, 5)
TILE = 256


def levels_of(level_count, dev_size):
    dev_bits = dev_size.bit_length() - 1
    return [
        ("grp", 1 - j) if j < 2 else ("dev", (j - 2) % dev_bits)
        for j in range(level_count)
    ]


def swapped(block, level):
    axis, bit = level
    count = lax.axis_size(axis)
    return lax.ppermute(block, axis, [(i, i ^ 1 << bit) for i in range(count)])


def half_bit(level):
    return lax.axis_index(level[0]) >> level[1] & 1


def cuts(sixteenths, boxes):
    unit = boxes // 16
    parts, at = [], 0
    for share in sixteenths:
        parts.append((at, share * unit))
        at += share * unit
    return parts


def split(values):
    high = values.astype(BF)
    return high, (values - high.astype(F32)).astype(BF)


def weights(re, im, column_bit, row_bit):
    def ordered(part):
        half = part.shape[0] // 2
        if column_bit is not None:
            turned = jnp.concatenate([part[:, half:], part[:, :half]], axis=1)
            part = jnp.where(column_bit == 1, turned, part)
        if row_bit is not None:
            turned = jnp.concatenate([part[half:], part[:half]], axis=0)
            part = jnp.where(row_bit == 1, turned, part)
        return part

    re, im = ordered(re), ordered(im)
    return split(
        jnp.concatenate(
            [jnp.concatenate([re, -im], axis=1), jnp.concatenate([im, re], axis=1)],
            axis=0,
        )
    )


def dot(a, b):
    return jnp.dot(a, b, preferred_element_type=F32)


def product(w, z):
    return dot(w[0], z[0]) + (dot(w[0], z[1]) + dot(w[1], z[0]))


def tiles(width):
    step = min(TILE, width)
    return [slice(at, min(at + step, width)) for at in range(0, width, step)]


def put_halves(result, keep_ref, send_ref, cols):
    half = result.shape[0] // 4
    for part in range(2):
        keep_ref[part, :, cols] = result[2 * part * half : (2 * part + 1) * half]
        send_ref[part, :, cols] = result[(2 * part + 1) * half : (2 * part + 2) * half]


def stacked(keep, recv):
    return jnp.concatenate([keep[0], recv[0], keep[1], recv[1]], axis=0)


def leaf_kernel(level, field_ref, leaf_ref, keep_ref, send_ref):
    w = weights(leaf_ref[0, 0], leaf_ref[0, 1], None, half_bit(level))
    for cols in tiles(keep_ref.shape[2]):
        field = field_ref[0, :, :, cols]
        z = split(field.reshape(-1, field.shape[-1]))
        put_halves(product(w, z), keep_ref, send_ref, cols)


def level_kernel(level, following, order_ref, factor_ref, keep_in, recv_in, keep_ref, send_ref):
    w = weights(factor_ref[0, 0, 0], factor_ref[0, 0, 1], half_bit(level), half_bit(following))
    for cols in tiles(keep_ref.shape[2]):
        z = split(stacked(keep_in[:, :, cols], recv_in[:, :, cols]))
        put_halves(product(w, z), keep_ref, send_ref, cols)


def picked(perm, terms, width):
    total = None
    for rows in tiles(terms.shape[1]):
        depth = rows.stop - rows.start
        at = lax.broadcasted_iota(jnp.int32, (depth, width), 0) + rows.start
        chosen = jnp.where(at == perm, 1.0, 0.0).astype(BF)
        here = dot(terms[:, rows], chosen)
        total = here if total is None else total + here
    return total.astype(BF)


def switch_kernel(level, following, order_ref, factor_ref, own_perm, other_perm, keep_in, recv_in, keep_ref, send_ref):
    w = weights(factor_ref[0, 0, 0], factor_ref[0, 0, 1], half_bit(level), half_bit(following))
    half = keep_ref.shape[1]
    for cols in tiles(keep_ref.shape[2]):
        width = cols.stop - cols.start
        keep = picked(own_perm[:, cols], keep_in, width)
        recv = picked(other_perm[:, cols], recv_in, width)
        z = [
            stacked(
                [keep[at : at + half], keep[at + half : at + 2 * half]],
                [recv[at : at + half], recv[at + half : at + 2 * half]],
            )
            for at in (0, 2 * half)
        ]
        put_halves(product(w, z), keep_ref, send_ref, cols)


def terms_kernel(parts, *refs):
    out_ref = refs[-1]
    half = out_ref.shape[0] // 4
    for (at, width), ref in zip(parts, refs[:-1]):
        for part in range(2):
            high, low = split(ref[part])
            out_ref[part * half : (part + 1) * half, at : at + width] = high
            out_ref[(2 + part) * half : (3 + part) * half, at : at + width] = low


def last_kernel(level, order_ref, factor_ref, closing_ref, measured_ref, keep_in, recv_in, *rest):
    out_ref = rest[-1]
    w = weights(factor_ref[0, 0, 0], factor_ref[0, 0, 1], half_bit(level), None)
    c = weights(closing_ref[0, 0], closing_ref[0, 1], None, None)
    for cols in tiles(out_ref.shape[3]):
        z = split(stacked(keep_in[:, :, cols], recv_in[:, :, cols]))
        image = product(c, split(product(w, z)))
        half = image.shape[0] // 2
        re, im = image[:half], image[half:]
        scale = measured_ref[0, :, cols] * lax.rsqrt(jnp.maximum(re * re + im * im, 0.25))
        out_ref[0, 0, :, cols] = re * scale
        out_ref[0, 1, :, cols] = im * scale


def whole():
    return pl.BlockSpec(memory_space=pltpu.VMEM)


def elements(*sizes):
    return tuple(pl.Element(size) for size in sizes)


def params():
    return pltpu.CompilerParams(vmem_limit_bytes=32 << 20)


def cost(flops, moved):
    return pl.CostEstimate(flops=int(flops), bytes_accessed=int(moved), transcendentals=0)


def per_device(wavefield, measured, leaf_map, factors, closing, box_perm, factor_order):
    _, _, cells, boxes = wavefield.shape
    level_count, slots = factors.shape[0], factors.shape[3]
    half = slots // 2
    levels = levels_of(level_count, lax.axis_size("dev"))
    switch_at = level_count // 2
    first, second = cuts(FIRST_SIXTEENTHS, boxes), cuts(SECOND_SIXTEENTHS, boxes)
    unit = boxes // 16

    def halves(width):
        return [jax.ShapeDtypeStruct((2, half, width), F32)] * 2

    def product_cost(width, times=1):
        return cost(times * 24 * slots * slots * width, 16 * slots * width)

    def factor_spec(j):
        return pl.BlockSpec((1, 1, 2, slots, slots), lambda i, order: (order[j], 0, 0, 0, 0))

    def spec(ins, outs):
        return pltpu.PrefetchScalarGridSpec(
            num_scalar_prefetch=1, grid=(1,), in_specs=ins, out_specs=outs
        )

    def leaf(part):
        at, width = part
        return pl.pallas_call(
            functools.partial(leaf_kernel, levels[0]),
            grid=(1,),
            out_shape=halves(width),
            in_specs=[
                pl.BlockSpec(elements(1, 2, cells, width), lambda i: (0, 0, 0, at)),
                pl.BlockSpec((1, 2, slots, cells), lambda i: (0, 0, 0, 0)),
            ],
            out_specs=[whole()] * 2,
            compiler_params=params(),
            cost_estimate=product_cost(width),
        )(wavefield, leaf_map)

    def level(j, keep, recv):
        width = keep.shape[2]
        return pl.pallas_call(
            functools.partial(level_kernel, levels[j], levels[j + 1]),
            grid_spec=spec([factor_spec(j), whole(), whole()], [whole()] * 2),
            out_shape=halves(width),
            compiler_params=params(),
            cost_estimate=product_cost(width),
        )(factor_order, factors, keep, recv)

    def terms(blocks):
        return pl.pallas_call(
            functools.partial(terms_kernel, first),
            out_shape=jax.ShapeDtypeStruct((4 * half, boxes), BF),
            in_specs=[whole()] * len(blocks),
            out_specs=whole(),
            compiler_params=params(),
            cost_estimate=cost(0, 12 * slots * boxes),
        )(*blocks)

    def switch(j, part, other_perm, keep, recv):
        at, width = part

        def perm_spec():
            return pl.BlockSpec(elements(1, width), lambda i, order: (0, at))

        return pl.pallas_call(
            functools.partial(switch_kernel, levels[j], levels[j + 1]),
            grid_spec=spec(
                [factor_spec(j), perm_spec(), perm_spec(), whole(), whole()], [whole()] * 2
            ),
            out_shape=halves(width),
            compiler_params=params(),
            cost_estimate=cost(16 * half * boxes * width, 32 * half * width),
        )(factor_order, factors, box_perm, other_perm, keep, recv)

    def last(part, keep, recv, so_far):
        at, width = part
        j = level_count - 1
        ins = [
            factor_spec(j),
            pl.BlockSpec((1, 2, cells, slots), lambda i, order: (0, 0, 0, 0)),
            pl.BlockSpec(elements(1, cells, width), lambda i, order: (0, 0, at)),
            whole(),
            whole(),
        ]
        args = [factor_order, factors, closing, measured, keep, recv]
        aliases = {}
        if so_far is not None:
            ins.append(pl.BlockSpec(memory_space=pl.ANY))
            aliases = {len(args): 0}
            args.append(so_far)
        return pl.pallas_call(
            functools.partial(last_kernel, levels[j]),
            grid_spec=spec(
                ins,
                pl.BlockSpec(elements(1, 2, cells, width), lambda i, order: (0, 0, 0, at)),
            ),
            out_shape=jax.ShapeDtypeStruct((1, 2, cells, boxes), F32),
            input_output_aliases=aliases,
            compiler_params=params(),
            cost_estimate=product_cost(width, 2),
        )(*args)

    other_perm = swapped(box_perm, levels[switch_at])
    kept, received = [], []
    for part in first:
        keep, send = leaf(part)
        for j in range(switch_at):
            keep, send = level(j, keep, swapped(send, levels[j]))
        kept.append(keep)
        received.append(swapped(send, levels[switch_at]))
    keep_terms, recv_terms = terms(kept), terms(received)
    out = None
    for part in second:
        keep, send = switch(switch_at, part, other_perm, keep_terms, recv_terms)
        for j in range(switch_at + 1, level_count - 1):
            keep, send = level(j, keep, swapped(send, levels[j]))
        out = last(part, keep, swapped(send, levels[level_count - 1]), out)
    return out


def solution(mesh):
    return jax.shard_map(
        per_device,
        mesh=mesh,
        in_specs=(
            P(("grp", "dev"), None, None, None),
            P(("grp", "dev"), None, None),
            P(("grp", "dev"), None, None, None),
            P(None, ("grp", "dev"), None, None, None),
            P(("grp", "dev"), None, None, None),
            P(("grp", "dev"), None),
            P(),
        ),
        out_specs=P(("grp", "dev"), None, None, None),
        check_vma=False,
    )
```

profile of v0, /device:TPU:0, one launch (start us, length us, event | category | flops | bytes accessed | tf_op | source)
XLA Modules:
  0.0 212.2 jit_solution(14097983819525624593)
XLA Ops:
  2.9 3.0 %collective-permute-start.9 = (f32[2,64,512]{2,1,0:T(8,128)S(1)}, f32[2,64,512]{2,1,0:T(8,128)S(1)}, u32[]{:S(2)}, u32[]{:S(2)}) collective-permute-start(f32[2,64,512]{2,1,0:T(8,128)S(1)} %get-tuple-element.98), channel_id=1, source_target_pairs={{0,16},{8,24},{16,0},{24,8},{1,17},{9,25},{17,1},{25,9},{2,18},{10... | collective-permute-start | bytes 786440 | tf_op jit(solution)/shard_map/ppermute | solution.py:28
  8.8 4.2 %collective-permute-done.9.recv_in = f32[2,64,512]{2,1,0:T(8,128)S(1)} collective-permute-done((f32[2,64,512]{2,1,0:T(8,128)S(1)}, f32[2,64,512]{2,1,0:T(8,128)S(1)}, u32[]{:S(2)}, u32[]{:S(2)}) %collective-permute-start.9) | collective-permute-done | bytes 262176 | tf_op jit(solution)/shard_map/ppermute | solution.py:28
  14.1 4.5 %collective-permute-done.17.recv_in = f32[2,64,512]{2,1,0:T(8,128)S(1)} collective-permute-done((f32[2,64,512]{2,1,0:T(8,128)S(1)}, f32[2,64,512]{2,1,0:T(8,128)S(1)}, u32[]{:S(2)}, u32[]{:S(2)}) %collective-permute-start.17) | collective-permute-done | bytes 262176 | tf_op jit(solution)/shard_map/ppermute | solution.py:28
  19.7 3.7 %collective-permute-done.13.recv_in = f32[2,64,512]{2,1,0:T(8,128)S(1)} collective-permute-done((f32[2,64,512]{2,1,0:T(8,128)S(1)}, f32[2,64,512]{2,1,0:T(8,128)S(1)}, u32[]{:S(2)}, u32[]{:S(2)}) %collective-permute-start.13) | collective-permute-done | bytes 262176 | tf_op jit(solution)/shard_map/ppermute | solution.py:28
  26.7 5.5 %collective-permute-done.5.recv_in = f32[2,64,384]{2,1,0:T(8,128)S(1)} collective-permute-done((f32[2,64,384]{2,1,0:T(8,128)S(1)}, f32[2,64,384]{2,1,0:T(8,128)S(1)}, u32[]{:S(2)}, u32[]{:S(2)}) %collective-permute-start.5) | collective-permute-done | bytes 196640 | tf_op jit(solution)/shard_map/ppermute | solution.py:28
  46.3 2.7 %collective-permute-done.19.recv_in = f32[2,64,512]{2,1,0:T(8,128)S(1)} collective-permute-done((f32[2,64,512]{2,1,0:T(8,128)S(1)}, f32[2,64,512]{2,1,0:T(8,128)S(1)}, u32[]{:S(2)}, u32[]{:S(2)}) %collective-permute-start.19) | collective-permute-done | bytes 262176 | tf_op jit(solution)/shard_map/ppermute | solution.py:28
  52.0 2.7 %collective-permute-done.15.recv_in = f32[2,64,512]{2,1,0:T(8,128)S(1)} collective-permute-done((f32[2,64,512]{2,1,0:T(8,128)S(1)}, f32[2,64,512]{2,1,0:T(8,128)S(1)}, u32[]{:S(2)}, u32[]{:S(2)}) %collective-permute-start.15) | collective-permute-done | bytes 262176 | tf_op jit(solution)/shard_map/ppermute | solution.py:28
  63.2 2.8 %collective-permute-done.1.recv_in = f32[2,64,128]{2,1,0:T(8,128)S(1)} collective-permute-done((f32[2,64,128]{2,1,0:T(8,128)S(1)}, f32[2,64,128]{2,1,0:T(8,128)S(1)}, u32[]{:S(2)}, u32[]{:S(2)}) %collective-permute-start.1) | collective-permute-done | bytes 65568 | tf_op jit(solution)/shard_map/ppermute | solution.py:28
  67.9 2.7 %collective-permute-start.23 = (f32[2,64,512]{2,1,0:T(8,128)S(1)}, f32[2,64,512]{2,1,0:T(8,128)S(1)}, u32[]{:S(2)}, u32[]{:S(2)}) collective-permute-start(f32[2,64,512]{2,1,0:T(8,128)S(1)} %get-tuple-element.126), channel_id=1, source_target_pairs={{0,4},{1,5},{2,6},{3,7},{4,0},{5,1},{6,2},{7,3},{8,12},{9,13},{10,... | collective-permute-start | bytes 786440 | tf_op jit(solution)/shard_map/ppermute | solution.py:28
  72.9 2.7 %collective-permute-start.24 = (f32[2,64,512]{2,1,0:T(8,128)S(1)}, f32[2,64,512]{2,1,0:T(8,128)S(1)}, u32[]{:S(2)}, u32[]{:S(2)}) collective-permute-start(f32[2,64,512]{2,1,0:T(8,128)S(1)} %get-tuple-element.127), channel_id=1, source_target_pairs={{0,4},{1,5},{2,6},{3,7},{4,0},{5,1},{6,2},{7,3},{8,12},{9,13},{10,... | collective-permute-start | bytes 786440 | tf_op jit(solution)/shard_map/ppermute | solution.py:28
  82.2 11.5 %collective-permute-done.4.recv_in = f32[2,64,128]{2,1,0:T(8,128)S(1)} collective-permute-done((f32[2,64,128]{2,1,0:T(8,128)S(1)}, f32[2,64,128]{2,1,0:T(8,128)S(1)}, u32[]{:S(2)}, u32[]{:S(2)}) %collective-permute-start.4) | collective-permute-done | bytes 65568 | tf_op jit(solution)/shard_map/ppermute | solution.py:28
  95.8 20.9 %collective-permute-done.21.refs_0_ = f32[2,64,128]{2,1,0:T(8,128)S(1)} collective-permute-done((f32[2,64,128]{2,1,0:T(8,128)S(1)}, f32[2,64,128]{2,1,0:T(8,128)S(1)}, u32[]{:S(2)}, u32[]{:S(2)}) %collective-permute-start.21) | collective-permute-done | bytes 65568 | tf_op jit(solution)/shard_map/ppermute | solution.py:28
  117.1 4.2 %collective-permute-done.other_perm = s32[1,2048]{1,0:T(1,128)S(1)} collective-permute-done((s32[1,2048]{1,0:T(1,128)S(1)}, s32[1,2048]{1,0:T(1,128)S(1)}, u32[]{:S(2)}, u32[]{:S(2)}) %collective-permute-start) | collective-permute-done | bytes 8224 | tf_op jit(solution)/shard_map/ppermute | solution.py:28
  121.3 3.2 %shard_map.103 = (f32[2,64,640]{2,1,0:T(8,128)S(1)}, f32[2,64,640]{2,1,0:T(8,128)S(1)}) custom-call(s32[8]{0:T(128)S(1)} %copy-done.7, f32[8,1,2,128,128]{4,3,2,1,0:T(8,128)S(1)} %copy-done, s32[1,2048]{1,0:T(1,128)S(1)} %copy-done.8, s32[1,2048]{1,0:T(1,128)S(1)} %collective-permute-done.other_perm, bf16[256,2048]{1,0:T(8,128)(2,1)S(1)} %shard_map.98.keep_in, ...), custom_call_target="tpu_custom_call" | custom-call | flops 1342177280 | bytes 1310720 | tf_op jit(solution)/shard_map/pallas_call | solution.py:240
  126.2 3.4 %shard_map.100 = (f32[2,64,640]{2,1,0:T(8,128)S(1)}, f32[2,64,640]{2,1,0:T(8,128)S(1)}) custom-call(s32[8]{0:T(128)S(1)} %copy-done.7, f32[8,1,2,128,128]{4,3,2,1,0:T(8,128)S(1)} %copy-done, s32[1,2048]{1,0:T(1,128)S(1)} %copy-done.8, s32[1,2048]{1,0:T(1,128)S(1)} %collective-permute-done.other_perm, bf16[256,2048]{1,0:T(8,128)(2,1)S(1)} %shard_map.98.keep_in, ...), custom_call_target="tpu_custom_call" | custom-call | flops 1342177280 | bytes 1310720 | tf_op jit(solution)/shard_map/pallas_call | solution.py:240
  130.1 2.4 %shard_map.106 = (f32[2,64,512]{2,1,0:T(8,128)S(1)}, f32[2,64,512]{2,1,0:T(8,128)S(1)}) custom-call(s32[8]{0:T(128)S(1)} %copy-done.7, f32[8,1,2,128,128]{4,3,2,1,0:T(8,128)S(1)} %copy-done, s32[1,2048]{1,0:T(1,128)S(1)} %copy-done.8, s32[1,2048]{1,0:T(1,128)S(1)} %collective-permute-done.other_perm, bf16[256,2048]{1,0:T(8,128)(2,1)S(1)} %shard_map.98.keep_in, ...), custom_call_target="tpu_custom_call" | custom-call | flops 1073741824 | bytes 1048576 | tf_op jit(solution)/shard_map/pallas_call | solution.py:240
  136.7 5.6 %collective-permute-done.26.recv_in = f32[2,64,640]{2,1,0:T(8,128)S(1)} collective-permute-done((f32[2,64,640]{2,1,0:T(8,128)S(1)}, f32[2,64,640]{2,1,0:T(8,128)S(1)}, u32[]{:S(2)}, u32[]{:S(2)}) %collective-permute-start.26) | collective-permute-done | bytes 327712 | tf_op jit(solution)/shard_map/ppermute | solution.py:28
  150.2 3.4 %collective-permute-done.35.recv_in = f32[2,64,256]{2,1,0:T(8,128)S(1)} collective-permute-done((f32[2,64,256]{2,1,0:T(8,128)S(1)}, f32[2,64,256]{2,1,0:T(8,128)S(1)}, u32[]{:S(2)}, u32[]{:S(2)}) %collective-permute-start.35) | collective-permute-done | bytes 131104 | tf_op jit(solution)/shard_map/ppermute | solution.py:28
  159.4 2.2 %collective-permute-start.34 = (f32[2,64,512]{2,1,0:T(8,128)S(1)}, f32[2,64,512]{2,1,0:T(8,128)S(1)}, u32[]{:S(2)}, u32[]{:S(2)}) collective-permute-start(f32[2,64,512]{2,1,0:T(8,128)S(1)} %get-tuple-element.146), channel_id=1, source_target_pairs={{0,4},{1,5},{2,6},{3,7},{4,0},{5,1},{6,2},{7,3},{8,12},{9,13},{10,... | collective-permute-start | bytes 786440 | tf_op jit(solution)/shard_map/ppermute | solution.py:28
  164.5 2.2 %collective-permute-start.37 = (f32[2,64,256]{2,1,0:T(8,128)S(1)}, f32[2,64,256]{2,1,0:T(8,128)S(1)}, u32[]{:S(2)}, u32[]{:S(2)}) collective-permute-start(f32[2,64,256]{2,1,0:T(8,128)S(1)} %get-tuple-element.152), channel_id=1, source_target_pairs={{0,4},{1,5},{2,6},{3,7},{4,0},{5,1},{6,2},{7,3},{8,12},{9,13},{10,... | collective-permute-start | bytes 393224 | tf_op jit(solution)/shard_map/ppermute | solution.py:28
  166.6 36.0 %collective-permute-done.37.recv_in = f32[2,64,256]{2,1,0:T(8,128)S(1)} collective-permute-done((f32[2,64,256]{2,1,0:T(8,128)S(1)}, f32[2,64,256]{2,1,0:T(8,128)S(1)}, u32[]{:S(2)}, u32[]{:S(2)}) %collective-permute-start.37) | collective-permute-done | bytes 131104 | tf_op jit(solution)/shard_map/ppermute | solution.py:28
  204.6 2.3 %shard_map.113.rest_0_ = f32[1,2,128,2048]{3,2,1,0:T(8,128)} custom-call(s32[8]{0:T(128)S(1)} %copy-done.7, f32[8,1,2,128,128]{4,3,2,1,0:T(8,128)S(1)} %copy-done, f32[1,2,128,128]{3,2,1,0:T(8,128)S(1)} %copy-done.6, f32[1,128,2048]{2,1,0:T(8,128)S(1)} %copy-done.3, f32[2,64,512]{2,1,0:T(8,128)S(1)} %get-tuple-element.145.keep_in, ...), custom_call_target="tpu_custom_call", output_to_operand_aliasing={{}: (6, {})} | custom-call | flops 402653184 | bytes 1048576 | tf_op jit(solution)/shard_map/pallas_call | solution.py:266
  206.9 2.7 %shard_map.114.rest_0_ = f32[1,2,128,2048]{3,2,1,0:T(8,128)} custom-call(s32[8]{0:T(128)S(1)} %copy-done.7, f32[8,1,2,128,128]{4,3,2,1,0:T(8,128)S(1)} %copy-done, f32[1,2,128,128]{3,2,1,0:T(8,128)S(1)} %copy-done.6, f32[1,128,2048]{2,1,0:T(8,128)S(1)} %copy-done.3, f32[2,64,640]{2,1,0:T(8,128)S(1)} %get-tuple-element.139.keep_in, ...), custom_call_target="tpu_custom_call", output_to_operand_aliasing={{}: (6, {})} | custom-call | flops 503316480 | bytes 1310720 | tf_op jit(solution)/shard_map/pallas_call | solution.py:266
  209.6 2.7 %shard_map.115 = f32[1,2,128,2048]{3,2,1,0:T(8,128)} custom-call(s32[8]{0:T(128)S(1)} %copy-done.7, f32[8,1,2,128,128]{4,3,2,1,0:T(8,128)S(1)} %copy-done, f32[1,2,128,128]{3,2,1,0:T(8,128)S(1)} %copy-done.6, f32[1,128,2048]{2,1,0:T(8,128)S(1)} %copy-done.3, f32[2,64,640]{2,1,0:T(8,128)S(1)} %get-tuple-element.133.keep_in, ...), custom_call_target="tpu_custom_call", output_to_operand_aliasing={{}: (6, {})} | custom-call | flops 503316480 | bytes 1310720 | tf_op jit(solution)/shard_map/pallas_call | solution.py:266
  (113 shorter events, 74.6 us)
Async XLA Ops:
  6.3 12.4 %collective-permute-start.17 = (f32[2,64,512]{2,1,0:T(8,128)S(1)}, f32[2,64,512]{2,1,0:T(8,128)S(1)}, u32[]{:S(2)}, u32[]{:S(2)}) collective-permute-start(f32[2,64,512]{2,1,0:T(8,128)S(1)} %get-tuple-element.116), channel_id=1, source_target_pairs={{0,16},{8,24},{16,0},{24,8},{1,17},{9,25},{17,1},{25,9},{2,18},{10... | collective-permute-start | bytes 786440 | tf_op jit(solution)/shard_map/ppermute | solution.py:28
  6.8 16.7 %collective-permute-start.13 = (f32[2,64,512]{2,1,0:T(8,128)S(1)}, f32[2,64,512]{2,1,0:T(8,128)S(1)}, u32[]{:S(2)}, u32[]{:S(2)}) collective-permute-start(f32[2,64,512]{2,1,0:T(8,128)S(1)} %get-tuple-element.107), channel_id=1, source_target_pairs={{0,16},{8,24},{16,0},{24,8},{1,17},{9,25},{17,1},{25,9},{2,18},{10... | collective-permute-start | bytes 786440 | tf_op jit(solution)/shard_map/ppermute | solution.py:28
  14.0 19.3 %collective-permute-start.10 = (f32[2,64,512]{2,1,0:T(8,128)S(1)}, f32[2,64,512]{2,1,0:T(8,128)S(1)}, u32[]{:S(2)}, u32[]{:S(2)}) collective-permute-start(f32[2,64,512]{2,1,0:T(8,128)S(1)} %get-tuple-element.100), channel_id=1, source_target_pairs={{0,8},{8,0},{16,24},{24,16},{1,9},{9,1},{17,25},{25,17},{2,10},{10... | collective-permute-start | bytes 786440 | tf_op jit(solution)/shard_map/ppermute | solution.py:28
  19.6 16.5 %collective-permute-start.18 = (f32[2,64,512]{2,1,0:T(8,128)S(1)}, f32[2,64,512]{2,1,0:T(8,128)S(1)}, u32[]{:S(2)}, u32[]{:S(2)}) collective-permute-start(f32[2,64,512]{2,1,0:T(8,128)S(1)} %get-tuple-element.118), channel_id=1, source_target_pairs={{0,8},{8,0},{16,24},{24,16},{1,9},{9,1},{17,25},{25,17},{2,10},{10... | collective-permute-start | bytes 786440 | tf_op jit(solution)/shard_map/ppermute | solution.py:28
  24.4 13.0 %collective-permute-start.14 = (f32[2,64,512]{2,1,0:T(8,128)S(1)}, f32[2,64,512]{2,1,0:T(8,128)S(1)}, u32[]{:S(2)}, u32[]{:S(2)}) collective-permute-start(f32[2,64,512]{2,1,0:T(8,128)S(1)} %get-tuple-element.109), channel_id=1, source_target_pairs={{0,8},{8,0},{16,24},{24,16},{1,9},{9,1},{17,25},{25,17},{2,10},{10... | collective-permute-start | bytes 786440 | tf_op jit(solution)/shard_map/ppermute | solution.py:28
  38.4 16.3 %collective-permute-start.15 = (f32[2,64,512]{2,1,0:T(8,128)S(1)}, f32[2,64,512]{2,1,0:T(8,128)S(1)}, u32[]{:S(2)}, u32[]{:S(2)}) collective-permute-start(f32[2,64,512]{2,1,0:T(8,128)S(1)} %get-tuple-element.111), channel_id=1, source_target_pairs={{0,1},{1,0},{2,3},{3,2},{4,5},{5,4},{6,7},{7,6},{8,9},{9,8},{10,11... | collective-permute-start | bytes 786440 | tf_op jit(solution)/shard_map/ppermute | solution.py:28
  41.2 17.3 %collective-permute-start.7 = (f32[2,64,384]{2,1,0:T(8,128)S(1)}, f32[2,64,384]{2,1,0:T(8,128)S(1)}, u32[]{:S(2)}, u32[]{:S(2)}) collective-permute-start(f32[2,64,384]{2,1,0:T(8,128)S(1)} %get-tuple-element.93), channel_id=1, source_target_pairs={{0,1},{1,0},{2,3},{3,2},{4,5},{5,4},{6,7},{7,6},{8,9},{9,8},{10,11... | collective-permute-start | bytes 589832 | tf_op jit(solution)/shard_map/ppermute | solution.py:28
  44.4 22.5 %collective-permute-start.12 = (f32[2,64,512]{2,1,0:T(8,128)S(1)}, f32[2,64,512]{2,1,0:T(8,128)S(1)}, u32[]{:S(2)}, u32[]{:S(2)}) collective-permute-start(f32[2,64,512]{2,1,0:T(8,128)S(1)} %get-tuple-element.104), channel_id=1, source_target_pairs={{0,2},{1,3},{2,0},{3,1},{4,6},{5,7},{6,4},{7,5},{8,10},{9,11},{10,... | collective-permute-start | bytes 786440 | tf_op jit(solution)/shard_map/ppermute | solution.py:28
  50.1 20.5 %collective-permute-start.20 = (f32[2,64,512]{2,1,0:T(8,128)S(1)}, f32[2,64,512]{2,1,0:T(8,128)S(1)}, u32[]{:S(2)}, u32[]{:S(2)}) collective-permute-start(f32[2,64,512]{2,1,0:T(8,128)S(1)} %get-tuple-element.122), channel_id=1, source_target_pairs={{0,2},{1,3},{2,0},{3,1},{4,6},{5,7},{6,4},{7,5},{8,10},{9,11},{10,... | collective-permute-start | bytes 786440 | tf_op jit(solution)/shard_map/ppermute | solution.py:28
  55.7 16.3 %collective-permute-start.16 = (f32[2,64,512]{2,1,0:T(8,128)S(1)}, f32[2,64,512]{2,1,0:T(8,128)S(1)}, u32[]{:S(2)}, u32[]{:S(2)}) collective-permute-start(f32[2,64,512]{2,1,0:T(8,128)S(1)} %get-tuple-element.113), channel_id=1, source_target_pairs={{0,2},{1,3},{2,0},{3,1},{4,6},{5,7},{6,4},{7,5},{8,10},{9,11},{10,... | collective-permute-start | bytes 786440 | tf_op jit(solution)/shard_map/ppermute | solution.py:28
  59.5 18.6 %collective-permute-start.8 = (f32[2,64,384]{2,1,0:T(8,128)S(1)}, f32[2,64,384]{2,1,0:T(8,128)S(1)}, u32[]{:S(2)}, u32[]{:S(2)}) collective-permute-start(f32[2,64,384]{2,1,0:T(8,128)S(1)} %get-tuple-element.95), channel_id=1, source_target_pairs={{0,2},{1,3},{2,0},{3,1},{4,6},{5,7},{6,4},{7,5},{8,10},{9,11},{10,... | collective-permute-start | bytes 589832 | tf_op jit(solution)/shard_map/ppermute | solution.py:28
  67.9 49.0 %collective-permute-start.23 = (f32[2,64,512]{2,1,0:T(8,128)S(1)}, f32[2,64,512]{2,1,0:T(8,128)S(1)}, u32[]{:S(2)}, u32[]{:S(2)}) collective-permute-start(f32[2,64,512]{2,1,0:T(8,128)S(1)} %get-tuple-element.126), channel_id=1, source_target_pairs={{0,4},{1,5},{2,6},{3,7},{4,0},{5,1},{6,2},{7,3},{8,12},{9,13},{10,... | collective-permute-start | bytes 786440 | tf_op jit(solution)/shard_map/ppermute | solution.py:28
  71.6 45.4 %collective-permute-start.25 = (f32[2,64,512]{2,1,0:T(8,128)S(1)}, f32[2,64,512]{2,1,0:T(8,128)S(1)}, u32[]{:S(2)}, u32[]{:S(2)}) collective-permute-start(f32[2,64,512]{2,1,0:T(8,128)S(1)} %get-tuple-element.128), channel_id=1, source_target_pairs={{0,4},{1,5},{2,6},{3,7},{4,0},{5,1},{6,2},{7,3},{8,12},{9,13},{10,... | collective-permute-start | bytes 786440 | tf_op jit(solution)/shard_map/ppermute | solution.py:28
  72.9 44.0 %collective-permute-start.24 = (f32[2,64,512]{2,1,0:T(8,128)S(1)}, f32[2,64,512]{2,1,0:T(8,128)S(1)}, u32[]{:S(2)}, u32[]{:S(2)}) collective-permute-start(f32[2,64,512]{2,1,0:T(8,128)S(1)} %get-tuple-element.127), channel_id=1, source_target_pairs={{0,4},{1,5},{2,6},{3,7},{4,0},{5,1},{6,2},{7,3},{8,12},{9,13},{10,... | collective-permute-start | bytes 786440 | tf_op jit(solution)/shard_map/ppermute | solution.py:28
  79.0 37.8 %collective-permute-start.22 = (f32[2,64,384]{2,1,0:T(8,128)S(1)}, f32[2,64,384]{2,1,0:T(8,128)S(1)}, u32[]{:S(2)}, u32[]{:S(2)}) collective-permute-start(f32[2,64,384]{2,1,0:T(8,128)S(1)} %get-tuple-element.125), channel_id=1, source_target_pairs={{0,4},{1,5},{2,6},{3,7},{4,0},{5,1},{6,2},{7,3},{8,12},{9,13},{10,... | collective-permute-start | bytes 589832 | tf_op jit(solution)/shard_map/ppermute | solution.py:28
  94.6 22.2 %collective-permute-start.21 = (f32[2,64,128]{2,1,0:T(8,128)S(1)}, f32[2,64,128]{2,1,0:T(8,128)S(1)}, u32[]{:S(2)}, u32[]{:S(2)}) collective-permute-start(f32[2,64,128]{2,1,0:T(8,128)S(1)} %get-tuple-element.124), channel_id=1, source_target_pairs={{0,4},{1,5},{2,6},{3,7},{4,0},{5,1},{6,2},{7,3},{8,12},{9,13},{10,... | collective-permute-start | bytes 196616 | tf_op jit(solution)/shard_map/ppermute | solution.py:28
  129.6 12.7 %collective-permute-start.26 = (f32[2,64,640]{2,1,0:T(8,128)S(1)}, f32[2,64,640]{2,1,0:T(8,128)S(1)}, u32[]{:S(2)}, u32[]{:S(2)}) collective-permute-start(f32[2,64,640]{2,1,0:T(8,128)S(1)} %get-tuple-element.130), channel_id=1, source_target_pairs={{0,1},{1,0},{2,3},{3,2},{4,5},{5,4},{6,7},{7,6},{8,9},{9,8},{10,11... | collective-permute-start | bytes 983048 | tf_op jit(solution)/shard_map/ppermute | solution.py:28
  132.5 13.3 %collective-permute-start.32 = (f32[2,64,512]{2,1,0:T(8,128)S(1)}, f32[2,64,512]{2,1,0:T(8,128)S(1)}, u32[]{:S(2)}, u32[]{:S(2)}) collective-permute-start(f32[2,64,512]{2,1,0:T(8,128)S(1)} %get-tuple-element.142), channel_id=1, source_target_pairs={{0,1},{1,0},{2,3},{3,2},{4,5},{5,4},{6,7},{7,6},{8,9},{9,8},{10,11... | collective-permute-start | bytes 786440 | tf_op jit(solution)/shard_map/ppermute | solution.py:28
  136.3 20.2 %collective-permute-start.30 = (f32[2,64,640]{2,1,0:T(8,128)S(1)}, f32[2,64,640]{2,1,0:T(8,128)S(1)}, u32[]{:S(2)}, u32[]{:S(2)}) collective-permute-start(f32[2,64,640]{2,1,0:T(8,128)S(1)} %get-tuple-element.138), channel_id=1, source_target_pairs={{0,2},{1,3},{2,0},{3,1},{4,6},{5,7},{6,4},{7,5},{8,10},{9,11},{10,... | collective-permute-start | bytes 983048 | tf_op jit(solution)/shard_map/ppermute | solution.py:28
  143.3 18.3 %collective-permute-start.27 = (f32[2,64,640]{2,1,0:T(8,128)S(1)}, f32[2,64,640]{2,1,0:T(8,128)S(1)}, u32[]{:S(2)}, u32[]{:S(2)}) collective-permute-start(f32[2,64,640]{2,1,0:T(8,128)S(1)} %get-tuple-element.132), channel_id=1, source_target_pairs={{0,2},{1,3},{2,0},{3,1},{4,6},{5,7},{6,4},{7,5},{8,10},{9,11},{10,... | collective-permute-start | bytes 983048 | tf_op jit(solution)/shard_map/ppermute | solution.py:28
  157.6 49.3 %collective-permute-start.31 = (f32[2,64,640]{2,1,0:T(8,128)S(1)}, f32[2,64,640]{2,1,0:T(8,128)S(1)}, u32[]{:S(2)}, u32[]{:S(2)}) collective-permute-start(f32[2,64,640]{2,1,0:T(8,128)S(1)} %get-tuple-element.140), channel_id=1, source_target_pairs={{0,4},{1,5},{2,6},{3,7},{4,0},{5,1},{6,2},{7,3},{8,12},{9,13},{10,... | collective-permute-start | bytes 983048 | tf_op jit(solution)/shard_map/ppermute | solution.py:28
  159.4 45.2 %collective-permute-start.34 = (f32[2,64,512]{2,1,0:T(8,128)S(1)}, f32[2,64,512]{2,1,0:T(8,128)S(1)}, u32[]{:S(2)}, u32[]{:S(2)}) collective-permute-start(f32[2,64,512]{2,1,0:T(8,128)S(1)} %get-tuple-element.146), channel_id=1, source_target_pairs={{0,4},{1,5},{2,6},{3,7},{4,0},{5,1},{6,2},{7,3},{8,12},{9,13},{10,... | collective-permute-start | bytes 786440 | tf_op jit(solution)/shard_map/ppermute | solution.py:28
  162.7 46.9 %collective-permute-start.28 = (f32[2,64,640]{2,1,0:T(8,128)S(1)}, f32[2,64,640]{2,1,0:T(8,128)S(1)}, u32[]{:S(2)}, u32[]{:S(2)}) collective-permute-start(f32[2,64,640]{2,1,0:T(8,128)S(1)} %get-tuple-element.134), channel_id=1, source_target_pairs={{0,4},{1,5},{2,6},{3,7},{4,0},{5,1},{6,2},{7,3},{8,12},{9,13},{10,... | collective-permute-start | bytes 983048 | tf_op jit(solution)/shard_map/ppermute | solution.py:28
  164.5 38.2 %collective-permute-start.37 = (f32[2,64,256]{2,1,0:T(8,128)S(1)}, f32[2,64,256]{2,1,0:T(8,128)S(1)}, u32[]{:S(2)}, u32[]{:S(2)}) collective-permute-start(f32[2,64,256]{2,1,0:T(8,128)S(1)} %get-tuple-element.152), channel_id=1, source_target_pairs={{0,4},{1,5},{2,6},{3,7},{4,0},{5,1},{6,2},{7,3},{8,12},{9,13},{10,... | collective-permute-start | bytes 393224 | tf_op jit(solution)/shard_map/ppermute | solution.py:28
  (23 other events, 290.5 us)
where the time goes:
time: 212 us
  waiting for transfers between devices  115 us (54%)
  Pallas kernels  49.2 us (23%)
  starting transfers between devices  44.6 us (21%)
  local copies, waits for them, and re-layouts  2.53 us (1%)
    ppermute x38, waiting for transfers between devices, swapped(): return lax.ppermute(block, axis, [(i, i ^ 1 << bit) for i in range(count)])  115 us
    ppermute x38, starting transfers between devices, swapped(): return lax.ppermute(block, axis, [(i, i ^ 1 << bit) for i in range(count)])  44.6 us
    pallas_call x28, Pallas kernels, level(): pl.pallas_call(functools.partial(level_kernel, levels[j], levels[j + 1]),...  27 us
    pallas_call x4, Pallas kernels, switch(): pl.pallas_call(functools.partial(switch_kernel, levels[j], levels[j + 1])...  10.7 us
    pallas_call x4, Pallas kernels, last(): pl.pallas_call(functools.partial(last_kernel, levels[j]), grid_spec=spec(...  9.57 us
  transfers between devices with their start and end apart: 38, of which 18 were waited for; matrix products, arithmetic and copies ran while one was open for 0% of the time, Pallas kernels for 20%

commit v1 on v0

v1 whole, which is shorter than its diff:
```python
import functools

import jax
import jax.numpy as jnp
from jax import lax
from jax.experimental import pallas as pl
from jax.experimental.pallas import tpu as pltpu
from jax.sharding import PartitionSpec as P

BF = jnp.bfloat16
F32 = jnp.float32
FIRST_SIXTEENTHS = (2, 3, 4, 4, 3)
SECOND_SIXTEENTHS = (2, 3, 4, 4, 3)
FIRST_STARTS = (0, 0, 1, 3, 6)
SECOND_STARTS = (0, 0, 1, 3, 5)
TILE = 256


def levels_of(level_count, dev_size):
    dev_bits = dev_size.bit_length() - 1
    return [
        ("grp", 1 - j) if j < 2 else ("dev", (j - 2) % dev_bits)
        for j in range(level_count)
    ]


def swapped(block, level, name):
    axis, bit = level
    count = lax.axis_size(axis)
    with jax.named_scope(name):
        return lax.ppermute(block, axis, [(i, i ^ 1 << bit) for i in range(count)])


def half_bit(level):
    return lax.axis_index(level[0]) >> level[1] & 1


def cuts(sixteenths, boxes):
    unit = boxes // 16
    parts, at = [], 0
    for share in sixteenths:
        parts.append((at, share * unit))
        at += share * unit
    return parts


def split(values):
    high = values.astype(BF)
    return high, (values - high.astype(F32)).astype(BF)


def weights(re, im, column_bit, row_bit):
    def ordered(part):
        half = part.shape[0] // 2
        if column_bit is not None:
            turned = jnp.concatenate([part[:, half:], part[:, :half]], axis=1)
            part = jnp.where(column_bit == 1, turned, part)
        if row_bit is not None:
            turned = jnp.concatenate([part[half:], part[:half]], axis=0)
            part = jnp.where(row_bit == 1, turned, part)
        return part

    re, im = ordered(re), ordered(im)
    return split(
        jnp.concatenate(
            [jnp.concatenate([re, -im], axis=1), jnp.concatenate([im, re], axis=1)],
            axis=0,
        )
    )


def dot(a, b):
    return jnp.dot(a, b, preferred_element_type=F32)


def product(w, z):
    return dot(w[0], z[0]) + (dot(w[0], z[1]) + dot(w[1], z[0]))


def tiles(width):
    step = min(TILE, width)
    return [slice(at, min(at + step, width)) for at in range(0, width, step)]


def put_halves(result, keep_ref, send_ref, cols):
    half = result.shape[0] // 4
    for part in range(2):
        keep_ref[part, :, cols] = result[2 * part * half : (2 * part + 1) * half]
        send_ref[part, :, cols] = result[(2 * part + 1) * half : (2 * part + 2) * half]


def stacked(keep, recv):
    return jnp.concatenate([keep[0], recv[0], keep[1], recv[1]], axis=0)


def in_turn(starts, steps, begin, go_on):
    pending, used, part = [], 0, 0
    while part < len(starts) or pending:
        if part < len(starts) and (used >= starts[part] or not pending):
            begin(part)
            pending.append((part, 1))
            part += 1
            continue
        at, step = pending.pop(0)
        go_on(at, step)
        used += 1
        if step < steps:
            pending.append((at, step + 1))


def leaf_kernel(level, parts, field_ref, leaf_ref, *refs):
    count = len(parts)
    outs, turn, rest = refs[: 2 * count], refs[2 * count], refs[2 * count + 1 :]
    fields, leaf, arrived = rest[:count], rest[count], rest[count + 1]
    copies = [pltpu.make_async_copy(leaf_ref, leaf, arrived.at[count])]
    for n, (at, width) in enumerate(parts):
        source = field_ref.at[0, :, :, pl.ds(at, width)]
        copies.append(pltpu.make_async_copy(source, fields[n], arrived.at[n]))
    for copy in copies:
        copy.start()
    copies[0].wait()
    w = weights(leaf[0, 0], leaf[0, 1], None, half_bit(level))
    for n in range(count):
        copies[n + 1].wait()
        for cols in tiles(parts[n][1]):
            field = fields[n][:, :, cols]
            z = split(field.reshape(-1, field.shape[-1]))
            put_halves(product(w, z), outs[2 * n], outs[2 * n + 1], cols)


def after_turn(kernel, turn, *refs):
    kernel(*refs)


def weights_kernel(levels, turn, order_ref, factors_ref, closing_ref, perm_ref, *outs):
    perm_out, closing_out, *factor_outs, next_turn = outs
    perm_out[...] = perm_ref[...]
    for j, out in enumerate(factor_outs):
        at = order_ref[j]
        following = half_bit(levels[j + 1]) if j + 1 < len(levels) else None
        high, low = weights(factors_ref[at, 0, 0], factors_ref[at, 0, 1], half_bit(levels[j]), following)
        out[0], out[1] = high, low
    closing_out[0], closing_out[1] = weights(closing_ref[0, 0], closing_ref[0, 1], None, None)


def put_terms(values, out_ref, cols):
    half = values[0].shape[0]
    for part in range(2):
        high, low = split(values[part])
        out_ref[part * half : (part + 1) * half, cols] = high
        out_ref[(2 + part) * half : (3 + part) * half, cols] = low


def level_kernel(before_switch, turn, w, keep_in, recv_in, *refs):
    keep_ref, send_ref, _ = refs[-3:]
    for cols in tiles(send_ref.shape[2]):
        z = split(stacked(keep_in[:, :, cols], recv_in[:, :, cols]))
        result = product(w, z)
        if before_switch:
            half = result.shape[0] // 4
            parts = [result[at * half : (at + 1) * half] for at in range(4)]
            put_terms((parts[0], parts[2]), keep_ref, cols)
            send_ref[0, :, cols], send_ref[1, :, cols] = parts[1], parts[3]
        else:
            put_halves(result, keep_ref, send_ref, cols)


def picked(perm, parts, width):
    total, at = None, 0
    for part in parts:
        for rows in tiles(part.shape[1]):
            depth = rows.stop - rows.start
            box = lax.broadcasted_iota(jnp.int32, (depth, width), 0) + at
            chosen = jnp.where(box == perm, 1.0, 0.0).astype(BF)
            here = dot(part[:, rows], chosen)
            total = here if total is None else total + here
            at += depth
    return total.astype(BF)


def switch_kernel(start, turn, w, own_perm, other_perm, *refs):
    *parts, keep_ref, send_ref, next_turn = refs
    kept, received = parts[: len(parts) // 2], parts[len(parts) // 2 :]
    half = keep_ref.shape[1]
    for cols in tiles(keep_ref.shape[2]):
        width = cols.stop - cols.start
        where = slice(start + cols.start, start + cols.stop)
        keep = picked(own_perm[:, where], kept, width)
        recv = picked(other_perm[:, where], received, width)
        z = [
            stacked(
                [keep[at : at + half], keep[at + half : at + 2 * half]],
                [recv[at : at + half], recv[at + half : at + 2 * half]],
            )
            for at in (0, 2 * half)
        ]
        put_halves(product(w, z), keep_ref, send_ref, cols)


def terms_kernel(turn, part_ref, out_ref, next_turn):
    for cols in tiles(part_ref.shape[2]):
        put_terms(part_ref[:, :, cols], out_ref, cols)


def last_kernel(turn, w, c, measured_ref, keep_in, recv_in, *rest):
    out_ref = rest[-2]
    for cols in tiles(out_ref.shape[3]):
        z = split(stacked(keep_in[:, :, cols], recv_in[:, :, cols]))
        image = product(c, split(product(w, z)))
        half = image.shape[0] // 2
        re, im = image[:half], image[half:]
        scale = measured_ref[0, :, cols] * lax.rsqrt(jnp.maximum(re * re + im * im, 0.25))
        out_ref[0, 0, :, cols] = re * scale
        out_ref[0, 1, :, cols] = im * scale


def elements(*sizes):
    return tuple(pl.Element(size) for size in sizes)


def whole():
    return pl.BlockSpec(memory_space=pltpu.VMEM)


def anywhere():
    return pl.BlockSpec(memory_space=pl.ANY)


COST = pl.CostEstimate(flops=1000000000, bytes_accessed=2500000, transcendentals=0)


def per_device(wavefield, measured, leaf_map, factors, closing, box_perm, factor_order):
    _, _, cells, boxes = wavefield.shape
    level_count, slots = factors.shape[0], factors.shape[3]
    half = slots // 2
    levels = levels_of(level_count, lax.axis_size("dev"))
    switch_at = level_count // 2
    first, second = cuts(FIRST_SIXTEENTHS, boxes), cuts(SECOND_SIXTEENTHS, boxes)
    params = pltpu.CompilerParams(vmem_limit_bytes=32 << 20)
    turn_shape = jax.ShapeDtypeStruct((8, 128), F32)
    turn = factor_order
    name = "product"

    def call(kernel, ins, args, shapes, **more):
        nonlocal turn, name
        *outs, turn = pl.pallas_call(
            kernel,
            in_specs=[anywhere(), *ins],
            out_specs=[*more.pop("outs", [whole()] * len(shapes)), anywhere()],
            out_shape=[*shapes, turn_shape],
            compiler_params=params,
            cost_estimate=COST,
            name=name,
            **more,
        )(turn, *args)
        return outs

    def halves(width):
        return [jax.ShapeDtypeStruct((2, half, width), F32)] * 2

    def leaf(parts, after):
        nonlocal turn
        stay = pl.BlockSpec(memory_space=pltpu.HBM)
        ins, args = [stay] * 2, [wavefield, leaf_map]
        kernel = functools.partial(leaf_kernel, levels[0], parts)
        if after:
            ins, args = [anywhere()] + ins, [turn] + args
            kernel = functools.partial(after_turn, kernel)
        *outs, turn = pl.pallas_call(
            kernel,
            in_specs=ins,
            out_specs=[*[whole()] * (2 * len(parts)), anywhere()],
            out_shape=[shape for part in parts for shape in halves(part[1])] + [turn_shape],
            scratch_shapes=[
                *[pltpu.VMEM((2, cells, part[1]), F32) for part in parts],
                pltpu.VMEM(leaf_map.shape, F32),
                pltpu.SemaphoreType.DMA((len(parts) + 1,)),
            ],
            compiler_params=pltpu.CompilerParams(vmem_limit_bytes=(32 if after else 61) << 20),
            cost_estimate=COST,
            name="leaf",
        )(*args)
        return list(zip(outs[::2], outs[1::2]))

    def prepared():
        matrix = jax.ShapeDtypeStruct((2, 2 * slots, 2 * slots), BF)
        shapes = [jax.ShapeDtypeStruct(box_perm.shape, box_perm.dtype)] + [matrix] * (level_count + 1)
        perm, closing_terms, *factor_terms = call(
            functools.partial(weights_kernel, levels),
            [pl.BlockSpec(memory_space=pltpu.SMEM)] + [whole()] * 3,
            [factor_order, factors, closing, box_perm],
            shapes,
        )
        return perm, closing_terms, factor_terms

    def terms_of(width):
        return jax.ShapeDtypeStruct((4 * half, width), BF)

    def level(w, keep, recv, before_switch=False, also=()):
        width = recv.shape[2]
        shapes = halves(width)
        if before_switch:
            shapes[0] = terms_of(width)
        kernel = functools.partial(level_kernel, before_switch)
        ins = [whole()] * 3 + [anywhere()] * len(also)
        return call(kernel, ins, [w, keep, recv, *also], shapes)

    def terms(block):
        return call(terms_kernel, [whole()], [block], [terms_of(block.shape[2])])[0]

    def switch(part, w, own_perm, other_perm, keep, recv):
        at, width = part
        return call(
            functools.partial(switch_kernel, at),
            [whole()] * (3 + len(keep) + len(recv)), [w, own_perm, other_perm, *keep, *recv],
            halves(width),
        )

    def last(part, w, c, keep, recv, so_far):
        at, width = part
        ins = [whole()] * 5
        args = [w, c, lax.slice_in_dim(measured, at, at + width, axis=2), keep, recv]
        aliases = {}
        if so_far is not None:
            ins.append(anywhere())
            aliases = {len(args) + 1: 0}
            args.append(so_far)
        return call(
            last_kernel, ins, args,
            [jax.ShapeDtypeStruct((1, 2, cells, boxes), F32)],
            outs=[pl.BlockSpec(elements(1, 2, cells, width), lambda i: (0, 0, 0, at))],
            grid=(1,), input_output_aliases=aliases,
        )[0]

    own, away = {}, {}

    def leave(part, step, keep, send):
        own[part], away[part] = keep, swapped(send, levels[step], f"send_{part}_{step}")

    first_leaf = leaf(first[:1], False)
    leaves = first_leaf + leaf(first[1:], True)
    name = "weights"
    own_perm, closing_terms, factor_terms = prepared()
    other_perm = swapped(own_perm, levels[switch_at], "send_order")

    def first_begin(part):
        leave(part, 0, *leaves[part])

    def first_step(part, step):
        nonlocal name
        name = f"part_{part}_{step}"
        if step > switch_at:
            away[part] = terms(away[part])
        else:
            w = factor_terms[step - 1]
            also = [other_perm] if (part, step) == (0, 1) else []
            leave(part, step, *level(w, own[part], away[part], step == switch_at, also))

    in_turn(FIRST_STARTS, switch_at + 1, first_begin, first_step)
    kept, received = ([held[part] for part in range(len(first))] for held in (own, away))
    out = None

    def second_begin(part):
        nonlocal name
        name = f"again_{part}_{switch_at}"
        w = factor_terms[switch_at]
        leave(part, switch_at + 1, *switch(second[part], w, own_perm, other_perm, kept, received))

    def second_step(part, step):
        nonlocal name, out
        step += switch_at
        name = f"again_{part}_{step}"
        w = factor_terms[step]
        if step == level_count - 1:
            out = last(second[part], w, closing_terms, own[part], away[part], out)
        else:
            leave(part, step + 1, *level(w, own[part], away[part]))

    in_turn(SECOND_STARTS, level_count - 1 - switch_at, second_begin, second_step)
    return out


def solution(mesh):
    return jax.shard_map(
        per_device,
        mesh=mesh,
        in_specs=(
            P(("grp", "dev"), None, None, None),
            P(("grp", "dev"), None, None),
            P(("grp", "dev"), None, None, None),
            P(None, ("grp", "dev"), None, None, None),
            P(("grp", "dev"), None, None, None),
            P(("grp", "dev"), None),
            P(),
        ),
        out_specs=P(("grp", "dev"), None, None, None),
        check_vma=False,
    )
```

time: 212 us -> 150 us (0.71)
  waiting for transfers between devices: 115 us -> 61.1 us
  Pallas kernels: 49.2 us -> 33 us
  starting transfers between devices: 44.6 us -> 53.6 us
    ppermute x38 -> x41, waiting for transfers between devices: 115 us -> 61.1 us  [swapped(): return lax.ppermute(block, axis, [(i, i ^ 1 << bit) for i in range(count)])]
    pallas_call x43 -> x48, Pallas kernels: 49.2 us -> 33 us  [the longest x46 28.9 us: call(): pl.pallas_call(kernel, in_specs=[anywhere(), *ins], out_specs=[*more.pop(...]
    ppermute x38 -> x41, starting transfers between devices: 44.6 us -> 53.6 us  [swapped(): return lax.ppermute(block, axis, [(i, i ^ 1 << bit) for i in range(count)])]
  transfers between devices with their start and end apart: 38 -> 41, of which waited for: 18 -> 22; matrix products, arithmetic and copies ran while one was open for 0% -> 0% of each run, Pallas kernels for 20% -> 19%
where the time goes in v1:
time: 150 us; the launch traced here: 149 us
  waiting for transfers between devices  61.1 us (41%)
  starting transfers between devices  53.6 us (36%)
  Pallas kernels  33 us (22%)
    ppermute x41, waiting for transfers between devices, swapped(): return lax.ppermute(block, axis, [(i, i ^ 1 << bit) for i in range(count)])  61.1 us
    ppermute x41, starting transfers between devices, swapped(): return lax.ppermute(block, axis, [(i, i ^ 1 << bit) for i in range(count)])  53.6 us
    pallas_call x46, Pallas kernels, call(): pl.pallas_call(kernel, in_specs=[anywhere(), *ins], out_specs=[*more.pop(...  28.9 us
    pallas_call x2, Pallas kernels, leaf(): pl.pallas_call(kernel, in_specs=ins, out_specs=[*[whole()] * (2 * len(par...  4.04 us
  transfers between devices with their start and end apart: 41, of which 22 were waited for; matrix products, arithmetic and copies ran while one was open for 0% of the time, Pallas kernels for 19%

profile of v1, /device:TPU:0, one launch (start us, length us, event | category | flops | bytes accessed | tf_op | source)
XLA Modules:
  0.0 149.0 jit_solution(7282190602432011532)
XLA Ops:
  0.0 2.1 %leaf.2 = (f32[2,64,256]{2,1,0:T(8,128)}, f32[2,64,256]{2,1,0:T(8,128)}, f32[8,128]{1,0:T(8,128)}) custom-call(f32[1,2,128,2048]{3,2,1,0:T(8,128)} %refs_0_.1, f32[1,2,128,128]{3,2,1,0:T(8,128)} %refs_1_.1), custom_call_target="tpu_custom_call" | custom-call | flops 1000000000 | bytes 2500000 | tf_op jit(solution)/shard_map/leaf/pallas_call | solution.py:269
  2.2 3.0 %collective-permute-start = (f32[2,64,256]{2,1,0:T(8,128)}, f32[2,64,256]{2,1,0:T(8,128)S(1)}, u32[]{:S(2)}, u32[]{:S(2)}) collective-permute-start(f32[2,64,256]{2,1,0:T(8,128)} %get-tuple-element.157), channel_id=1, source_target_pairs={{0,16},{8,24},{16,0},{24,8},{1,17},{9,25},{17,1},{25,9},{2,18},{10... | collective-permute-start | bytes 393224 | tf_op jit(solution)/shard_map/send_0_0/ppermute | solution.py:31
  5.9 1.9 %leaf.3 = (f32[2,64,384]{2,1,0:T(8,128)S(1)}, f32[2,64,384]{2,1,0:T(8,128)S(1)}, f32[2,64,512]{2,1,0:T(8,128)S(1)}, f32[2,64,512]{2,1,0:T(8,128)S(1)}, f32[2,64,...) custom-call(f32[8,128]{1,0:T(8,128)S(1)} %copy-done.7, ...), custom_call_target="tpu_custom_call" | custom-call | flops 1000000000 | bytes 2500000 | tf_op jit(solution)/shard_map/leaf/pallas_call | solution.py:269
  9.0 3.1 %collective-permute-start.1 = (s32[1,2048]{1,0:T(1,128)S(1)}, s32[1,2048]{1,0:T(1,128)S(1)}, u32[]{:S(2)}, u32[]{:S(2)}) collective-permute-start(s32[1,2048]{1,0:T(1,128)S(1)} %get-tuple-element.158.own_perm), channel_id=1, source_target_pairs={{0,4},{1,5},{2,6},{3,7},{4,0},{5,1},{6,2},{7,3},{8,12},{9,13},{10,... | collective-permute-start | bytes 24584 | tf_op jit(solution)/shard_map/send_order/ppermute | solution.py:31
  19.2 2.1 %collective-permute-done.4.recv_in = f32[2,64,512]{2,1,0:T(8,128)S(1)} collective-permute-done((f32[2,64,512]{2,1,0:T(8,128)S(1)}, f32[2,64,512]{2,1,0:T(8,128)S(1)}, u32[]{:S(2)}, u32[]{:S(2)}) %collective-permute-start.4) | collective-permute-done | bytes 262176 | tf_op jit(solution)/shard_map/send_2_0/ppermute | solution.py:31
  45.4 4.8 %collective-permute-done.18.recv_in = f32[2,64,512]{2,1,0:T(8,128)S(1)} collective-permute-done((f32[2,64,512]{2,1,0:T(8,128)S(1)}, f32[2,64,512]{2,1,0:T(8,128)S(1)}, u32[]{:S(2)}, u32[]{:S(2)}) %collective-permute-start.18) | collective-permute-done | bytes 262176 | tf_op jit(solution)/shard_map/send_2_3/ppermute | solution.py:31
  51.5 3.0 %collective-permute-start.23 = (f32[2,64,384]{2,1,0:T(8,128)S(1)}, f32[2,64,384]{2,1,0:T(8,128)S(1)}, u32[]{:S(2)}, u32[]{:S(2)}) collective-permute-start(f32[2,64,384]{2,1,0:T(8,128)S(1)} %get-tuple-element.224), channel_id=1, source_target_pairs={{0,2},{1,3},{2,0},{3,1},{4,6},{5,7},{6,4},{7,5},{8,10},{9,11},{10,... | collective-permute-start | bytes 589832 | tf_op jit(solution)/shard_map/send_4_3/ppermute | solution.py:31
  54.6 5.5 %collective-permute-done.21.recv_in = f32[2,64,512]{2,1,0:T(8,128)S(1)} collective-permute-done((f32[2,64,512]{2,1,0:T(8,128)S(1)}, f32[2,64,512]{2,1,0:T(8,128)S(1)}, u32[]{:S(2)}, u32[]{:S(2)}) %collective-permute-start.21) | collective-permute-done | bytes 262176 | tf_op jit(solution)/shard_map/send_3_3/ppermute | solution.py:31
  61.4 3.3 %collective-permute-done.22.part_ref = f32[2,64,512]{2,1,0:T(8,128)S(1)} collective-permute-done((f32[2,64,512]{2,1,0:T(8,128)S(1)}, f32[2,64,512]{2,1,0:T(8,128)S(1)}, u32[]{:S(2)}, u32[]{:S(2)}) %collective-permute-start.22) | collective-permute-done | bytes 262176 | tf_op jit(solution)/shard_map/send_2_4/ppermute | solution.py:31
  64.8 2.8 %collective-permute-done.23.recv_in = f32[2,64,384]{2,1,0:T(8,128)S(1)} collective-permute-done((f32[2,64,384]{2,1,0:T(8,128)S(1)}, f32[2,64,384]{2,1,0:T(8,128)S(1)}, u32[]{:S(2)}, u32[]{:S(2)}) %collective-permute-start.23) | collective-permute-done | bytes 196640 | tf_op jit(solution)/shard_map/send_4_3/ppermute | solution.py:31
  68.5 12.0 %collective-permute-done.24.part_ref = f32[2,64,512]{2,1,0:T(8,128)S(1)} collective-permute-done((f32[2,64,512]{2,1,0:T(8,128)S(1)}, f32[2,64,512]{2,1,0:T(8,128)S(1)}, u32[]{:S(2)}, u32[]{:S(2)}) %collective-permute-start.24) | collective-permute-done | bytes 262176 | tf_op jit(solution)/shard_map/send_3_4/ppermute | solution.py:31
  80.5 2.8 %collective-permute-done.25.part_ref = f32[2,64,384]{2,1,0:T(8,128)S(1)} collective-permute-done((f32[2,64,384]{2,1,0:T(8,128)S(1)}, f32[2,64,384]{2,1,0:T(8,128)S(1)}, u32[]{:S(2)}, u32[]{:S(2)}) %collective-permute-start.25) | collective-permute-done | bytes 196640 | tf_op jit(solution)/shard_map/send_4_4/ppermute | solution.py:31
  88.5 2.4 %collective-permute-done.26.recv_in = f32[2,64,256]{2,1,0:T(8,128)S(1)} collective-permute-done((f32[2,64,256]{2,1,0:T(8,128)S(1)}, f32[2,64,256]{2,1,0:T(8,128)S(1)}, u32[]{:S(2)}, u32[]{:S(2)}) %collective-permute-start.26) | collective-permute-done | bytes 131104 | tf_op jit(solution)/shard_map/send_0_5/ppermute | solution.py:31
  91.3 2.2 %again_2_4.1 = (f32[2,64,512]{2,1,0:T(8,128)S(1)}, f32[2,64,512]{2,1,0:T(8,128)S(1)}, f32[8,128]{1,0:T(8,128)S(1)}) custom-call(f32[8,128]{1,0:T(8,128)S(1)} %get-tuple-element.246.turn, bf16[2,256,256]{2,1,0:T(8,128)(2,1)S(1)} %get-tuple-element.230.w, s32[1,2048]{1,0:T(1,128)S(1)} %get-tuple-element.158.own_perm, ...), custom_call_target="tpu_custom_call" | custom-call | flops 1000000000 | bytes 2500000 | tf_op jit(solution)/shard_map/again_2_4/pallas_call | solution.py:246
  95.3 2.1 %collective-permute-start.30 = (f32[2,64,384]{2,1,0:T(8,128)S(1)}, f32[2,64,384]{2,1,0:T(8,128)S(1)}, u32[]{:S(2)}, u32[]{:S(2)}) collective-permute-start(f32[2,64,384]{2,1,0:T(8,128)S(1)} %get-tuple-element.260), channel_id=1, source_target_pairs={{0,2},{1,3},{2,0},{3,1},{4,6},{5,7},{6,4},{7,5},{8,10},{9,11},{10,... | collective-permute-start | bytes 589832 | tf_op jit(solution)/shard_map/send_1_6/ppermute | solution.py:31
  100.1 2.0 %again_3_4.1 = (f32[2,64,512]{2,1,0:T(8,128)S(1)}, f32[2,64,512]{2,1,0:T(8,128)S(1)}, f32[8,128]{1,0:T(8,128)S(1)}) custom-call(f32[8,128]{1,0:T(8,128)S(1)} %get-tuple-element.254.turn, bf16[2,256,256]{2,1,0:T(8,128)(2,1)S(1)} %get-tuple-element.230.w, s32[1,2048]{1,0:T(1,128)S(1)} %get-tuple-element.158.own_perm, ...), custom_call_target="tpu_custom_call" | custom-call | flops 1000000000 | bytes 2500000 | tf_op jit(solution)/shard_map/again_3_4/pallas_call | solution.py:246
  103.9 2.6 %collective-permute-start.33 = (f32[2,64,512]{2,1,0:T(8,128)S(1)}, f32[2,64,512]{2,1,0:T(8,128)S(1)}, u32[]{:S(2)}, u32[]{:S(2)}) collective-permute-start(f32[2,64,512]{2,1,0:T(8,128)S(1)} %get-tuple-element.272), channel_id=1, source_target_pairs={{0,2},{1,3},{2,0},{3,1},{4,6},{5,7},{6,4},{7,5},{8,10},{9,11},{10,... | collective-permute-start | bytes 786440 | tf_op jit(solution)/shard_map/send_2_6/ppermute | solution.py:31
  111.9 2.1 %collective-permute-start.36 = (f32[2,64,512]{2,1,0:T(8,128)S(1)}, f32[2,64,512]{2,1,0:T(8,128)S(1)}, u32[]{:S(2)}, u32[]{:S(2)}) collective-permute-start(f32[2,64,512]{2,1,0:T(8,128)S(1)} %get-tuple-element.282), channel_id=1, source_target_pairs={{0,2},{1,3},{2,0},{3,1},{4,6},{5,7},{6,4},{7,5},{8,10},{9,11},{10,... | collective-permute-start | bytes 786440 | tf_op jit(solution)/shard_map/send_3_6/ppermute | solution.py:31
  114.0 2.9 %collective-permute-done.33.recv_in = f32[2,64,512]{2,1,0:T(8,128)S(1)} collective-permute-done((f32[2,64,512]{2,1,0:T(8,128)S(1)}, f32[2,64,512]{2,1,0:T(8,128)S(1)}, u32[]{:S(2)}, u32[]{:S(2)}) %collective-permute-start.33) | collective-permute-done | bytes 262176 | tf_op jit(solution)/shard_map/send_2_6/ppermute | solution.py:31
  120.1 2.7 %collective-permute-start.38 = (f32[2,64,384]{2,1,0:T(8,128)S(1)}, f32[2,64,384]{2,1,0:T(8,128)S(1)}, u32[]{:S(2)}, u32[]{:S(2)}) collective-permute-start(f32[2,64,384]{2,1,0:T(8,128)S(1)} %get-tuple-element.289), channel_id=1, source_target_pairs={{0,2},{1,3},{2,0},{3,1},{4,6},{5,7},{6,4},{7,5},{8,10},{9,11},{10,... | collective-permute-start | bytes 589832 | tf_op jit(solution)/shard_map/send_4_6/ppermute | solution.py:31
  122.9 3.9 %collective-permute-done.36.recv_in = f32[2,64,512]{2,1,0:T(8,128)S(1)} collective-permute-done((f32[2,64,512]{2,1,0:T(8,128)S(1)}, f32[2,64,512]{2,1,0:T(8,128)S(1)}, u32[]{:S(2)}, u32[]{:S(2)}) %collective-permute-start.36) | collective-permute-done | bytes 262176 | tf_op jit(solution)/shard_map/send_3_6/ppermute | solution.py:31
  129.0 2.5 %collective-permute-done.38.recv_in = f32[2,64,384]{2,1,0:T(8,128)S(1)} collective-permute-done((f32[2,64,384]{2,1,0:T(8,128)S(1)}, f32[2,64,384]{2,1,0:T(8,128)S(1)}, u32[]{:S(2)}, u32[]{:S(2)}) %collective-permute-start.38) | collective-permute-done | bytes 196640 | tf_op jit(solution)/shard_map/send_4_6/ppermute | solution.py:31
  131.9 3.5 %collective-permute-start.40 = (f32[2,64,384]{2,1,0:T(8,128)S(1)}, f32[2,64,384]{2,1,0:T(8,128)S(1)}, u32[]{:S(2)}, u32[]{:S(2)}) collective-permute-start(f32[2,64,384]{2,1,0:T(8,128)S(1)} %get-tuple-element.296), channel_id=1, source_target_pairs={{0,4},{1,5},{2,6},{3,7},{4,0},{5,1},{6,2},{7,3},{8,12},{9,13},{10,... | collective-permute-start | bytes 589832 | tf_op jit(solution)/shard_map/send_4_7/ppermute | solution.py:31
  135.4 9.0 %collective-permute-done.39.recv_in = f32[2,64,512]{2,1,0:T(8,128)S(1)} collective-permute-done((f32[2,64,512]{2,1,0:T(8,128)S(1)}, f32[2,64,512]{2,1,0:T(8,128)S(1)}, u32[]{:S(2)}, u32[]{:S(2)}) %collective-permute-start.39) | collective-permute-done | bytes 262176 | tf_op jit(solution)/shard_map/send_3_7/ppermute | solution.py:31
  (127 shorter events, 64.2 us)
Async XLA Ops:
  2.2 11.5 %collective-permute-start = (f32[2,64,256]{2,1,0:T(8,128)}, f32[2,64,256]{2,1,0:T(8,128)S(1)}, u32[]{:S(2)}, u32[]{:S(2)}) collective-permute-start(f32[2,64,256]{2,1,0:T(8,128)} %get-tuple-element.157), channel_id=1, source_target_pairs={{0,16},{8,24},{16,0},{24,8},{1,17},{9,25},{17,1},{25,9},{2,18},{10... | collective-permute-start | bytes 393224 | tf_op jit(solution)/shard_map/send_0_0/ppermute | solution.py:31
  15.2 11.7 %collective-permute-start.7 = (f32[2,64,512]{2,1,0:T(8,128)S(1)}, f32[2,64,512]{2,1,0:T(8,128)S(1)}, u32[]{:S(2)}, u32[]{:S(2)}) collective-permute-start(f32[2,64,512]{2,1,0:T(8,128)S(1)} %get-tuple-element.178), channel_id=1, source_target_pairs={{0,16},{8,24},{16,0},{24,8},{1,17},{9,25},{17,1},{25,9},{2,18},{10... | collective-permute-start | bytes 786440 | tf_op jit(solution)/shard_map/send_3_0/ppermute | solution.py:31
  16.8 16.7 %collective-permute-start.11 = (f32[2,64,384]{2,1,0:T(8,128)S(1)}, f32[2,64,384]{2,1,0:T(8,128)S(1)}, u32[]{:S(2)}, u32[]{:S(2)}) collective-permute-start(f32[2,64,384]{2,1,0:T(8,128)S(1)} %get-tuple-element.191), channel_id=1, source_target_pairs={{0,16},{8,24},{16,0},{24,8},{1,17},{9,25},{17,1},{25,9},{2,18},{10... | collective-permute-start | bytes 589832 | tf_op jit(solution)/shard_map/send_4_0/ppermute | solution.py:31
  29.9 10.0 %collective-permute-start.14 = (f32[2,64,384]{2,1,0:T(8,128)S(1)}, f32[2,64,384]{2,1,0:T(8,128)S(1)}, u32[]{:S(2)}, u32[]{:S(2)}) collective-permute-start(f32[2,64,384]{2,1,0:T(8,128)S(1)} %get-tuple-element.200), channel_id=1, source_target_pairs={{0,2},{1,3},{2,0},{3,1},{4,6},{5,7},{6,4},{7,5},{8,10},{9,11},{10,... | collective-permute-start | bytes 589832 | tf_op jit(solution)/shard_map/send_1_3/ppermute | solution.py:31
  37.0 13.3 %collective-permute-start.18 = (f32[2,64,512]{2,1,0:T(8,128)S(1)}, f32[2,64,512]{2,1,0:T(8,128)S(1)}, u32[]{:S(2)}, u32[]{:S(2)}) collective-permute-start(f32[2,64,512]{2,1,0:T(8,128)S(1)} %get-tuple-element.211), channel_id=1, source_target_pairs={{0,2},{1,3},{2,0},{3,1},{4,6},{5,7},{6,4},{7,5},{8,10},{9,11},{10,... | collective-permute-start | bytes 786440 | tf_op jit(solution)/shard_map/send_2_3/ppermute | solution.py:31
  40.3 10.8 %collective-permute-start.19 = (f32[2,64,384]{2,1,0:T(8,128)S(1)}, f32[2,64,384]{2,1,0:T(8,128)S(1)}, u32[]{:S(2)}, u32[]{:S(2)}) collective-permute-start(f32[2,64,384]{2,1,0:T(8,128)S(1)} %get-tuple-element.213), channel_id=1, source_target_pairs={{0,4},{1,5},{2,6},{3,7},{4,0},{5,1},{6,2},{7,3},{8,12},{9,13},{10,... | collective-permute-start | bytes 589832 | tf_op jit(solution)/shard_map/send_1_4/ppermute | solution.py:31
  41.5 9.6 %collective-permute-start.20 = (f32[2,64,384]{2,1,0:T(8,128)S(1)}, f32[2,64,384]{2,1,0:T(8,128)S(1)}, u32[]{:S(2)}, u32[]{:S(2)}) collective-permute-start(f32[2,64,384]{2,1,0:T(8,128)S(1)} %get-tuple-element.216), channel_id=1, source_target_pairs={{0,1},{1,0},{2,3},{3,2},{4,5},{5,4},{6,7},{7,6},{8,9},{9,8},{10,11... | collective-permute-start | bytes 589832 | tf_op jit(solution)/shard_map/send_4_2/ppermute | solution.py:31
  43.7 16.4 %collective-permute-start.21 = (f32[2,64,512]{2,1,0:T(8,128)S(1)}, f32[2,64,512]{2,1,0:T(8,128)S(1)}, u32[]{:S(2)}, u32[]{:S(2)}) collective-permute-start(f32[2,64,512]{2,1,0:T(8,128)S(1)} %get-tuple-element.219), channel_id=1, source_target_pairs={{0,2},{1,3},{2,0},{3,1},{4,6},{5,7},{6,4},{7,5},{8,10},{9,11},{10,... | collective-permute-start | bytes 786440 | tf_op jit(solution)/shard_map/send_3_3/ppermute | solution.py:31
  50.6 14.1 %collective-permute-start.22 = (f32[2,64,512]{2,1,0:T(8,128)S(1)}, f32[2,64,512]{2,1,0:T(8,128)S(1)}, u32[]{:S(2)}, u32[]{:S(2)}) collective-permute-start(f32[2,64,512]{2,1,0:T(8,128)S(1)} %get-tuple-element.221), channel_id=1, source_target_pairs={{0,4},{1,5},{2,6},{3,7},{4,0},{5,1},{6,2},{7,3},{8,12},{9,13},{10,... | collective-permute-start | bytes 786440 | tf_op jit(solution)/shard_map/send_2_4/ppermute | solution.py:31
  51.5 16.0 %collective-permute-start.23 = (f32[2,64,384]{2,1,0:T(8,128)S(1)}, f32[2,64,384]{2,1,0:T(8,128)S(1)}, u32[]{:S(2)}, u32[]{:S(2)}) collective-permute-start(f32[2,64,384]{2,1,0:T(8,128)S(1)} %get-tuple-element.224), channel_id=1, source_target_pairs={{0,2},{1,3},{2,0},{3,1},{4,6},{5,7},{6,4},{7,5},{8,10},{9,11},{10,... | collective-permute-start | bytes 589832 | tf_op jit(solution)/shard_map/send_4_3/ppermute | solution.py:31
  60.5 20.0 %collective-permute-start.24 = (f32[2,64,512]{2,1,0:T(8,128)S(1)}, f32[2,64,512]{2,1,0:T(8,128)S(1)}, u32[]{:S(2)}, u32[]{:S(2)}) collective-permute-start(f32[2,64,512]{2,1,0:T(8,128)S(1)} %get-tuple-element.226), channel_id=1, source_target_pairs={{0,4},{1,5},{2,6},{3,7},{4,0},{5,1},{6,2},{7,3},{8,12},{9,13},{10,... | collective-permute-start | bytes 786440 | tf_op jit(solution)/shard_map/send_3_4/ppermute | solution.py:31
  67.9 15.4 %collective-permute-start.25 = (f32[2,64,384]{2,1,0:T(8,128)S(1)}, f32[2,64,384]{2,1,0:T(8,128)S(1)}, u32[]{:S(2)}, u32[]{:S(2)}) collective-permute-start(f32[2,64,384]{2,1,0:T(8,128)S(1)} %get-tuple-element.228), channel_id=1, source_target_pairs={{0,4},{1,5},{2,6},{3,7},{4,0},{5,1},{6,2},{7,3},{8,12},{9,13},{10,... | collective-permute-start | bytes 589832 | tf_op jit(solution)/shard_map/send_4_4/ppermute | solution.py:31
  93.4 10.0 %collective-permute-start.29 = (f32[2,64,512]{2,1,0:T(8,128)S(1)}, f32[2,64,512]{2,1,0:T(8,128)S(1)}, u32[]{:S(2)}, u32[]{:S(2)}) collective-permute-start(f32[2,64,512]{2,1,0:T(8,128)S(1)} %get-tuple-element.257), channel_id=1, source_target_pairs={{0,1},{1,0},{2,3},{3,2},{4,5},{5,4},{6,7},{7,6},{8,9},{9,8},{10,11... | collective-permute-start | bytes 786440 | tf_op jit(solution)/shard_map/send_2_5/ppermute | solution.py:31
  95.3 11.1 %collective-permute-start.30 = (f32[2,64,384]{2,1,0:T(8,128)S(1)}, f32[2,64,384]{2,1,0:T(8,128)S(1)}, u32[]{:S(2)}, u32[]{:S(2)}) collective-permute-start(f32[2,64,384]{2,1,0:T(8,128)S(1)} %get-tuple-element.260), channel_id=1, source_target_pairs={{0,2},{1,3},{2,0},{3,1},{4,6},{5,7},{6,4},{7,5},{8,10},{9,11},{10,... | collective-permute-start | bytes 589832 | tf_op jit(solution)/shard_map/send_1_6/ppermute | solution.py:31
  99.2 10.9 %collective-permute-start.31 = (f32[2,64,256]{2,1,0:T(8,128)S(1)}, f32[2,64,256]{2,1,0:T(8,128)S(1)}, u32[]{:S(2)}, u32[]{:S(2)}) collective-permute-start(f32[2,64,256]{2,1,0:T(8,128)S(1)} %get-tuple-element.266), channel_id=1, source_target_pairs={{0,4},{1,5},{2,6},{3,7},{4,0},{5,1},{6,2},{7,3},{8,12},{9,13},{10,... | collective-permute-start | bytes 393224 | tf_op jit(solution)/shard_map/send_0_7/ppermute | solution.py:31
  102.0 9.5 %collective-permute-start.32 = (f32[2,64,512]{2,1,0:T(8,128)S(1)}, f32[2,64,512]{2,1,0:T(8,128)S(1)}, u32[]{:S(2)}, u32[]{:S(2)}) collective-permute-start(f32[2,64,512]{2,1,0:T(8,128)S(1)} %get-tuple-element.269), channel_id=1, source_target_pairs={{0,1},{1,0},{2,3},{3,2},{4,5},{5,4},{6,7},{7,6},{8,9},{9,8},{10,11... | collective-permute-start | bytes 786440 | tf_op jit(solution)/shard_map/send_3_5/ppermute | solution.py:31
  103.9 13.1 %collective-permute-start.33 = (f32[2,64,512]{2,1,0:T(8,128)S(1)}, f32[2,64,512]{2,1,0:T(8,128)S(1)}, u32[]{:S(2)}, u32[]{:S(2)}) collective-permute-start(f32[2,64,512]{2,1,0:T(8,128)S(1)} %get-tuple-element.272), channel_id=1, source_target_pairs={{0,2},{1,3},{2,0},{3,1},{4,6},{5,7},{6,4},{7,5},{8,10},{9,11},{10,... | collective-permute-start | bytes 786440 | tf_op jit(solution)/shard_map/send_2_6/ppermute | solution.py:31
  106.8 11.2 %collective-permute-start.34 = (f32[2,64,384]{2,1,0:T(8,128)S(1)}, f32[2,64,384]{2,1,0:T(8,128)S(1)}, u32[]{:S(2)}, u32[]{:S(2)}) collective-permute-start(f32[2,64,384]{2,1,0:T(8,128)S(1)} %get-tuple-element.275), channel_id=1, source_target_pairs={{0,4},{1,5},{2,6},{3,7},{4,0},{5,1},{6,2},{7,3},{8,12},{9,13},{10,... | collective-permute-start | bytes 589832 | tf_op jit(solution)/shard_map/send_1_7/ppermute | solution.py:31
  108.7 11.1 %collective-permute-start.35 = (f32[2,64,384]{2,1,0:T(8,128)S(1)}, f32[2,64,384]{2,1,0:T(8,128)S(1)}, u32[]{:S(2)}, u32[]{:S(2)}) collective-permute-start(f32[2,64,384]{2,1,0:T(8,128)S(1)} %get-tuple-element.279), channel_id=1, source_target_pairs={{0,1},{1,0},{2,3},{3,2},{4,5},{5,4},{6,7},{7,6},{8,9},{9,8},{10,11... | collective-permute-start | bytes 589832 | tf_op jit(solution)/shard_map/send_4_5/ppermute | solution.py:31
  111.9 14.8 %collective-permute-start.36 = (f32[2,64,512]{2,1,0:T(8,128)S(1)}, f32[2,64,512]{2,1,0:T(8,128)S(1)}, u32[]{:S(2)}, u32[]{:S(2)}) collective-permute-start(f32[2,64,512]{2,1,0:T(8,128)S(1)} %get-tuple-element.282), channel_id=1, source_target_pairs={{0,2},{1,3},{2,0},{3,1},{4,6},{5,7},{6,4},{7,5},{8,10},{9,11},{10,... | collective-permute-start | bytes 786440 | tf_op jit(solution)/shard_map/send_3_6/ppermute | solution.py:31
  117.3 10.0 %collective-permute-start.37 = (f32[2,64,512]{2,1,0:T(8,128)S(1)}, f32[2,64,512]{2,1,0:T(8,128)S(1)}, u32[]{:S(2)}, u32[]{:S(2)}) collective-permute-start(f32[2,64,512]{2,1,0:T(8,128)S(1)} %get-tuple-element.285), channel_id=1, source_target_pairs={{0,4},{1,5},{2,6},{3,7},{4,0},{5,1},{6,2},{7,3},{8,12},{9,13},{10,... | collective-permute-start | bytes 786440 | tf_op jit(solution)/shard_map/send_2_7/ppermute | solution.py:31
  120.1 11.4 %collective-permute-start.38 = (f32[2,64,384]{2,1,0:T(8,128)S(1)}, f32[2,64,384]{2,1,0:T(8,128)S(1)}, u32[]{:S(2)}, u32[]{:S(2)}) collective-permute-start(f32[2,64,384]{2,1,0:T(8,128)S(1)} %get-tuple-element.289), channel_id=1, source_target_pairs={{0,2},{1,3},{2,0},{3,1},{4,6},{5,7},{6,4},{7,5},{8,10},{9,11},{10,... | collective-permute-start | bytes 589832 | tf_op jit(solution)/shard_map/send_4_6/ppermute | solution.py:31
  127.2 17.3 %collective-permute-start.39 = (f32[2,64,512]{2,1,0:T(8,128)S(1)}, f32[2,64,512]{2,1,0:T(8,128)S(1)}, u32[]{:S(2)}, u32[]{:S(2)}) collective-permute-start(f32[2,64,512]{2,1,0:T(8,128)S(1)} %get-tuple-element.292), channel_id=1, source_target_pairs={{0,4},{1,5},{2,6},{3,7},{4,0},{5,1},{6,2},{7,3},{8,12},{9,13},{10,... | collective-permute-start | bytes 786440 | tf_op jit(solution)/shard_map/send_3_7/ppermute | solution.py:31
  131.9 15.3 %collective-permute-start.40 = (f32[2,64,384]{2,1,0:T(8,128)S(1)}, f32[2,64,384]{2,1,0:T(8,128)S(1)}, u32[]{:S(2)}, u32[]{:S(2)}) collective-permute-start(f32[2,64,384]{2,1,0:T(8,128)S(1)} %get-tuple-element.296), channel_id=1, source_target_pairs={{0,4},{1,5},{2,6},{3,7},{4,0},{5,1},{6,2},{7,3},{8,12},{9,13},{10,... | collective-permute-start | bytes 589832 | tf_op jit(solution)/shard_map/send_4_7/ppermute | solution.py:31
  (26 other events, 164.0 us)

commit v2 on v1

--- a/solution.py
+++ b/solution.py
@@ -9,10 +9,12 @@
 
 BF = jnp.bfloat16
 F32 = jnp.float32
-FIRST_SIXTEENTHS = (2, 3, 4, 4, 3)
-SECOND_SIXTEENTHS = (2, 3, 4, 4, 3)
+FIRST_SIXTEENTHS = (3, 3, 4, 4, 2)
+SECOND_SIXTEENTHS = (3, 4, 4, 3, 2)
 FIRST_STARTS = (0, 0, 1, 3, 6)
-SECOND_STARTS = (0, 0, 1, 3, 5)
+SECOND_STARTS = (0, 1, 3, 5, 7)
+ORDER_USED = (2, 3)
+LATE_ROWS = 32
 TILE = 256
 
 
@@ -93,19 +95,26 @@
     return jnp.concatenate([keep[0], recv[0], keep[1], recv[1]], axis=0)
 
 
-def in_turn(starts, steps, begin, go_on):
-    pending, used, part = [], 0, 0
-    while part < len(starts) or pending:
-        if part < len(starts) and (used >= starts[part] or not pending):
-            begin(part)
-            pending.append((part, 1))
-            part += 1
-            continue
-        at, step = pending.pop(0)
-        go_on(at, step)
-        used += 1
-        if step < steps:
-            pending.append((at, step + 1))
+def in_turn(first, second):
+    pending, used, begun, ready = [], [0, 0], [0, 0], 0
+    phases = (first, second)
+    while pending or begun[1] < len(second[0]):
+        for phase, (starts, _, begin, _) in enumerate(phases):
+            part = begun[phase]
+            open_now = phase == 0 or ready == len(first[0])
+            if part < len(starts) and open_now and (used[phase] >= starts[part] or not pending):
+                begin(part)
+                pending.append((phase, part, 1))
+                begun[phase] += 1
+                break
+        else:
+            phase, part, step = pending.pop(0)
+            _, steps, _, go_on = phases[phase]
+            used = [used[0] + 1, used[1] + (ready == len(first[0]))]
+            go_on(part, step)
+            ready += phase == 0 and step == steps - 1
+            if step < steps:
+                pending.append((phase, part, step + 1))
 
 
 def leaf_kernel(level, parts, field_ref, leaf_ref, *refs):
@@ -144,25 +153,39 @@
 
 
 def put_terms(values, out_ref, cols):
-    half = values[0].shape[0]
-    for part in range(2):
-        high, low = split(values[part])
-        out_ref[part * half : (part + 1) * half, cols] = high
-        out_ref[(2 + part) * half : (3 + part) * half, cols] = low
-
-
-def level_kernel(before_switch, turn, w, keep_in, recv_in, *refs):
+    at = 0
+    for terms in zip(*(split(value) for value in values)):
+        for term in terms:
+            out_ref[at : at + term.shape[0], cols] = term
+            at += term.shape[0]
+
+
+def level_kernel(turn, w, keep_in, recv_in, *refs):
     keep_ref, send_ref, _ = refs[-3:]
     for cols in tiles(send_ref.shape[2]):
         z = split(stacked(keep_in[:, :, cols], recv_in[:, :, cols]))
+        put_halves(product(w, z), keep_ref, send_ref, cols)
+
+
+def ready_kernel(turn, w, keep_in, recv_in, *refs):
+    own_ref, send_ref, _ = refs[-3:]
+    early = send_ref.shape[1]
+    for cols in tiles(send_ref.shape[2]):
+        z = split(stacked(keep_in[:, :, cols], recv_in[:, :, cols]))
         result = product(w, z)
-        if before_switch:
-            half = result.shape[0] // 4
-            parts = [result[at * half : (at + 1) * half] for at in range(4)]
-            put_terms((parts[0], parts[2]), keep_ref, cols)
-            send_ref[0, :, cols], send_ref[1, :, cols] = parts[1], parts[3]
-        else:
-            put_halves(result, keep_ref, send_ref, cols)
+        slots = result.shape[0] // 2
+        half = slots // 2
+        own = []
+        for part in range(2):
+            rows = result[part * slots : (part + 1) * slots]
+            own.append(jnp.concatenate([rows[:half], rows[half + early :]], axis=0))
+            send_ref[part, :, cols] = rows[half : half + early]
+        put_terms(own, own_ref, cols)
+
+
+def terms_kernel(turn, part_ref, out_ref, next_turn):
+    for cols in tiles(part_ref.shape[2]):
+        put_terms([part_ref[0, :, cols], part_ref[1, :, cols]], out_ref, cols)
 
 
 def picked(perm, parts, width):
@@ -175,31 +198,45 @@
             here = dot(part[:, rows], chosen)
             total = here if total is None else total + here
             at += depth
-    return total.astype(BF)
-
-
-def switch_kernel(start, turn, w, own_perm, other_perm, *refs):
-    *parts, keep_ref, send_ref, next_turn = refs
-    kept, received = parts[: len(parts) // 2], parts[len(parts) // 2 :]
-    half = keep_ref.shape[1]
-    for cols in tiles(keep_ref.shape[2]):
-        width = cols.stop - cols.start
+    return total
+
+
+def pick_own_kernel(start, turn, own_perm, *refs):
+    *own, keep_ref, send_ref, _ = refs
+    half, late = keep_ref.shape[0] // 4, send_ref.shape[1]
+    for cols in tiles(send_ref.shape[2]):
         where = slice(start + cols.start, start + cols.stop)
-        keep = picked(own_perm[:, where], kept, width)
-        recv = picked(other_perm[:, where], received, width)
-        z = [
-            stacked(
-                [keep[at : at + half], keep[at + half : at + 2 * half]],
-                [recv[at : at + half], recv[at + half : at + 2 * half]],
-            )
-            for at in (0, 2 * half)
-        ]
+        rows = picked(own_perm[:, where], own, cols.stop - cols.start)
+        at = 0
+        for term in range(2):
+            for part in range(2):
+                to = (2 * term + part) * half
+                keep_ref[to : to + half, cols] = rows[at : at + half].astype(BF)
+                at += half + late
+        high, low = rows[: 2 * (half + late)], rows[2 * (half + late) :]
+        for part in range(2):
+            at = part * (half + late) + half
+            send_ref[part, :, cols] = high[at : at + late] + low[at : at + late]
+
+
+def switch_kernel(start, turn, w, other_perm, keep_in, late_in, *refs):
+    *early, keep_ref, send_ref, _ = refs
+    half, late = keep_ref.shape[1], late_in.shape[1]
+    rest = half - late
+    for cols in tiles(send_ref.shape[2]):
+        where = slice(start + cols.start, start + cols.stop)
+        recv = picked(other_perm[:, where], early, cols.stop - cols.start).astype(BF)
+        late_terms = [split(late_in[part, :, cols]) for part in range(2)]
+        z = []
+        for term in range(2):
+            rows = []
+            for part in range(2):
+                at = 2 * term + part
+                rows.append(keep_in[at * half : (at + 1) * half, cols])
+                rows.append(recv[at * rest : (at + 1) * rest])
+                rows.append(late_terms[part][term])
+            z.append(jnp.concatenate(rows, axis=0))
         put_halves(product(w, z), keep_ref, send_ref, cols)
-
-
-def terms_kernel(turn, part_ref, out_ref, next_turn):
-    for cols in tiles(part_ref.shape[2]):
-        put_terms(part_ref[:, :, cols], out_ref, cols)
 
 
 def last_kernel(turn, w, c, measured_ref, keep_in, recv_in, *rest):
@@ -233,6 +270,7 @@
     _, _, cells, boxes = wavefield.shape
     level_count, slots = factors.shape[0], factors.shape[3]
     half = slots // 2
+    late = half * LATE_ROWS // 64
     levels = levels_of(level_count, lax.axis_size("dev"))
     switch_at = level_count // 2
     first, second = cuts(FIRST_SIXTEENTHS, boxes), cuts(SECOND_SIXTEENTHS, boxes)
@@ -293,28 +331,34 @@
         )
         return perm, closing_terms, factor_terms
 
-    def terms_of(width):
-        return jax.ShapeDtypeStruct((4 * half, width), BF)
-
-    def level(w, keep, recv, before_switch=False, also=()):
+    def terms_of(rows, width):
+        return jax.ShapeDtypeStruct((4 * rows, width), BF)
+
+    def block_of(rows, width):
+        return jax.ShapeDtypeStruct((2, rows, width), F32)
+
+    def level(w, keep, recv, ready=False, also=()):
         width = recv.shape[2]
         shapes = halves(width)
-        if before_switch:
-            shapes[0] = terms_of(width)
-        kernel = functools.partial(level_kernel, before_switch)
+        if ready:
+            shapes = [terms_of(half + late, width), block_of(half - late, width)]
         ins = [whole()] * 3 + [anywhere()] * len(also)
-        return call(kernel, ins, [w, keep, recv, *also], shapes)
+        return call(ready_kernel if ready else level_kernel, ins, [w, keep, recv, *also], shapes)
 
     def terms(block):
-        return call(terms_kernel, [whole()], [block], [terms_of(block.shape[2])])[0]
-
-    def switch(part, w, own_perm, other_perm, keep, recv):
+        return call(terms_kernel, [whole()], [block], [terms_of(*block.shape[1:])])[0]
+
+    def pick_own(part, own_perm, parts):
         at, width = part
-        return call(
-            functools.partial(switch_kernel, at),
-            [whole()] * (3 + len(keep) + len(recv)), [w, own_perm, other_perm, *keep, *recv],
-            halves(width),
-        )
+        kernel = functools.partial(pick_own_kernel, at)
+        shapes = [terms_of(half, width), block_of(late, width)]
+        return call(kernel, [whole()] * (1 + len(parts)), [own_perm, *parts], shapes)
+
+    def switch(part, w, other_perm, keep, late_rows, early):
+        at, width = part
+        kernel = functools.partial(switch_kernel, at)
+        args = [w, other_perm, keep, late_rows, *early]
+        return call(kernel, [whole()] * len(args), args, halves(width))
 
     def last(part, w, c, keep, recv, so_far):
         at, width = part
@@ -353,30 +397,36 @@
             away[part] = terms(away[part])
         else:
             w = factor_terms[step - 1]
-            also = [other_perm] if (part, step) == (0, 1) else []
+            also = [other_perm] if (part, step) == ORDER_USED else []
             leave(part, step, *level(w, own[part], away[part], step == switch_at, also))
-
-    in_turn(FIRST_STARTS, switch_at + 1, first_begin, first_step)
-    kept, received = ([held[part] for part in range(len(first))] for held in (own, away))
-    out = None
 
     def second_begin(part):
         nonlocal name
-        name = f"again_{part}_{switch_at}"
-        w = factor_terms[switch_at]
-        leave(part, switch_at + 1, *switch(second[part], w, own_perm, other_perm, kept, received))
+        name = f"again_{part}_{switch_at - 1}"
+        kept = [own[n] for n in range(len(first))]
+        keep, send = pick_own(second[part], own_perm, kept)
+        own2[part], away2[part] = keep, swapped(send, levels[switch_at], f"send_{part}_late")
 
     def second_step(part, step):
         nonlocal name, out
-        step += switch_at
+        step += switch_at - 1
         name = f"again_{part}_{step}"
         w = factor_terms[step]
         if step == level_count - 1:
-            out = last(second[part], w, closing_terms, own[part], away[part], out)
+            out = last(second[part], w, closing_terms, own2[part], away2[part], out)
+            return
+        if step == switch_at:
+            early = [away[n] for n in range(len(first))]
+            keep, send = switch(second[part], w, other_perm, own2[part], away2[part], early)
         else:
-            leave(part, step + 1, *level(w, own[part], away[part]))
-
-    in_turn(SECOND_STARTS, level_count - 1 - switch_at, second_begin, second_step)
+            keep, send = level(w, own2[part], away2[part])
+        own2[part], away2[part] = keep, swapped(send, levels[step + 1], f"send_{part}_{step + 1}")
+
+    own2, away2, out = {}, {}, None
+    in_turn(
+        (FIRST_STARTS, switch_at + 1, first_begin, first_step),
+        (SECOND_STARTS, level_count - switch_at, second_begin, second_step),
+    )
     return out
 
 

time: 150 us -> 146 us (0.973)
  starting transfers between devices: 53.6 us -> 47 us
  Pallas kernels: 33 us -> 35.1 us
    ppermute x41 -> x46, starting transfers between devices: 53.6 us -> 47 us  [swapped(): return lax.ppermute(block, axis, [(i, i ^ 1 << bit) for i in range(count)])]
    pallas_call x46 -> x51, Pallas kernels: 28.9 us -> 30.9 us  [call(): pl.pallas_call(kernel, in_specs=[anywhere(), *ins], out_specs=[*more.pop(...]
    ppermute x41 -> x46, waiting for transfers between devices: 61.1 us -> 62.3 us  [swapped(): return lax.ppermute(block, axis, [(i, i ^ 1 << bit) for i in range(count)])]
  transfers between devices with their start and end apart: 41 -> 46, of which waited for: 22 -> 24; matrix products, arithmetic and copies ran while one was open for 0% -> 0% of each run, Pallas kernels for 19% -> 22%
where the time goes in v2:
time: 146 us
  waiting for transfers between devices  62.3 us (43%)
  starting transfers between devices  47 us (32%)
  Pallas kernels  35.1 us (24%)
    ppermute x46, waiting for transfers between devices, swapped(): return lax.ppermute(block, axis, [(i, i ^ 1 << bit) for i in range(count)])  62.3 us
    ppermute x46, starting transfers between devices, swapped(): return lax.ppermute(block, axis, [(i, i ^ 1 << bit) for i in range(count)])  47 us
    pallas_call x51, Pallas kernels, call(): pl.pallas_call(kernel, in_specs=[anywhere(), *ins], out_specs=[*more.pop(...  30.9 us
    pallas_call x2, Pallas kernels, leaf(): pl.pallas_call(kernel, in_specs=ins, out_specs=[*[whole()] * (2 * len(par...  4.21 us
  transfers between devices with their start and end apart: 46, of which 24 were waited for; matrix products, arithmetic and copies ran while one was open for 0% of the time, Pallas kernels for 22%

profile of v2, /device:TPU:0, one launch (start us, length us, event | category | flops | bytes accessed | tf_op | source)
XLA Modules:
  0.0 145.8 jit_solution(10329809196749754698)
XLA Ops:
  0.0 2.3 %leaf.2 = (f32[2,64,384]{2,1,0:T(8,128)}, f32[2,64,384]{2,1,0:T(8,128)}, f32[8,128]{1,0:T(8,128)}) custom-call(f32[1,2,128,2048]{3,2,1,0:T(8,128)} %refs_0_.1, f32[1,2,128,128]{3,2,1,0:T(8,128)} %refs_1_.1), custom_call_target="tpu_custom_call" | custom-call | flops 1000000000 | bytes 2500000 | tf_op jit(solution)/shard_map/leaf/pallas_call | solution.py:307
  2.4 3.0 %collective-permute-start = (f32[2,64,384]{2,1,0:T(8,128)}, f32[2,64,384]{2,1,0:T(8,128)S(1)}, u32[]{:S(2)}, u32[]{:S(2)}) collective-permute-start(f32[2,64,384]{2,1,0:T(8,128)} %get-tuple-element.172), channel_id=1, source_target_pairs={{0,16},{8,24},{16,0},{24,8},{1,17},{9,25},{17,1},{25,9},{2,18},{10... | collective-permute-start | bytes 589832 | tf_op jit(solution)/shard_map/send_0_0/ppermute | solution.py:33
  6.1 1.9 %leaf.3 = (f32[2,64,384]{2,1,0:T(8,128)S(1)}, f32[2,64,384]{2,1,0:T(8,128)S(1)}, f32[2,64,512]{2,1,0:T(8,128)S(1)}, f32[2,64,512]{2,1,0:T(8,128)S(1)}, f32[2,64,...) custom-call(f32[8,128]{1,0:T(8,128)S(1)} %copy-done.7, ...), custom_call_target="tpu_custom_call" | custom-call | flops 1000000000 | bytes 2500000 | tf_op jit(solution)/shard_map/leaf/pallas_call | solution.py:307
  9.1 1.9 %collective-permute-done.recv_in = f32[2,64,384]{2,1,0:T(8,128)S(1)} collective-permute-done((f32[2,64,384]{2,1,0:T(8,128)}, f32[2,64,384]{2,1,0:T(8,128)S(1)}, u32[]{:S(2)}, u32[]{:S(2)}) %collective-permute-start) | collective-permute-done | bytes 196640 | tf_op jit(solution)/shard_map/send_0_0/ppermute | solution.py:33
  11.5 2.4 %collective-permute-start.3 = (f32[2,64,512]{2,1,0:T(8,128)S(1)}, f32[2,64,512]{2,1,0:T(8,128)S(1)}, u32[]{:S(2)}, u32[]{:S(2)}) collective-permute-start(f32[2,64,512]{2,1,0:T(8,128)S(1)} %get-tuple-element.182), channel_id=1, source_target_pairs={{0,16},{8,24},{16,0},{24,8},{1,17},{9,25},{17,1},{25,9},{2,18},{10... | collective-permute-start | bytes 786440 | tf_op jit(solution)/shard_map/send_2_0/ppermute | solution.py:33
  14.0 1.9 %collective-permute-start.10 = (f32[2,64,256]{2,1,0:T(8,128)S(1)}, f32[2,64,256]{2,1,0:T(8,128)S(1)}, u32[]{:S(2)}, u32[]{:S(2)}) collective-permute-start(f32[2,64,256]{2,1,0:T(8,128)S(1)} %get-tuple-element.205), channel_id=1, source_target_pairs={{0,16},{8,24},{16,0},{24,8},{1,17},{9,25},{17,1},{25,9},{2,18},{10... | collective-permute-start | bytes 393224 | tf_op jit(solution)/shard_map/send_4_0/ppermute | solution.py:33
  18.4 2.7 %collective-permute-done.3.recv_in = f32[2,64,512]{2,1,0:T(8,128)S(1)} collective-permute-done((f32[2,64,512]{2,1,0:T(8,128)S(1)}, f32[2,64,512]{2,1,0:T(8,128)S(1)}, u32[]{:S(2)}, u32[]{:S(2)}) %collective-permute-start.3) | collective-permute-done | bytes 262176 | tf_op jit(solution)/shard_map/send_2_0/ppermute | solution.py:33
  21.1 2.6 %collective-permute-start.13 = (s32[1,2048]{1,0:T(1,128)S(1)}, s32[1,2048]{1,0:T(1,128)S(1)}, u32[]{:S(2)}, u32[]{:S(2)}) collective-permute-start(s32[1,2048]{1,0:T(1,128)S(1)} %get-tuple-element.212.own_perm), channel_id=1, source_target_pairs={{0,4},{1,5},{2,6},{3,7},{4,0},{5,1},{6,2},{7,3},{8,12},{9,13},{10,... | collective-permute-start | bytes 24584 | tf_op jit(solution)/shard_map/send_order/ppermute | solution.py:33
  29.1 2.8 %collective-permute-done.8.recv_in = f32[2,64,384]{2,1,0:T(8,128)S(1)} collective-permute-done((f32[2,64,384]{2,1,0:T(8,128)S(1)}, f32[2,64,384]{2,1,0:T(8,128)S(1)}, u32[]{:S(2)}, u32[]{:S(2)}) %collective-permute-start.8) | collective-permute-done | bytes 196640 | tf_op jit(solution)/shard_map/send_1_2/ppermute | solution.py:33
  35.8 1.9 %collective-permute-start.15 = (f32[2,32,384]{2,1,0:T(8,128)S(1)}, f32[2,32,384]{2,1,0:T(8,128)S(1)}, u32[]{:S(2)}, u32[]{:S(2)}) collective-permute-start(f32[2,32,384]{2,1,0:T(8,128)S(1)} %get-tuple-element.217), channel_id=1, source_target_pairs={{0,4},{1,5},{2,6},{3,7},{4,0},{5,1},{6,2},{7,3},{8,12},{9,13},{10,... | collective-permute-start | bytes 294920 | tf_op jit(solution)/shard_map/send_0_4/ppermute | solution.py:33
  43.3 2.0 %collective-permute-start.20 = (f32[2,64,256]{2,1,0:T(8,128)S(1)}, f32[2,64,256]{2,1,0:T(8,128)S(1)}, u32[]{:S(2)}, u32[]{:S(2)}) collective-permute-start(f32[2,64,256]{2,1,0:T(8,128)S(1)} %get-tuple-element.231), channel_id=1, source_target_pairs={{0,1},{1,0},{2,3},{3,2},{4,5},{5,4},{6,7},{7,6},{8,9},{9,8},{10,11... | collective-permute-start | bytes 393224 | tf_op jit(solution)/shard_map/send_4_2/ppermute | solution.py:33
  45.4 2.2 %collective-permute-done.17.recv_in = f32[2,64,512]{2,1,0:T(8,128)S(1)} collective-permute-done((f32[2,64,512]{2,1,0:T(8,128)S(1)}, f32[2,64,512]{2,1,0:T(8,128)S(1)}, u32[]{:S(2)}, u32[]{:S(2)}) %collective-permute-start.17) | collective-permute-done | bytes 262176 | tf_op jit(solution)/shard_map/send_3_2/ppermute | solution.py:33
  48.5 3.2 %collective-permute-done.18.recv_in = f32[2,64,512]{2,1,0:T(8,128)S(1)} collective-permute-done((f32[2,64,512]{2,1,0:T(8,128)S(1)}, f32[2,64,512]{2,1,0:T(8,128)S(1)}, u32[]{:S(2)}, u32[]{:S(2)}) %collective-permute-start.18) | collective-permute-done | bytes 262176 | tf_op jit(solution)/shard_map/send_2_3/ppermute | solution.py:33
  54.0 6.2 %collective-permute-done.21.recv_in = f32[2,64,512]{2,1,0:T(8,128)S(1)} collective-permute-done((f32[2,64,512]{2,1,0:T(8,128)S(1)}, f32[2,64,512]{2,1,0:T(8,128)S(1)}, u32[]{:S(2)}, u32[]{:S(2)}) %collective-permute-start.21) | collective-permute-done | bytes 262176 | tf_op jit(solution)/shard_map/send_3_3/ppermute | solution.py:33
  66.8 6.4 %collective-permute-done.24.part_ref = f32[2,32,512]{2,1,0:T(8,128)S(1)} collective-permute-done((f32[2,32,512]{2,1,0:T(8,128)S(1)}, f32[2,32,512]{2,1,0:T(8,128)S(1)}, u32[]{:S(2)}, u32[]{:S(2)}) %collective-permute-start.24) | collective-permute-done | bytes 131104 | tf_op jit(solution)/shard_map/send_3_4/ppermute | solution.py:33
  74.6 2.1 %collective-permute-done.26.late_in = f32[2,32,384]{2,1,0:T(8,128)S(1)} collective-permute-done((f32[2,32,384]{2,1,0:T(8,128)S(1)}, f32[2,32,384]{2,1,0:T(8,128)S(1)}, u32[]{:S(2)}, u32[]{:S(2)}) %collective-permute-start.26) | collective-permute-done | bytes 98336 | tf_op jit(solution)/shard_map/send_0_late/ppermute | solution.py:33
  87.0 2.8 %collective-permute-start.32 = (f32[2,32,384]{2,1,0:T(8,128)S(1)}, f32[2,32,384]{2,1,0:T(8,128)S(1)}, u32[]{:S(2)}, u32[]{:S(2)}) collective-permute-start(f32[2,32,384]{2,1,0:T(8,128)S(1)} %get-tuple-element.282), channel_id=1, source_target_pairs={{0,4},{1,5},{2,6},{3,7},{4,0},{5,1},{6,2},{7,3},{8,12},{9,13},{10,... | collective-permute-start | bytes 294920 | tf_op jit(solution)/shard_map/send_3_late/ppermute | solution.py:33
  101.5 5.3 %collective-permute-done.34.recv_in = f32[2,64,512]{2,1,0:T(8,128)S(1)} collective-permute-done((f32[2,64,512]{2,1,0:T(8,128)S(1)}, f32[2,64,512]{2,1,0:T(8,128)S(1)}, u32[]{:S(2)}, u32[]{:S(2)}) %collective-permute-start.34) | collective-permute-done | bytes 262176 | tf_op jit(solution)/shard_map/send_1_6/ppermute | solution.py:33
  108.0 1.9 %collective-permute-start.40 = (f32[2,64,256]{2,1,0:T(8,128)S(1)}, f32[2,64,256]{2,1,0:T(8,128)S(1)}, u32[]{:S(2)}, u32[]{:S(2)}) collective-permute-start(f32[2,64,256]{2,1,0:T(8,128)S(1)} %get-tuple-element.309), channel_id=1, source_target_pairs={{0,1},{1,0},{2,3},{3,2},{4,5},{5,4},{6,7},{7,6},{8,9},{9,8},{10,11... | collective-permute-start | bytes 393224 | tf_op jit(solution)/shard_map/send_4_5/ppermute | solution.py:33
  112.0 1.9 %collective-permute-start.41 = (f32[2,64,384]{2,1,0:T(8,128)S(1)}, f32[2,64,384]{2,1,0:T(8,128)S(1)}, u32[]{:S(2)}, u32[]{:S(2)}) collective-permute-start(f32[2,64,384]{2,1,0:T(8,128)S(1)} %get-tuple-element.312), channel_id=1, source_target_pairs={{0,2},{1,3},{2,0},{3,1},{4,6},{5,7},{6,4},{7,5},{8,10},{9,11},{10,... | collective-permute-start | bytes 589832 | tf_op jit(solution)/shard_map/send_3_6/ppermute | solution.py:33
  113.9 3.4 %collective-permute-done.38.recv_in = f32[2,64,512]{2,1,0:T(8,128)S(1)} collective-permute-done((f32[2,64,512]{2,1,0:T(8,128)S(1)}, f32[2,64,512]{2,1,0:T(8,128)S(1)}, u32[]{:S(2)}, u32[]{:S(2)}) %collective-permute-start.38) | collective-permute-done | bytes 262176 | tf_op jit(solution)/shard_map/send_2_6/ppermute | solution.py:33
  117.8 4.1 %collective-permute-done.39.recv_in = f32[2,64,512]{2,1,0:T(8,128)S(1)} collective-permute-done((f32[2,64,512]{2,1,0:T(8,128)S(1)}, f32[2,64,512]{2,1,0:T(8,128)S(1)}, u32[]{:S(2)}, u32[]{:S(2)}) %collective-permute-start.39) | collective-permute-done | bytes 262176 | tf_op jit(solution)/shard_map/send_1_7/ppermute | solution.py:33
  126.4 10.0 %collective-permute-done.42.recv_in = f32[2,64,512]{2,1,0:T(8,128)S(1)} collective-permute-done((f32[2,64,512]{2,1,0:T(8,128)S(1)}, f32[2,64,512]{2,1,0:T(8,128)S(1)}, u32[]{:S(2)}, u32[]{:S(2)}) %collective-permute-start.42) | collective-permute-done | bytes 262176 | tf_op jit(solution)/shard_map/send_2_7/ppermute | solution.py:33
  141.7 2.7 %collective-permute-done.45.recv_in = f32[2,64,256]{2,1,0:T(8,128)S(1)} collective-permute-done((f32[2,64,256]{2,1,0:T(8,128)S(1)}, f32[2,64,256]{2,1,0:T(8,128)S(1)}, u32[]{:S(2)}, u32[]{:S(2)}) %collective-permute-start.45) | collective-permute-done | bytes 131104 | tf_op jit(solution)/shard_map/send_4_7/ppermute | solution.py:33
  (142 shorter events, 67.6 us)
Async XLA Ops:
  13.9 12.8 %collective-permute-start.6 = (f32[2,64,512]{2,1,0:T(8,128)S(1)}, f32[2,64,512]{2,1,0:T(8,128)S(1)}, u32[]{:S(2)}, u32[]{:S(2)}) collective-permute-start(f32[2,64,512]{2,1,0:T(8,128)S(1)} %get-tuple-element.192), channel_id=1, source_target_pairs={{0,16},{8,24},{16,0},{24,8},{1,17},{9,25},{17,1},{25,9},{2,18},{10... | collective-permute-start | bytes 786440 | tf_op jit(solution)/shard_map/send_3_0/ppermute | solution.py:33
  14.0 21.8 %collective-permute-start.10 = (f32[2,64,256]{2,1,0:T(8,128)S(1)}, f32[2,64,256]{2,1,0:T(8,128)S(1)}, u32[]{:S(2)}, u32[]{:S(2)}) collective-permute-start(f32[2,64,256]{2,1,0:T(8,128)S(1)} %get-tuple-element.205), channel_id=1, source_target_pairs={{0,16},{8,24},{16,0},{24,8},{1,17},{9,25},{17,1},{25,9},{2,18},{10... | collective-permute-start | bytes 393224 | tf_op jit(solution)/shard_map/send_4_0/ppermute | solution.py:33
  21.1 17.4 %collective-permute-start.13 = (s32[1,2048]{1,0:T(1,128)S(1)}, s32[1,2048]{1,0:T(1,128)S(1)}, u32[]{:S(2)}, u32[]{:S(2)}) collective-permute-start(s32[1,2048]{1,0:T(1,128)S(1)} %get-tuple-element.212.own_perm), channel_id=1, source_target_pairs={{0,4},{1,5},{2,6},{3,7},{4,0},{5,1},{6,2},{7,3},{8,12},{9,13},{10,... | collective-permute-start | bytes 24584 | tf_op jit(solution)/shard_map/send_order/ppermute | solution.py:33
  40.4 11.3 %collective-permute-start.18 = (f32[2,64,512]{2,1,0:T(8,128)S(1)}, f32[2,64,512]{2,1,0:T(8,128)S(1)}, u32[]{:S(2)}, u32[]{:S(2)}) collective-permute-start(f32[2,64,512]{2,1,0:T(8,128)S(1)} %get-tuple-element.226), channel_id=1, source_target_pairs={{0,2},{1,3},{2,0},{3,1},{4,6},{5,7},{6,4},{7,5},{8,10},{9,11},{10,... | collective-permute-start | bytes 786440 | tf_op jit(solution)/shard_map/send_2_3/ppermute | solution.py:33
  42.6 9.7 %collective-permute-start.19 = (f32[2,32,384]{2,1,0:T(8,128)S(1)}, f32[2,32,384]{2,1,0:T(8,128)S(1)}, u32[]{:S(2)}, u32[]{:S(2)}) collective-permute-start(f32[2,32,384]{2,1,0:T(8,128)S(1)} %get-tuple-element.228), channel_id=1, source_target_pairs={{0,4},{1,5},{2,6},{3,7},{4,0},{5,1},{6,2},{7,3},{8,12},{9,13},{10,... | collective-permute-start | bytes 294920 | tf_op jit(solution)/shard_map/send_1_4/ppermute | solution.py:33
  48.0 12.2 %collective-permute-start.21 = (f32[2,64,512]{2,1,0:T(8,128)S(1)}, f32[2,64,512]{2,1,0:T(8,128)S(1)}, u32[]{:S(2)}, u32[]{:S(2)}) collective-permute-start(f32[2,64,512]{2,1,0:T(8,128)S(1)} %get-tuple-element.234), channel_id=1, source_target_pairs={{0,2},{1,3},{2,0},{3,1},{4,6},{5,7},{6,4},{7,5},{8,10},{9,11},{10,... | collective-permute-start | bytes 786440 | tf_op jit(solution)/shard_map/send_3_3/ppermute | solution.py:33
  52.6 9.8 %collective-permute-start.23 = (f32[2,64,256]{2,1,0:T(8,128)S(1)}, f32[2,64,256]{2,1,0:T(8,128)S(1)}, u32[]{:S(2)}, u32[]{:S(2)}) collective-permute-start(f32[2,64,256]{2,1,0:T(8,128)S(1)} %get-tuple-element.239), channel_id=1, source_target_pairs={{0,2},{1,3},{2,0},{3,1},{4,6},{5,7},{6,4},{7,5},{8,10},{9,11},{10,... | collective-permute-start | bytes 393224 | tf_op jit(solution)/shard_map/send_4_3/ppermute | solution.py:33
  60.6 12.6 %collective-permute-start.24 = (f32[2,32,512]{2,1,0:T(8,128)S(1)}, f32[2,32,512]{2,1,0:T(8,128)S(1)}, u32[]{:S(2)}, u32[]{:S(2)}) collective-permute-start(f32[2,32,512]{2,1,0:T(8,128)S(1)} %get-tuple-element.247), channel_id=1, source_target_pairs={{0,4},{1,5},{2,6},{3,7},{4,0},{5,1},{6,2},{7,3},{8,12},{9,13},{10,... | collective-permute-start | bytes 393224 | tf_op jit(solution)/shard_map/send_3_4/ppermute | solution.py:33
  62.7 11.9 %collective-permute-start.25 = (f32[2,32,256]{2,1,0:T(8,128)S(1)}, f32[2,32,256]{2,1,0:T(8,128)S(1)}, u32[]{:S(2)}, u32[]{:S(2)}) collective-permute-start(f32[2,32,256]{2,1,0:T(8,128)S(1)} %get-tuple-element.250), channel_id=1, source_target_pairs={{0,4},{1,5},{2,6},{3,7},{4,0},{5,1},{6,2},{7,3},{8,12},{9,13},{10,... | collective-permute-start | bytes 196616 | tf_op jit(solution)/shard_map/send_4_4/ppermute | solution.py:33
  65.0 11.6 %collective-permute-start.26 = (f32[2,32,384]{2,1,0:T(8,128)S(1)}, f32[2,32,384]{2,1,0:T(8,128)S(1)}, u32[]{:S(2)}, u32[]{:S(2)}) collective-permute-start(f32[2,32,384]{2,1,0:T(8,128)S(1)} %get-tuple-element.254), channel_id=1, source_target_pairs={{0,4},{1,5},{2,6},{3,7},{4,0},{5,1},{6,2},{7,3},{8,12},{9,13},{10,... | collective-permute-start | bytes 294920 | tf_op jit(solution)/shard_map/send_0_late/ppermute | solution.py:33
  80.2 9.6 %collective-permute-start.29 = (f32[2,32,512]{2,1,0:T(8,128)S(1)}, f32[2,32,512]{2,1,0:T(8,128)S(1)}, u32[]{:S(2)}, u32[]{:S(2)}) collective-permute-start(f32[2,32,512]{2,1,0:T(8,128)S(1)} %get-tuple-element.271), channel_id=1, source_target_pairs={{0,4},{1,5},{2,6},{3,7},{4,0},{5,1},{6,2},{7,3},{8,12},{9,13},{10,... | collective-permute-start | bytes 393224 | tf_op jit(solution)/shard_map/send_2_late/ppermute | solution.py:33
  85.9 10.4 %collective-permute-start.31 = (f32[2,64,384]{2,1,0:T(8,128)S(1)}, f32[2,64,384]{2,1,0:T(8,128)S(1)}, u32[]{:S(2)}, u32[]{:S(2)}) collective-permute-start(f32[2,64,384]{2,1,0:T(8,128)S(1)} %get-tuple-element.279), channel_id=1, source_target_pairs={{0,2},{1,3},{2,0},{3,1},{4,6},{5,7},{6,4},{7,5},{8,10},{9,11},{10,... | collective-permute-start | bytes 589832 | tf_op jit(solution)/shard_map/send_0_6/ppermute | solution.py:33
  87.0 9.7 %collective-permute-start.32 = (f32[2,32,384]{2,1,0:T(8,128)S(1)}, f32[2,32,384]{2,1,0:T(8,128)S(1)}, u32[]{:S(2)}, u32[]{:S(2)}) collective-permute-start(f32[2,32,384]{2,1,0:T(8,128)S(1)} %get-tuple-element.282), channel_id=1, source_target_pairs={{0,4},{1,5},{2,6},{3,7},{4,0},{5,1},{6,2},{7,3},{8,12},{9,13},{10,... | collective-permute-start | bytes 294920 | tf_op jit(solution)/shard_map/send_3_late/ppermute | solution.py:33
  93.1 13.7 %collective-permute-start.34 = (f32[2,64,512]{2,1,0:T(8,128)S(1)}, f32[2,64,512]{2,1,0:T(8,128)S(1)}, u32[]{:S(2)}, u32[]{:S(2)}) collective-permute-start(f32[2,64,512]{2,1,0:T(8,128)S(1)} %get-tuple-element.288), channel_id=1, source_target_pairs={{0,2},{1,3},{2,0},{3,1},{4,6},{5,7},{6,4},{7,5},{8,10},{9,11},{10,... | collective-permute-start | bytes 786440 | tf_op jit(solution)/shard_map/send_1_6/ppermute | solution.py:33
  93.1 14.1 %collective-permute-start.35 = (f32[2,32,256]{2,1,0:T(8,128)S(1)}, f32[2,32,256]{2,1,0:T(8,128)S(1)}, u32[]{:S(2)}, u32[]{:S(2)}) collective-permute-start(f32[2,32,256]{2,1,0:T(8,128)S(1)} %get-tuple-element.291), channel_id=1, source_target_pairs={{0,4},{1,5},{2,6},{3,7},{4,0},{5,1},{6,2},{7,3},{8,12},{9,13},{10,... | collective-permute-start | bytes 196616 | tf_op jit(solution)/shard_map/send_4_late/ppermute | solution.py:33
  96.7 13.2 %collective-permute-start.36 = (f32[2,64,384]{2,1,0:T(8,128)S(1)}, f32[2,64,384]{2,1,0:T(8,128)S(1)}, u32[]{:S(2)}, u32[]{:S(2)}) collective-permute-start(f32[2,64,384]{2,1,0:T(8,128)S(1)} %get-tuple-element.296), channel_id=1, source_target_pairs={{0,4},{1,5},{2,6},{3,7},{4,0},{5,1},{6,2},{7,3},{8,12},{9,13},{10,... | collective-permute-start | bytes 589832 | tf_op jit(solution)/shard_map/send_0_7/ppermute | solution.py:33
  98.0 13.7 %collective-permute-start.37 = (f32[2,64,384]{2,1,0:T(8,128)S(1)}, f32[2,64,384]{2,1,0:T(8,128)S(1)}, u32[]{:S(2)}, u32[]{:S(2)}) collective-permute-start(f32[2,64,384]{2,1,0:T(8,128)S(1)} %get-tuple-element.299), channel_id=1, source_target_pairs={{0,1},{1,0},{2,3},{3,2},{4,5},{5,4},{6,7},{7,6},{8,9},{9,8},{10,11... | collective-permute-start | bytes 589832 | tf_op jit(solution)/shard_map/send_3_5/ppermute | solution.py:33
  100.2 17.2 %collective-permute-start.38 = (f32[2,64,512]{2,1,0:T(8,128)S(1)}, f32[2,64,512]{2,1,0:T(8,128)S(1)}, u32[]{:S(2)}, u32[]{:S(2)}) collective-permute-start(f32[2,64,512]{2,1,0:T(8,128)S(1)} %get-tuple-element.302), channel_id=1, source_target_pairs={{0,2},{1,3},{2,0},{3,1},{4,6},{5,7},{6,4},{7,5},{8,10},{9,11},{10,... | collective-permute-start | bytes 786440 | tf_op jit(solution)/shard_map/send_2_6/ppermute | solution.py:33
  107.2 14.7 %collective-permute-start.39 = (f32[2,64,512]{2,1,0:T(8,128)S(1)}, f32[2,64,512]{2,1,0:T(8,128)S(1)}, u32[]{:S(2)}, u32[]{:S(2)}) collective-permute-start(f32[2,64,512]{2,1,0:T(8,128)S(1)} %get-tuple-element.305), channel_id=1, source_target_pairs={{0,4},{1,5},{2,6},{3,7},{4,0},{5,1},{6,2},{7,3},{8,12},{9,13},{10,... | collective-permute-start | bytes 786440 | tf_op jit(solution)/shard_map/send_1_7/ppermute | solution.py:33
  108.0 15.5 %collective-permute-start.40 = (f32[2,64,256]{2,1,0:T(8,128)S(1)}, f32[2,64,256]{2,1,0:T(8,128)S(1)}, u32[]{:S(2)}, u32[]{:S(2)}) collective-permute-start(f32[2,64,256]{2,1,0:T(8,128)S(1)} %get-tuple-element.309), channel_id=1, source_target_pairs={{0,1},{1,0},{2,3},{3,2},{4,5},{5,4},{6,7},{7,6},{8,9},{9,8},{10,11... | collective-permute-start | bytes 393224 | tf_op jit(solution)/shard_map/send_4_5/ppermute | solution.py:33
  112.0 12.3 %collective-permute-start.41 = (f32[2,64,384]{2,1,0:T(8,128)S(1)}, f32[2,64,384]{2,1,0:T(8,128)S(1)}, u32[]{:S(2)}, u32[]{:S(2)}) collective-permute-start(f32[2,64,384]{2,1,0:T(8,128)S(1)} %get-tuple-element.312), channel_id=1, source_target_pairs={{0,2},{1,3},{2,0},{3,1},{4,6},{5,7},{6,4},{7,5},{8,10},{9,11},{10,... | collective-permute-start | bytes 589832 | tf_op jit(solution)/shard_map/send_3_6/ppermute | solution.py:33
  117.7 18.7 %collective-permute-start.42 = (f32[2,64,512]{2,1,0:T(8,128)S(1)}, f32[2,64,512]{2,1,0:T(8,128)S(1)}, u32[]{:S(2)}, u32[]{:S(2)}) collective-permute-start(f32[2,64,512]{2,1,0:T(8,128)S(1)} %get-tuple-element.315), channel_id=1, source_target_pairs={{0,4},{1,5},{2,6},{3,7},{4,0},{5,1},{6,2},{7,3},{8,12},{9,13},{10,... | collective-permute-start | bytes 786440 | tf_op jit(solution)/shard_map/send_2_7/ppermute | solution.py:33
  123.8 14.3 %collective-permute-start.43 = (f32[2,64,256]{2,1,0:T(8,128)S(1)}, f32[2,64,256]{2,1,0:T(8,128)S(1)}, u32[]{:S(2)}, u32[]{:S(2)}) collective-permute-start(f32[2,64,256]{2,1,0:T(8,128)S(1)} %get-tuple-element.319), channel_id=1, source_target_pairs={{0,2},{1,3},{2,0},{3,1},{4,6},{5,7},{6,4},{7,5},{8,10},{9,11},{10,... | collective-permute-start | bytes 393224 | tf_op jit(solution)/shard_map/send_4_6/ppermute | solution.py:33
  124.7 15.3 %collective-permute-start.44 = (f32[2,64,384]{2,1,0:T(8,128)S(1)}, f32[2,64,384]{2,1,0:T(8,128)S(1)}, u32[]{:S(2)}, u32[]{:S(2)}) collective-permute-start(f32[2,64,384]{2,1,0:T(8,128)S(1)} %get-tuple-element.322), channel_id=1, source_target_pairs={{0,4},{1,5},{2,6},{3,7},{4,0},{5,1},{6,2},{7,3},{8,12},{9,13},{10,... | collective-permute-start | bytes 589832 | tf_op jit(solution)/shard_map/send_3_7/ppermute | solution.py:33
  (31 other events, 208.9 us)

commit v3 on v2

--- a/solution.py
+++ b/solution.py
@@ -10,11 +10,11 @@
 BF = jnp.bfloat16
 F32 = jnp.float32
 FIRST_SIXTEENTHS = (3, 3, 4, 4, 2)
-SECOND_SIXTEENTHS = (3, 4, 4, 3, 2)
+SECOND_SIXTEENTHS = (3, 3, 4, 4, 2)
 FIRST_STARTS = (0, 0, 1, 3, 6)
-SECOND_STARTS = (0, 1, 3, 5, 7)
-ORDER_USED = (2, 3)
+SECOND_STARTS = (0, 1, 3, 5, 8)
 LATE_ROWS = 32
+ORDER_ROWS = 8
 TILE = 256
 
 
@@ -160,8 +160,7 @@
             at += term.shape[0]
 
 
-def level_kernel(turn, w, keep_in, recv_in, *refs):
-    keep_ref, send_ref, _ = refs[-3:]
+def level_kernel(turn, w, keep_in, recv_in, keep_ref, send_ref, next_turn):
     for cols in tiles(send_ref.shape[2]):
         z = split(stacked(keep_in[:, :, cols], recv_in[:, :, cols]))
         put_halves(product(w, z), keep_ref, send_ref, cols)
@@ -170,6 +169,9 @@
 def ready_kernel(turn, w, keep_in, recv_in, *refs):
     own_ref, send_ref, _ = refs[-3:]
     early = send_ref.shape[1]
+    if len(refs) > 3:
+        early -= ORDER_ROWS
+        put_order(refs[0], send_ref, early)
     for cols in tiles(send_ref.shape[2]):
         z = split(stacked(keep_in[:, :, cols], recv_in[:, :, cols]))
         result = product(w, z)
@@ -179,13 +181,38 @@
         for part in range(2):
             rows = result[part * slots : (part + 1) * slots]
             own.append(jnp.concatenate([rows[:half], rows[half + early :]], axis=0))
-            send_ref[part, :, cols] = rows[half : half + early]
+            send_ref[part, :early, cols] = rows[half : half + early]
         put_terms(own, own_ref, cols)
 
 
-def terms_kernel(turn, part_ref, out_ref, next_turn):
+def order_places(boxes, width):
+    places = [(n // ORDER_ROWS, n % ORDER_ROWS, n * width) for n in range(-(-boxes // width))]
+    return [(part, row, slice(at, min(at + width, boxes))) for part, row, at in places]
+
+
+def put_order(perm_ref, send_ref, early):
+    boxes, width = perm_ref.shape[1], send_ref.shape[2]
+    blank = jnp.zeros((1, width), F32)
+    rows = [[blank] * ORDER_ROWS for _ in range(2)]
+    for part, row, where in order_places(boxes, width):
+        here = perm_ref[:, where].astype(F32)
+        if here.shape[1] < width:
+            here = jnp.concatenate([here, blank[:, here.shape[1] :]], axis=1)
+        rows[part][row] = here
+    for part in range(2):
+        send_ref[part, early:] = jnp.concatenate(rows[part], axis=0)
+
+
+def terms_kernel(turn, part_ref, out_ref, *rest):
+    early = out_ref.shape[0] // 4
     for cols in tiles(part_ref.shape[2]):
-        put_terms([part_ref[0, :, cols], part_ref[1, :, cols]], out_ref, cols)
+        put_terms([part_ref[part, :early, cols] for part in range(2)], out_ref, cols)
+    if len(rest) > 1:
+        perm_ref = rest[0]
+        for part, row, where in order_places(perm_ref.shape[1], part_ref.shape[2]):
+            width = where.stop - where.start
+            here = part_ref[part, early + row : early + row + 1, :width]
+            perm_ref[:, where] = here.astype(jnp.int32)
 
 
 def picked(perm, parts, width):
@@ -219,13 +246,17 @@
             send_ref[part, :, cols] = high[at : at + late] + low[at : at + late]
 
 
-def switch_kernel(start, turn, w, other_perm, keep_in, late_in, *refs):
-    *early, keep_ref, send_ref, _ = refs
+def pick_early_kernel(start, turn, other_perm, *refs):
+    *early, out_ref, _ = refs
+    for cols in tiles(out_ref.shape[1]):
+        where = slice(start + cols.start, start + cols.stop)
+        out_ref[:, cols] = picked(other_perm[:, where], early, cols.stop - cols.start).astype(BF)
+
+
+def switch_kernel(turn, w, keep_in, early_in, late_in, keep_ref, send_ref, next_turn):
     half, late = keep_ref.shape[1], late_in.shape[1]
     rest = half - late
     for cols in tiles(send_ref.shape[2]):
-        where = slice(start + cols.start, start + cols.stop)
-        recv = picked(other_perm[:, where], early, cols.stop - cols.start).astype(BF)
         late_terms = [split(late_in[part, :, cols]) for part in range(2)]
         z = []
         for term in range(2):
@@ -233,26 +264,28 @@
             for part in range(2):
                 at = 2 * term + part
                 rows.append(keep_in[at * half : (at + 1) * half, cols])
-                rows.append(recv[at * rest : (at + 1) * rest])
+                rows.append(early_in[at * rest : (at + 1) * rest, cols])
                 rows.append(late_terms[part][term])
             z.append(jnp.concatenate(rows, axis=0))
         put_halves(product(w, z), keep_ref, send_ref, cols)
 
 
-def last_kernel(turn, w, c, measured_ref, keep_in, recv_in, *rest):
-    out_ref = rest[-2]
-    for cols in tiles(out_ref.shape[3]):
+def last_kernel(at, turn, w, c, measured_ref, keep_in, recv_in, *rest):
+    out_ref, _, tile_ref, left = rest[-4:]
+    copies = []
+    for n, cols in enumerate(tiles(keep_in.shape[2])):
         z = split(stacked(keep_in[:, :, cols], recv_in[:, :, cols]))
         image = product(c, split(product(w, z)))
         half = image.shape[0] // 2
         re, im = image[:half], image[half:]
         scale = measured_ref[0, :, cols] * lax.rsqrt(jnp.maximum(re * re + im * im, 0.25))
-        out_ref[0, 0, :, cols] = re * scale
-        out_ref[0, 1, :, cols] = im * scale
-
-
-def elements(*sizes):
-    return tuple(pl.Element(size) for size in sizes)
+        tile_ref[0, :, cols] = re * scale
+        tile_ref[1, :, cols] = im * scale
+        target = out_ref.at[0, :, :, pl.ds(at + cols.start, cols.stop - cols.start)]
+        copies.append(pltpu.make_async_copy(tile_ref.at[:, :, cols], target, left.at[n]))
+        copies[-1].start()
+    for copy in copies:
+        copy.wait()
 
 
 def whole():
@@ -337,16 +370,18 @@
     def block_of(rows, width):
         return jax.ShapeDtypeStruct((2, rows, width), F32)
 
-    def level(w, keep, recv, ready=False, also=()):
-        width = recv.shape[2]
-        shapes = halves(width)
-        if ready:
-            shapes = [terms_of(half + late, width), block_of(half - late, width)]
-        ins = [whole()] * 3 + [anywhere()] * len(also)
-        return call(ready_kernel if ready else level_kernel, ins, [w, keep, recv, *also], shapes)
-
-    def terms(block):
-        return call(terms_kernel, [whole()], [block], [terms_of(*block.shape[1:])])[0]
+    def level(w, keep, recv):
+        return call(level_kernel, [whole()] * 3, [w, keep, recv], halves(recv.shape[2]))
+
+    def ready(w, keep, recv, order):
+        width, early = recv.shape[2], half - late + ORDER_ROWS * len(order)
+        shapes = [terms_of(half + late, width), block_of(early, width)]
+        args = [w, keep, recv, *order]
+        return call(ready_kernel, [whole()] * len(args), args, shapes)
+
+    def terms(block, order):
+        shapes = [terms_of(half - late, block.shape[2])]
+        return call(terms_kernel, [whole()], [block], shapes + order)
 
     def pick_own(part, own_perm, parts):
         at, width = part
@@ -354,11 +389,13 @@
         shapes = [terms_of(half, width), block_of(late, width)]
         return call(kernel, [whole()] * (1 + len(parts)), [own_perm, *parts], shapes)
 
-    def switch(part, w, other_perm, keep, late_rows, early):
+    def pick_early(part, order, parts):
         at, width = part
-        kernel = functools.partial(switch_kernel, at)
-        args = [w, other_perm, keep, late_rows, *early]
-        return call(kernel, [whole()] * len(args), args, halves(width))
+        kernel = functools.partial(pick_early_kernel, at)
+        return call(kernel, [whole()] * (1 + len(parts)), [order, *parts], [terms_of(half - late, width)])[0]
+
+    def switch(w, keep, early, late_rows):
+        return call(switch_kernel, [whole()] * 4, [w, keep, early, late_rows], halves(late_rows.shape[2]))
 
     def last(part, w, c, keep, recv, so_far):
         at, width = part
@@ -366,14 +403,14 @@
         args = [w, c, lax.slice_in_dim(measured, at, at + width, axis=2), keep, recv]
         aliases = {}
         if so_far is not None:
-            ins.append(anywhere())
+            ins.append(pl.BlockSpec(memory_space=pltpu.HBM))
             aliases = {len(args) + 1: 0}
             args.append(so_far)
         return call(
-            last_kernel, ins, args,
+            functools.partial(last_kernel, at), ins, args,
             [jax.ShapeDtypeStruct((1, 2, cells, boxes), F32)],
-            outs=[pl.BlockSpec(elements(1, 2, cells, width), lambda i: (0, 0, 0, at))],
-            grid=(1,), input_output_aliases=aliases,
+            outs=[pl.BlockSpec(memory_space=pltpu.HBM)], input_output_aliases=aliases,
+            scratch_shapes=[pltpu.VMEM((2, cells, width), F32), pltpu.SemaphoreType.DMA((len(tiles(width)),))],
         )[0]
 
     own, away = {}, {}
@@ -385,7 +422,7 @@
     leaves = first_leaf + leaf(first[1:], True)
     name = "weights"
     own_perm, closing_terms, factor_terms = prepared()
-    other_perm = swapped(own_perm, levels[switch_at], "send_order")
+    other_perm, arrived, early = [], [], {}
 
     def first_begin(part):
         leave(part, 0, *leaves[part])
@@ -393,12 +430,20 @@
     def first_step(part, step):
         nonlocal name
         name = f"part_{part}_{step}"
+        w = factor_terms[step - 1]
         if step > switch_at:
-            away[part] = terms(away[part])
+            order = [jax.ShapeDtypeStruct(box_perm.shape, box_perm.dtype)] if part == 0 else []
+            away[part], *other = terms(away[part], order)
+            other_perm.extend(other)
+            arrived.append(part)
+            if len(arrived) == len(first):
+                for waiting in sorted(own2):
+                    gather(waiting)
+        elif step == switch_at:
+            order = [own_perm] if part == 0 else []
+            leave(part, step, *ready(w, own[part], away[part], order))
         else:
-            w = factor_terms[step - 1]
-            also = [other_perm] if (part, step) == ORDER_USED else []
-            leave(part, step, *level(w, own[part], away[part], step == switch_at, also))
+            leave(part, step, *level(w, own[part], away[part]))
 
     def second_begin(part):
         nonlocal name
@@ -406,6 +451,14 @@
         kept = [own[n] for n in range(len(first))]
         keep, send = pick_own(second[part], own_perm, kept)
         own2[part], away2[part] = keep, swapped(send, levels[switch_at], f"send_{part}_late")
+        if len(arrived) == len(first):
+            gather(part)
+
+    def gather(part):
+        nonlocal name
+        name = f"early_{part}"
+        parts = [away[n] for n in range(len(first))]
+        early[part] = pick_early(second[part], *other_perm, parts)
 
     def second_step(part, step):
         nonlocal name, out
@@ -416,8 +469,7 @@
             out = last(second[part], w, closing_terms, own2[part], away2[part], out)
             return
         if step == switch_at:
-            early = [away[n] for n in range(len(first))]
-            keep, send = switch(second[part], w, other_perm, own2[part], away2[part], early)
+            keep, send = switch(w, own2[part], early[part], away2[part])
         else:
             keep, send = level(w, own2[part], away2[part])
         own2[part], away2[part] = keep, swapped(send, levels[step + 1], f"send_{part}_{step + 1}")

time: 146 us -> 143 us (0.979)
  waiting for transfers between devices: 62.3 us -> 54.4 us
  starting transfers between devices: 47 us -> 54.1 us
  Pallas kernels: 35.1 us -> 33 us
    ppermute x46 -> x45, waiting for transfers between devices: 62.3 us -> 54.4 us  [swapped(): return lax.ppermute(block, axis, [(i, i ^ 1 << bit) for i in range(count)])]
    ppermute x46 -> x45, starting transfers between devices: 47 us -> 54.1 us  [swapped(): return lax.ppermute(block, axis, [(i, i ^ 1 << bit) for i in range(count)])]
    pallas_call x51 -> x56, Pallas kernels: 30.9 us -> 28.8 us  [call(): pl.pallas_call(kernel, in_specs=[anywhere(), *ins], out_specs=[*more.pop(...]
  transfers between devices with their start and end apart: 46 -> 45, of which waited for: 24 -> 22; matrix products, arithmetic and copies ran while one was open for 0% -> 0% of each run, Pallas kernels for 22% -> 20%
where the time goes in v3:
time: 143 us
  waiting for transfers between devices  54.4 us (38%)
  starting transfers between devices  54.1 us (38%)
  Pallas kernels  33 us (23%)
    ppermute x45, waiting for transfers between devices, swapped(): return lax.ppermute(block, axis, [(i, i ^ 1 << bit) for i in range(count)])  54.4 us
    ppermute x45, starting transfers between devices, swapped(): return lax.ppermute(block, axis, [(i, i ^ 1 << bit) for i in range(count)])  54.1 us
    pallas_call x56, Pallas kernels, call(): pl.pallas_call(kernel, in_specs=[anywhere(), *ins], out_specs=[*more.pop(...  28.8 us
    pallas_call x2, Pallas kernels, leaf(): pl.pallas_call(kernel, in_specs=ins, out_specs=[*[whole()] * (2 * len(par...  4.2 us
  transfers between devices with their start and end apart: 45, of which 22 were waited for; matrix products, arithmetic and copies ran while one was open for 0% of the time, Pallas kernels for 20%

profile of v3, /device:TPU:0, one launch (start us, length us, event | category | flops | bytes accessed | tf_op | source)
XLA Modules:
  0.0 143.1 jit_solution(10911600779401391768)
XLA Ops:
  0.0 2.3 %leaf.2 = (f32[2,64,384]{2,1,0:T(8,128)}, f32[2,64,384]{2,1,0:T(8,128)}, f32[8,128]{1,0:T(8,128)}) custom-call(f32[1,2,128,2048]{3,2,1,0:T(8,128)} %refs_0_.1, f32[1,2,128,128]{3,2,1,0:T(8,128)} %refs_1_.1), custom_call_target="tpu_custom_call" | custom-call | flops 1000000000 | bytes 2500000 | tf_op jit(solution)/shard_map/leaf/pallas_call | solution.py:340
  2.4 3.0 %collective-permute-start = (f32[2,64,384]{2,1,0:T(8,128)}, f32[2,64,384]{2,1,0:T(8,128)S(1)}, u32[]{:S(2)}, u32[]{:S(2)}) collective-permute-start(f32[2,64,384]{2,1,0:T(8,128)} %get-tuple-element.183), channel_id=1, source_target_pairs={{0,16},{8,24},{16,0},{24,8},{1,17},{9,25},{17,1},{25,9},{2,18},{10... | collective-permute-start | bytes 589832 | tf_op jit(solution)/shard_map/send_0_0/ppermute | solution.py:33
  11.5 2.4 %collective-permute-start.3 = (f32[2,64,512]{2,1,0:T(8,128)S(1)}, f32[2,64,512]{2,1,0:T(8,128)S(1)}, u32[]{:S(2)}, u32[]{:S(2)}) collective-permute-start(f32[2,64,512]{2,1,0:T(8,128)S(1)} %get-tuple-element.193), channel_id=1, source_target_pairs={{0,16},{8,24},{16,0},{24,8},{1,17},{9,25},{17,1},{25,9},{2,18},{10... | collective-permute-start | bytes 786440 | tf_op jit(solution)/shard_map/send_2_0/ppermute | solution.py:33
  14.0 1.9 %collective-permute-start.10 = (f32[2,64,256]{2,1,0:T(8,128)S(1)}, f32[2,64,256]{2,1,0:T(8,128)S(1)}, u32[]{:S(2)}, u32[]{:S(2)}) collective-permute-start(f32[2,64,256]{2,1,0:T(8,128)S(1)} %get-tuple-element.217), channel_id=1, source_target_pairs={{0,16},{8,24},{16,0},{24,8},{1,17},{9,25},{17,1},{25,9},{2,18},{10... | collective-permute-start | bytes 393224 | tf_op jit(solution)/shard_map/send_4_0/ppermute | solution.py:33
  18.4 2.7 %collective-permute-done.3.recv_in = f32[2,64,512]{2,1,0:T(8,128)S(1)} collective-permute-done((f32[2,64,512]{2,1,0:T(8,128)S(1)}, f32[2,64,512]{2,1,0:T(8,128)S(1)}, u32[]{:S(2)}, u32[]{:S(2)}) %collective-permute-start.3) | collective-permute-done | bytes 262176 | tf_op jit(solution)/shard_map/send_2_0/ppermute | solution.py:33
  31.7 2.7 %collective-permute-start.14 = (f32[2,40,384]{2,1,0:T(8,128)S(1)}, f32[2,40,384]{2,1,0:T(8,128)S(1)}, u32[]{:S(2)}, u32[]{:S(2)}) collective-permute-start(f32[2,40,384]{2,1,0:T(8,128)S(1)} %get-tuple-element.228), channel_id=1, source_target_pairs={{0,4},{1,5},{2,6},{3,7},{4,0},{5,1},{6,2},{7,3},{8,12},{9,13},{10,... | collective-permute-start | bytes 368648 | tf_op jit(solution)/shard_map/send_0_4/ppermute | solution.py:33
  39.6 2.2 %collective-permute-start.18 = (f32[2,32,384]{2,1,0:T(8,128)S(1)}, f32[2,32,384]{2,1,0:T(8,128)S(1)}, u32[]{:S(2)}, u32[]{:S(2)}) collective-permute-start(f32[2,32,384]{2,1,0:T(8,128)S(1)} %get-tuple-element.239), channel_id=1, source_target_pairs={{0,4},{1,5},{2,6},{3,7},{4,0},{5,1},{6,2},{7,3},{8,12},{9,13},{10,... | collective-permute-start | bytes 294920 | tf_op jit(solution)/shard_map/send_1_4/ppermute | solution.py:33
  45.7 2.7 %collective-permute-done.17.recv_in = f32[2,64,512]{2,1,0:T(8,128)S(1)} collective-permute-done((f32[2,64,512]{2,1,0:T(8,128)S(1)}, f32[2,64,512]{2,1,0:T(8,128)S(1)}, u32[]{:S(2)}, u32[]{:S(2)}) %collective-permute-start.17) | collective-permute-done | bytes 262176 | tf_op jit(solution)/shard_map/send_2_3/ppermute | solution.py:33
  51.0 2.6 %collective-permute-start.22 = (f32[2,64,256]{2,1,0:T(8,128)S(1)}, f32[2,64,256]{2,1,0:T(8,128)S(1)}, u32[]{:S(2)}, u32[]{:S(2)}) collective-permute-start(f32[2,64,256]{2,1,0:T(8,128)S(1)} %get-tuple-element.250), channel_id=1, source_target_pairs={{0,2},{1,3},{2,0},{3,1},{4,6},{5,7},{6,4},{7,5},{8,10},{9,11},{10,... | collective-permute-start | bytes 393224 | tf_op jit(solution)/shard_map/send_4_3/ppermute | solution.py:33
  53.6 3.3 %collective-permute-done.20.recv_in = f32[2,64,512]{2,1,0:T(8,128)S(1)} collective-permute-done((f32[2,64,512]{2,1,0:T(8,128)S(1)}, f32[2,64,512]{2,1,0:T(8,128)S(1)}, u32[]{:S(2)}, u32[]{:S(2)}) %collective-permute-start.20) | collective-permute-done | bytes 262176 | tf_op jit(solution)/shard_map/send_3_3/ppermute | solution.py:33
  59.4 3.2 %collective-permute-start.24 = (f32[2,32,256]{2,1,0:T(8,128)S(1)}, f32[2,32,256]{2,1,0:T(8,128)S(1)}, u32[]{:S(2)}, u32[]{:S(2)}) collective-permute-start(f32[2,32,256]{2,1,0:T(8,128)S(1)} %get-tuple-element.261), channel_id=1, source_target_pairs={{0,4},{1,5},{2,6},{3,7},{4,0},{5,1},{6,2},{7,3},{8,12},{9,13},{10,... | collective-permute-start | bytes 196616 | tf_op jit(solution)/shard_map/send_4_4/ppermute | solution.py:33
  63.7 5.6 %collective-permute-done.23.part_ref = f32[2,32,512]{2,1,0:T(8,128)S(1)} collective-permute-done((f32[2,32,512]{2,1,0:T(8,128)S(1)}, f32[2,32,512]{2,1,0:T(8,128)S(1)}, u32[]{:S(2)}, u32[]{:S(2)}) %collective-permute-start.23) | collective-permute-done | bytes 131104 | tf_op jit(solution)/shard_map/send_3_4/ppermute | solution.py:33
  84.4 2.3 %collective-permute-start.31 = (f32[2,32,512]{2,1,0:T(8,128)S(1)}, f32[2,32,512]{2,1,0:T(8,128)S(1)}, u32[]{:S(2)}, u32[]{:S(2)}) collective-permute-start(f32[2,32,512]{2,1,0:T(8,128)S(1)} %get-tuple-element.303), channel_id=1, source_target_pairs={{0,4},{1,5},{2,6},{3,7},{4,0},{5,1},{6,2},{7,3},{8,12},{9,13},{10,... | collective-permute-start | bytes 393224 | tf_op jit(solution)/shard_map/send_3_late/ppermute | solution.py:33
  89.9 2.1 %collective-permute-done.30.recv_in = f32[2,64,384]{2,1,0:T(8,128)S(1)} collective-permute-done((f32[2,64,384]{2,1,0:T(8,128)S(1)}, f32[2,64,384]{2,1,0:T(8,128)S(1)}, u32[]{:S(2)}, u32[]{:S(2)}) %collective-permute-start.30) | collective-permute-done | bytes 196640 | tf_op jit(solution)/shard_map/send_0_6/ppermute | solution.py:33
  93.7 2.6 %collective-permute-start.35 = (f32[2,32,256]{2,1,0:T(8,128)S(1)}, f32[2,32,256]{2,1,0:T(8,128)S(1)}, u32[]{:S(2)}, u32[]{:S(2)}) collective-permute-start(f32[2,32,256]{2,1,0:T(8,128)S(1)} %get-tuple-element.318), channel_id=1, source_target_pairs={{0,4},{1,5},{2,6},{3,7},{4,0},{5,1},{6,2},{7,3},{8,12},{9,13},{10,... | collective-permute-start | bytes 196616 | tf_op jit(solution)/shard_map/send_4_late/ppermute | solution.py:33
  96.7 2.3 %collective-permute-start.36 = (f32[2,64,512]{2,1,0:T(8,128)S(1)}, f32[2,64,512]{2,1,0:T(8,128)S(1)}, u32[]{:S(2)}, u32[]{:S(2)}) collective-permute-start(f32[2,64,512]{2,1,0:T(8,128)S(1)} %get-tuple-element.321), channel_id=1, source_target_pairs={{0,1},{1,0},{2,3},{3,2},{4,5},{5,4},{6,7},{7,6},{8,9},{9,8},{10,11... | collective-permute-start | bytes 786440 | tf_op jit(solution)/shard_map/send_3_5/ppermute | solution.py:33
  99.8 2.0 %collective-permute-start.38 = (f32[2,64,384]{2,1,0:T(8,128)S(1)}, f32[2,64,384]{2,1,0:T(8,128)S(1)}, u32[]{:S(2)}, u32[]{:S(2)}) collective-permute-start(f32[2,64,384]{2,1,0:T(8,128)S(1)} %get-tuple-element.327), channel_id=1, source_target_pairs={{0,4},{1,5},{2,6},{3,7},{4,0},{5,1},{6,2},{7,3},{8,12},{9,13},{10,... | collective-permute-start | bytes 589832 | tf_op jit(solution)/shard_map/send_1_7/ppermute | solution.py:33
  101.8 5.4 %collective-permute-done.34.recv_in = f32[2,64,384]{2,1,0:T(8,128)S(1)} collective-permute-done((f32[2,64,384]{2,1,0:T(8,128)S(1)}, f32[2,64,384]{2,1,0:T(8,128)S(1)}, u32[]{:S(2)}, u32[]{:S(2)}) %collective-permute-start.34) | collective-permute-done | bytes 196640 | tf_op jit(solution)/shard_map/send_0_7/ppermute | solution.py:33
  110.2 2.7 %collective-permute-done.37.recv_in = f32[2,64,512]{2,1,0:T(8,128)S(1)} collective-permute-done((f32[2,64,512]{2,1,0:T(8,128)S(1)}, f32[2,64,512]{2,1,0:T(8,128)S(1)}, u32[]{:S(2)}, u32[]{:S(2)}) %collective-permute-start.37) | collective-permute-done | bytes 262176 | tf_op jit(solution)/shard_map/send_2_6/ppermute | solution.py:33
  114.0 2.9 %collective-permute-done.38.recv_in = f32[2,64,384]{2,1,0:T(8,128)S(1)} collective-permute-done((f32[2,64,384]{2,1,0:T(8,128)S(1)}, f32[2,64,384]{2,1,0:T(8,128)S(1)}, u32[]{:S(2)}, u32[]{:S(2)}) %collective-permute-start.38) | collective-permute-done | bytes 196640 | tf_op jit(solution)/shard_map/send_1_7/ppermute | solution.py:33
  119.0 2.9 %collective-permute-done.40.recv_in = f32[2,64,512]{2,1,0:T(8,128)S(1)} collective-permute-done((f32[2,64,512]{2,1,0:T(8,128)S(1)}, f32[2,64,512]{2,1,0:T(8,128)S(1)}, u32[]{:S(2)}, u32[]{:S(2)}) %collective-permute-start.40) | collective-permute-done | bytes 262176 | tf_op jit(solution)/shard_map/send_3_6/ppermute | solution.py:33
  122.5 9.8 %collective-permute-done.41.recv_in = f32[2,64,512]{2,1,0:T(8,128)S(1)} collective-permute-done((f32[2,64,512]{2,1,0:T(8,128)S(1)}, f32[2,64,512]{2,1,0:T(8,128)S(1)}, u32[]{:S(2)}, u32[]{:S(2)}) %collective-permute-start.41) | collective-permute-done | bytes 262176 | tf_op jit(solution)/shard_map/send_2_7/ppermute | solution.py:33
  134.3 3.3 %collective-permute-done.43.recv_in = f32[2,64,512]{2,1,0:T(8,128)S(1)} collective-permute-done((f32[2,64,512]{2,1,0:T(8,128)S(1)}, f32[2,64,512]{2,1,0:T(8,128)S(1)}, u32[]{:S(2)}, u32[]{:S(2)}) %collective-permute-start.43) | collective-permute-done | bytes 262176 | tf_op jit(solution)/shard_map/send_3_7/ppermute | solution.py:33
  139.2 2.3 %collective-permute-done.44.recv_in = f32[2,64,256]{2,1,0:T(8,128)S(1)} collective-permute-done((f32[2,64,256]{2,1,0:T(8,128)S(1)}, f32[2,64,256]{2,1,0:T(8,128)S(1)}, u32[]{:S(2)}, u32[]{:S(2)}) %collective-permute-start.44) | collective-permute-done | bytes 131104 | tf_op jit(solution)/shard_map/send_4_7/ppermute | solution.py:33
  (145 shorter events, 67.1 us)
Async XLA Ops:
  11.5 9.6 %collective-permute-start.3 = (f32[2,64,512]{2,1,0:T(8,128)S(1)}, f32[2,64,512]{2,1,0:T(8,128)S(1)}, u32[]{:S(2)}, u32[]{:S(2)}) collective-permute-start(f32[2,64,512]{2,1,0:T(8,128)S(1)} %get-tuple-element.193), channel_id=1, source_target_pairs={{0,16},{8,24},{16,0},{24,8},{1,17},{9,25},{17,1},{25,9},{2,18},{10... | collective-permute-start | bytes 786440 | tf_op jit(solution)/shard_map/send_2_0/ppermute | solution.py:33
  13.9 12.8 %collective-permute-start.6 = (f32[2,64,512]{2,1,0:T(8,128)S(1)}, f32[2,64,512]{2,1,0:T(8,128)S(1)}, u32[]{:S(2)}, u32[]{:S(2)}) collective-permute-start(f32[2,64,512]{2,1,0:T(8,128)S(1)} %get-tuple-element.203), channel_id=1, source_target_pairs={{0,16},{8,24},{16,0},{24,8},{1,17},{9,25},{17,1},{25,9},{2,18},{10... | collective-permute-start | bytes 786440 | tf_op jit(solution)/shard_map/send_3_0/ppermute | solution.py:33
  14.0 20.3 %collective-permute-start.10 = (f32[2,64,256]{2,1,0:T(8,128)S(1)}, f32[2,64,256]{2,1,0:T(8,128)S(1)}, u32[]{:S(2)}, u32[]{:S(2)}) collective-permute-start(f32[2,64,256]{2,1,0:T(8,128)S(1)} %get-tuple-element.217), channel_id=1, source_target_pairs={{0,16},{8,24},{16,0},{24,8},{1,17},{9,25},{17,1},{25,9},{2,18},{10... | collective-permute-start | bytes 393224 | tf_op jit(solution)/shard_map/send_4_0/ppermute | solution.py:33
  29.7 9.6 %collective-permute-start.13 = (f32[2,64,384]{2,1,0:T(8,128)S(1)}, f32[2,64,384]{2,1,0:T(8,128)S(1)}, u32[]{:S(2)}, u32[]{:S(2)}) collective-permute-start(f32[2,64,384]{2,1,0:T(8,128)S(1)} %get-tuple-element.226), channel_id=1, source_target_pairs={{0,2},{1,3},{2,0},{3,1},{4,6},{5,7},{6,4},{7,5},{8,10},{9,11},{10,... | collective-permute-start | bytes 589832 | tf_op jit(solution)/shard_map/send_1_3/ppermute | solution.py:33
  31.7 10.1 %collective-permute-start.14 = (f32[2,40,384]{2,1,0:T(8,128)S(1)}, f32[2,40,384]{2,1,0:T(8,128)S(1)}, u32[]{:S(2)}, u32[]{:S(2)}) collective-permute-start(f32[2,40,384]{2,1,0:T(8,128)S(1)} %get-tuple-element.228), channel_id=1, source_target_pairs={{0,4},{1,5},{2,6},{3,7},{4,0},{5,1},{6,2},{7,3},{8,12},{9,13},{10,... | collective-permute-start | bytes 368648 | tf_op jit(solution)/shard_map/send_0_4/ppermute | solution.py:33
  37.1 11.3 %collective-permute-start.17 = (f32[2,64,512]{2,1,0:T(8,128)S(1)}, f32[2,64,512]{2,1,0:T(8,128)S(1)}, u32[]{:S(2)}, u32[]{:S(2)}) collective-permute-start(f32[2,64,512]{2,1,0:T(8,128)S(1)} %get-tuple-element.237), channel_id=1, source_target_pairs={{0,2},{1,3},{2,0},{3,1},{4,6},{5,7},{6,4},{7,5},{8,10},{9,11},{10,... | collective-permute-start | bytes 786440 | tf_op jit(solution)/shard_map/send_2_3/ppermute | solution.py:33
  39.6 11.1 %collective-permute-start.18 = (f32[2,32,384]{2,1,0:T(8,128)S(1)}, f32[2,32,384]{2,1,0:T(8,128)S(1)}, u32[]{:S(2)}, u32[]{:S(2)}) collective-permute-start(f32[2,32,384]{2,1,0:T(8,128)S(1)} %get-tuple-element.239), channel_id=1, source_target_pairs={{0,4},{1,5},{2,6},{3,7},{4,0},{5,1},{6,2},{7,3},{8,12},{9,13},{10,... | collective-permute-start | bytes 294920 | tf_op jit(solution)/shard_map/send_1_4/ppermute | solution.py:33
  44.5 12.3 %collective-permute-start.20 = (f32[2,64,512]{2,1,0:T(8,128)S(1)}, f32[2,64,512]{2,1,0:T(8,128)S(1)}, u32[]{:S(2)}, u32[]{:S(2)}) collective-permute-start(f32[2,64,512]{2,1,0:T(8,128)S(1)} %get-tuple-element.245), channel_id=1, source_target_pairs={{0,2},{1,3},{2,0},{3,1},{4,6},{5,7},{6,4},{7,5},{8,10},{9,11},{10,... | collective-permute-start | bytes 786440 | tf_op jit(solution)/shard_map/send_3_3/ppermute | solution.py:33
  57.2 12.1 %collective-permute-start.23 = (f32[2,32,512]{2,1,0:T(8,128)S(1)}, f32[2,32,512]{2,1,0:T(8,128)S(1)}, u32[]{:S(2)}, u32[]{:S(2)}) collective-permute-start(f32[2,32,512]{2,1,0:T(8,128)S(1)} %get-tuple-element.258), channel_id=1, source_target_pairs={{0,4},{1,5},{2,6},{3,7},{4,0},{5,1},{6,2},{7,3},{8,12},{9,13},{10,... | collective-permute-start | bytes 393224 | tf_op jit(solution)/shard_map/send_3_4/ppermute | solution.py:33
  59.4 12.4 %collective-permute-start.24 = (f32[2,32,256]{2,1,0:T(8,128)S(1)}, f32[2,32,256]{2,1,0:T(8,128)S(1)}, u32[]{:S(2)}, u32[]{:S(2)}) collective-permute-start(f32[2,32,256]{2,1,0:T(8,128)S(1)} %get-tuple-element.261), channel_id=1, source_target_pairs={{0,4},{1,5},{2,6},{3,7},{4,0},{5,1},{6,2},{7,3},{8,12},{9,13},{10,... | collective-permute-start | bytes 196616 | tf_op jit(solution)/shard_map/send_4_4/ppermute | solution.py:33
  63.6 10.1 %collective-permute-start.25 = (f32[2,32,384]{2,1,0:T(8,128)S(1)}, f32[2,32,384]{2,1,0:T(8,128)S(1)}, u32[]{:S(2)}, u32[]{:S(2)}) collective-permute-start(f32[2,32,384]{2,1,0:T(8,128)S(1)} %get-tuple-element.274), channel_id=1, source_target_pairs={{0,4},{1,5},{2,6},{3,7},{4,0},{5,1},{6,2},{7,3},{8,12},{9,13},{10,... | collective-permute-start | bytes 294920 | tf_op jit(solution)/shard_map/send_0_late/ppermute | solution.py:33
  76.1 10.7 %collective-permute-start.28 = (f32[2,32,512]{2,1,0:T(8,128)S(1)}, f32[2,32,512]{2,1,0:T(8,128)S(1)}, u32[]{:S(2)}, u32[]{:S(2)}) collective-permute-start(f32[2,32,512]{2,1,0:T(8,128)S(1)} %get-tuple-element.290), channel_id=1, source_target_pairs={{0,4},{1,5},{2,6},{3,7},{4,0},{5,1},{6,2},{7,3},{8,12},{9,13},{10,... | collective-permute-start | bytes 393224 | tf_op jit(solution)/shard_map/send_2_late/ppermute | solution.py:33
  84.4 11.9 %collective-permute-start.31 = (f32[2,32,512]{2,1,0:T(8,128)S(1)}, f32[2,32,512]{2,1,0:T(8,128)S(1)}, u32[]{:S(2)}, u32[]{:S(2)}) collective-permute-start(f32[2,32,512]{2,1,0:T(8,128)S(1)} %get-tuple-element.303), channel_id=1, source_target_pairs={{0,4},{1,5},{2,6},{3,7},{4,0},{5,1},{6,2},{7,3},{8,12},{9,13},{10,... | collective-permute-start | bytes 393224 | tf_op jit(solution)/shard_map/send_3_late/ppermute | solution.py:33
  87.1 11.8 %collective-permute-start.32 = (f32[2,64,512]{2,1,0:T(8,128)S(1)}, f32[2,64,512]{2,1,0:T(8,128)S(1)}, u32[]{:S(2)}, u32[]{:S(2)}) collective-permute-start(f32[2,64,512]{2,1,0:T(8,128)S(1)} %get-tuple-element.306), channel_id=1, source_target_pairs={{0,1},{1,0},{2,3},{3,2},{4,5},{5,4},{6,7},{7,6},{8,9},{9,8},{10,11... | collective-permute-start | bytes 786440 | tf_op jit(solution)/shard_map/send_2_5/ppermute | solution.py:33
  88.1 11.3 %collective-permute-start.33 = (f32[2,64,384]{2,1,0:T(8,128)S(1)}, f32[2,64,384]{2,1,0:T(8,128)S(1)}, u32[]{:S(2)}, u32[]{:S(2)}) collective-permute-start(f32[2,64,384]{2,1,0:T(8,128)S(1)} %get-tuple-element.309), channel_id=1, source_target_pairs={{0,2},{1,3},{2,0},{3,1},{4,6},{5,7},{6,4},{7,5},{8,10},{9,11},{10,... | collective-permute-start | bytes 589832 | tf_op jit(solution)/shard_map/send_1_6/ppermute | solution.py:33
  93.3 13.8 %collective-permute-start.34 = (f32[2,64,384]{2,1,0:T(8,128)S(1)}, f32[2,64,384]{2,1,0:T(8,128)S(1)}, u32[]{:S(2)}, u32[]{:S(2)}) collective-permute-start(f32[2,64,384]{2,1,0:T(8,128)S(1)} %get-tuple-element.314), channel_id=1, source_target_pairs={{0,4},{1,5},{2,6},{3,7},{4,0},{5,1},{6,2},{7,3},{8,12},{9,13},{10,... | collective-permute-start | bytes 589832 | tf_op jit(solution)/shard_map/send_0_7/ppermute | solution.py:33
  93.7 15.2 %collective-permute-start.35 = (f32[2,32,256]{2,1,0:T(8,128)S(1)}, f32[2,32,256]{2,1,0:T(8,128)S(1)}, u32[]{:S(2)}, u32[]{:S(2)}) collective-permute-start(f32[2,32,256]{2,1,0:T(8,128)S(1)} %get-tuple-element.318), channel_id=1, source_target_pairs={{0,4},{1,5},{2,6},{3,7},{4,0},{5,1},{6,2},{7,3},{8,12},{9,13},{10,... | collective-permute-start | bytes 196616 | tf_op jit(solution)/shard_map/send_4_late/ppermute | solution.py:33
  96.7 13.1 %collective-permute-start.36 = (f32[2,64,512]{2,1,0:T(8,128)S(1)}, f32[2,64,512]{2,1,0:T(8,128)S(1)}, u32[]{:S(2)}, u32[]{:S(2)}) collective-permute-start(f32[2,64,512]{2,1,0:T(8,128)S(1)} %get-tuple-element.321), channel_id=1, source_target_pairs={{0,1},{1,0},{2,3},{3,2},{4,5},{5,4},{6,7},{7,6},{8,9},{9,8},{10,11... | collective-permute-start | bytes 786440 | tf_op jit(solution)/shard_map/send_3_5/ppermute | solution.py:33
  99.3 13.6 %collective-permute-start.37 = (f32[2,64,512]{2,1,0:T(8,128)S(1)}, f32[2,64,512]{2,1,0:T(8,128)S(1)}, u32[]{:S(2)}, u32[]{:S(2)}) collective-permute-start(f32[2,64,512]{2,1,0:T(8,128)S(1)} %get-tuple-element.324), channel_id=1, source_target_pairs={{0,2},{1,3},{2,0},{3,1},{4,6},{5,7},{6,4},{7,5},{8,10},{9,11},{10,... | collective-permute-start | bytes 786440 | tf_op jit(solution)/shard_map/send_2_6/ppermute | solution.py:33
  99.8 17.1 %collective-permute-start.38 = (f32[2,64,384]{2,1,0:T(8,128)S(1)}, f32[2,64,384]{2,1,0:T(8,128)S(1)}, u32[]{:S(2)}, u32[]{:S(2)}) collective-permute-start(f32[2,64,384]{2,1,0:T(8,128)S(1)} %get-tuple-element.327), channel_id=1, source_target_pairs={{0,4},{1,5},{2,6},{3,7},{4,0},{5,1},{6,2},{7,3},{8,12},{9,13},{10,... | collective-permute-start | bytes 589832 | tf_op jit(solution)/shard_map/send_1_7/ppermute | solution.py:33
  110.1 11.8 %collective-permute-start.40 = (f32[2,64,512]{2,1,0:T(8,128)S(1)}, f32[2,64,512]{2,1,0:T(8,128)S(1)}, u32[]{:S(2)}, u32[]{:S(2)}) collective-permute-start(f32[2,64,512]{2,1,0:T(8,128)S(1)} %get-tuple-element.334), channel_id=1, source_target_pairs={{0,2},{1,3},{2,0},{3,1},{4,6},{5,7},{6,4},{7,5},{8,10},{9,11},{10,... | collective-permute-start | bytes 786440 | tf_op jit(solution)/shard_map/send_3_6/ppermute | solution.py:33
  113.3 18.9 %collective-permute-start.41 = (f32[2,64,512]{2,1,0:T(8,128)S(1)}, f32[2,64,512]{2,1,0:T(8,128)S(1)}, u32[]{:S(2)}, u32[]{:S(2)}) collective-permute-start(f32[2,64,512]{2,1,0:T(8,128)S(1)} %get-tuple-element.337), channel_id=1, source_target_pairs={{0,4},{1,5},{2,6},{3,7},{4,0},{5,1},{6,2},{7,3},{8,12},{9,13},{10,... | collective-permute-start | bytes 786440 | tf_op jit(solution)/shard_map/send_2_7/ppermute | solution.py:33
  118.9 15.0 %collective-permute-start.42 = (f32[2,64,256]{2,1,0:T(8,128)S(1)}, f32[2,64,256]{2,1,0:T(8,128)S(1)}, u32[]{:S(2)}, u32[]{:S(2)}) collective-permute-start(f32[2,64,256]{2,1,0:T(8,128)S(1)} %get-tuple-element.341), channel_id=1, source_target_pairs={{0,2},{1,3},{2,0},{3,1},{4,6},{5,7},{6,4},{7,5},{8,10},{9,11},{10,... | collective-permute-start | bytes 393224 | tf_op jit(solution)/shard_map/send_4_6/ppermute | solution.py:33
  122.3 15.2 %collective-permute-start.43 = (f32[2,64,512]{2,1,0:T(8,128)S(1)}, f32[2,64,512]{2,1,0:T(8,128)S(1)}, u32[]{:S(2)}, u32[]{:S(2)}) collective-permute-start(f32[2,64,512]{2,1,0:T(8,128)S(1)} %get-tuple-element.344), channel_id=1, source_target_pairs={{0,4},{1,5},{2,6},{3,7},{4,0},{5,1},{6,2},{7,3},{8,12},{9,13},{10,... | collective-permute-start | bytes 786440 | tf_op jit(solution)/shard_map/send_3_7/ppermute | solution.py:33
  (30 other events, 202.9 us)

commit v4 on v3

--- a/solution.py
+++ b/solution.py
@@ -15,7 +15,7 @@
 SECOND_STARTS = (0, 1, 3, 5, 8)
 LATE_ROWS = 32
 ORDER_ROWS = 8
-TILE = 256
+TILE = 512
 
 
 def levels_of(level_count, dev_size):

time: 143 us -> 142 us (level); the launches traced: 143 us -> 140 us
  waiting for transfers between devices: 54.4 us -> 48.5 us
  starting transfers between devices: 54.1 us -> 57.4 us
    ppermute x45, waiting for transfers between devices: 54.4 us -> 48.5 us  [swapped(): return lax.ppermute(block, axis, [(i, i ^ 1 << bit) for i in range(count)])]
    ppermute x45, starting transfers between devices: 54.1 us -> 57.4 us  [swapped(): return lax.ppermute(block, axis, [(i, i ^ 1 << bit) for i in range(count)])]
  transfers between devices with their start and end apart: 45 -> 45, of which waited for: 22 -> 22; matrix products, arithmetic and copies ran while one was open for 0% -> 0% of each run, Pallas kernels for 20% -> 21%
where the time goes in v4:
time: 142 us; the launch traced here: 140 us
  starting transfers between devices  57.4 us (40%)
  waiting for transfers between devices  48.5 us (34%)
  Pallas kernels  32.4 us (23%)
    ppermute x45, starting transfers between devices, swapped(): return lax.ppermute(block, axis, [(i, i ^ 1 << bit) for i in range(count)])  57.4 us
    ppermute x45, waiting for transfers between devices, swapped(): return lax.ppermute(block, axis, [(i, i ^ 1 << bit) for i in range(count)])  48.5 us
    pallas_call x56, Pallas kernels, call(): pl.pallas_call(kernel, in_specs=[anywhere(), *ins], out_specs=[*more.pop(...  28.2 us
    pallas_call x2, Pallas kernels, leaf(): pl.pallas_call(kernel, in_specs=ins, out_specs=[*[whole()] * (2 * len(par...  4.21 us
  transfers between devices with their start and end apart: 45, of which 22 were waited for; matrix products, arithmetic and copies ran while one was open for 0% of the time, Pallas kernels for 21%

profile of v4, /device:TPU:0, one launch (start us, length us, event | category | flops | bytes accessed | tf_op | source)
XLA Modules:
  0.0 139.9 jit_solution(15216336248435095572)
XLA Ops:
  0.0 2.3 %leaf.2 = (f32[2,64,384]{2,1,0:T(8,128)}, f32[2,64,384]{2,1,0:T(8,128)}, f32[8,128]{1,0:T(8,128)}) custom-call(f32[1,2,128,2048]{3,2,1,0:T(8,128)} %refs_0_.1, f32[1,2,128,128]{3,2,1,0:T(8,128)} %refs_1_.1), custom_call_target="tpu_custom_call" | custom-call | flops 1000000000 | bytes 2500000 | tf_op jit(solution)/shard_map/leaf/pallas_call | solution.py:340
  2.4 3.0 %collective-permute-start = (f32[2,64,384]{2,1,0:T(8,128)}, f32[2,64,384]{2,1,0:T(8,128)S(1)}, u32[]{:S(2)}, u32[]{:S(2)}) collective-permute-start(f32[2,64,384]{2,1,0:T(8,128)} %get-tuple-element.183), channel_id=1, source_target_pairs={{0,16},{8,24},{16,0},{24,8},{1,17},{9,25},{17,1},{25,9},{2,18},{10... | collective-permute-start | bytes 589832 | tf_op jit(solution)/shard_map/send_0_0/ppermute | solution.py:33
  6.1 1.9 %leaf.3 = (f32[2,64,384]{2,1,0:T(8,128)S(1)}, f32[2,64,384]{2,1,0:T(8,128)S(1)}, f32[2,64,512]{2,1,0:T(8,128)S(1)}, f32[2,64,512]{2,1,0:T(8,128)S(1)}, f32[2,64,...) custom-call(f32[8,128]{1,0:T(8,128)S(1)} %copy-done.7, ...), custom_call_target="tpu_custom_call" | custom-call | flops 1000000000 | bytes 2500000 | tf_op jit(solution)/shard_map/leaf/pallas_call | solution.py:340
  11.5 2.4 %collective-permute-start.3 = (f32[2,64,512]{2,1,0:T(8,128)S(1)}, f32[2,64,512]{2,1,0:T(8,128)S(1)}, u32[]{:S(2)}, u32[]{:S(2)}) collective-permute-start(f32[2,64,512]{2,1,0:T(8,128)S(1)} %get-tuple-element.193), channel_id=1, source_target_pairs={{0,16},{8,24},{16,0},{24,8},{1,17},{9,25},{17,1},{25,9},{2,18},{10... | collective-permute-start | bytes 786440 | tf_op jit(solution)/shard_map/send_2_0/ppermute | solution.py:33
  14.0 1.9 %collective-permute-start.10 = (f32[2,64,256]{2,1,0:T(8,128)S(1)}, f32[2,64,256]{2,1,0:T(8,128)S(1)}, u32[]{:S(2)}, u32[]{:S(2)}) collective-permute-start(f32[2,64,256]{2,1,0:T(8,128)S(1)} %get-tuple-element.217), channel_id=1, source_target_pairs={{0,16},{8,24},{16,0},{24,8},{1,17},{9,25},{17,1},{25,9},{2,18},{10... | collective-permute-start | bytes 393224 | tf_op jit(solution)/shard_map/send_4_0/ppermute | solution.py:33
  18.4 2.7 %collective-permute-done.3.recv_in = f32[2,64,512]{2,1,0:T(8,128)S(1)} collective-permute-done((f32[2,64,512]{2,1,0:T(8,128)S(1)}, f32[2,64,512]{2,1,0:T(8,128)S(1)}, u32[]{:S(2)}, u32[]{:S(2)}) %collective-permute-start.3) | collective-permute-done | bytes 262176 | tf_op jit(solution)/shard_map/send_2_0/ppermute | solution.py:33
  31.7 2.7 %collective-permute-start.14 = (f32[2,40,384]{2,1,0:T(8,128)S(1)}, f32[2,40,384]{2,1,0:T(8,128)S(1)}, u32[]{:S(2)}, u32[]{:S(2)}) collective-permute-start(f32[2,40,384]{2,1,0:T(8,128)S(1)} %get-tuple-element.228), channel_id=1, source_target_pairs={{0,4},{1,5},{2,6},{3,7},{4,0},{5,1},{6,2},{7,3},{8,12},{9,13},{10,... | collective-permute-start | bytes 368648 | tf_op jit(solution)/shard_map/send_0_4/ppermute | solution.py:33
  39.6 2.2 %collective-permute-start.18 = (f32[2,32,384]{2,1,0:T(8,128)S(1)}, f32[2,32,384]{2,1,0:T(8,128)S(1)}, u32[]{:S(2)}, u32[]{:S(2)}) collective-permute-start(f32[2,32,384]{2,1,0:T(8,128)S(1)} %get-tuple-element.239), channel_id=1, source_target_pairs={{0,4},{1,5},{2,6},{3,7},{4,0},{5,1},{6,2},{7,3},{8,12},{9,13},{10,... | collective-permute-start | bytes 294920 | tf_op jit(solution)/shard_map/send_1_4/ppermute | solution.py:33
  45.7 2.7 %collective-permute-done.17.recv_in = f32[2,64,512]{2,1,0:T(8,128)S(1)} collective-permute-done((f32[2,64,512]{2,1,0:T(8,128)S(1)}, f32[2,64,512]{2,1,0:T(8,128)S(1)}, u32[]{:S(2)}, u32[]{:S(2)}) %collective-permute-start.17) | collective-permute-done | bytes 262176 | tf_op jit(solution)/shard_map/send_2_3/ppermute | solution.py:33
  51.0 2.6 %collective-permute-start.22 = (f32[2,64,256]{2,1,0:T(8,128)S(1)}, f32[2,64,256]{2,1,0:T(8,128)S(1)}, u32[]{:S(2)}, u32[]{:S(2)}) collective-permute-start(f32[2,64,256]{2,1,0:T(8,128)S(1)} %get-tuple-element.250), channel_id=1, source_target_pairs={{0,2},{1,3},{2,0},{3,1},{4,6},{5,7},{6,4},{7,5},{8,10},{9,11},{10,... | collective-permute-start | bytes 393224 | tf_op jit(solution)/shard_map/send_4_3/ppermute | solution.py:33
  53.6 3.3 %collective-permute-done.20.recv_in = f32[2,64,512]{2,1,0:T(8,128)S(1)} collective-permute-done((f32[2,64,512]{2,1,0:T(8,128)S(1)}, f32[2,64,512]{2,1,0:T(8,128)S(1)}, u32[]{:S(2)}, u32[]{:S(2)}) %collective-permute-start.20) | collective-permute-done | bytes 262176 | tf_op jit(solution)/shard_map/send_3_3/ppermute | solution.py:33
  59.4 3.2 %collective-permute-start.24 = (f32[2,32,256]{2,1,0:T(8,128)S(1)}, f32[2,32,256]{2,1,0:T(8,128)S(1)}, u32[]{:S(2)}, u32[]{:S(2)}) collective-permute-start(f32[2,32,256]{2,1,0:T(8,128)S(1)} %get-tuple-element.261), channel_id=1, source_target_pairs={{0,4},{1,5},{2,6},{3,7},{4,0},{5,1},{6,2},{7,3},{8,12},{9,13},{10,... | collective-permute-start | bytes 196616 | tf_op jit(solution)/shard_map/send_4_4/ppermute | solution.py:33
  63.7 5.6 %collective-permute-done.23.part_ref = f32[2,32,512]{2,1,0:T(8,128)S(1)} collective-permute-done((f32[2,32,512]{2,1,0:T(8,128)S(1)}, f32[2,32,512]{2,1,0:T(8,128)S(1)}, u32[]{:S(2)}, u32[]{:S(2)}) %collective-permute-start.23) | collective-permute-done | bytes 131104 | tf_op jit(solution)/shard_map/send_3_4/ppermute | solution.py:33
  78.2 1.9 %collective-permute-start.29 = (f32[2,64,384]{2,1,0:T(8,128)S(1)}, f32[2,64,384]{2,1,0:T(8,128)S(1)}, u32[]{:S(2)}, u32[]{:S(2)}) collective-permute-start(f32[2,64,384]{2,1,0:T(8,128)S(1)} %get-tuple-element.293), channel_id=1, source_target_pairs={{0,1},{1,0},{2,3},{3,2},{4,5},{5,4},{6,7},{7,6},{8,9},{9,8},{10,11... | collective-permute-start | bytes 589832 | tf_op jit(solution)/shard_map/send_1_5/ppermute | solution.py:33
  84.5 2.3 %collective-permute-start.31 = (f32[2,32,512]{2,1,0:T(8,128)S(1)}, f32[2,32,512]{2,1,0:T(8,128)S(1)}, u32[]{:S(2)}, u32[]{:S(2)}) collective-permute-start(f32[2,32,512]{2,1,0:T(8,128)S(1)} %get-tuple-element.303), channel_id=1, source_target_pairs={{0,4},{1,5},{2,6},{3,7},{4,0},{5,1},{6,2},{7,3},{8,12},{9,13},{10,... | collective-permute-start | bytes 393224 | tf_op jit(solution)/shard_map/send_3_late/ppermute | solution.py:33
  89.9 2.1 %collective-permute-done.30.recv_in = f32[2,64,384]{2,1,0:T(8,128)S(1)} collective-permute-done((f32[2,64,384]{2,1,0:T(8,128)S(1)}, f32[2,64,384]{2,1,0:T(8,128)S(1)}, u32[]{:S(2)}, u32[]{:S(2)}) %collective-permute-start.30) | collective-permute-done | bytes 196640 | tf_op jit(solution)/shard_map/send_0_6/ppermute | solution.py:33
  94.4 1.9 %collective-permute-start.35 = (f32[2,32,256]{2,1,0:T(8,128)S(1)}, f32[2,32,256]{2,1,0:T(8,128)S(1)}, u32[]{:S(2)}, u32[]{:S(2)}) collective-permute-start(f32[2,32,256]{2,1,0:T(8,128)S(1)} %get-tuple-element.318), channel_id=1, source_target_pairs={{0,4},{1,5},{2,6},{3,7},{4,0},{5,1},{6,2},{7,3},{8,12},{9,13},{10,... | collective-permute-start | bytes 196616 | tf_op jit(solution)/shard_map/send_4_late/ppermute | solution.py:33
  96.7 2.3 %collective-permute-start.36 = (f32[2,64,512]{2,1,0:T(8,128)S(1)}, f32[2,64,512]{2,1,0:T(8,128)S(1)}, u32[]{:S(2)}, u32[]{:S(2)}) collective-permute-start(f32[2,64,512]{2,1,0:T(8,128)S(1)} %get-tuple-element.321), channel_id=1, source_target_pairs={{0,1},{1,0},{2,3},{3,2},{4,5},{5,4},{6,7},{7,6},{8,9},{9,8},{10,11... | collective-permute-start | bytes 786440 | tf_op jit(solution)/shard_map/send_3_5/ppermute | solution.py:33
  99.9 1.9 %collective-permute-start.38 = (f32[2,64,384]{2,1,0:T(8,128)S(1)}, f32[2,64,384]{2,1,0:T(8,128)S(1)}, u32[]{:S(2)}, u32[]{:S(2)}) collective-permute-start(f32[2,64,384]{2,1,0:T(8,128)S(1)} %get-tuple-element.327), channel_id=1, source_target_pairs={{0,4},{1,5},{2,6},{3,7},{4,0},{5,1},{6,2},{7,3},{8,12},{9,13},{10,... | collective-permute-start | bytes 589832 | tf_op jit(solution)/shard_map/send_1_7/ppermute | solution.py:33
  101.8 5.0 %collective-permute-done.34.recv_in = f32[2,64,384]{2,1,0:T(8,128)S(1)} collective-permute-done((f32[2,64,384]{2,1,0:T(8,128)S(1)}, f32[2,64,384]{2,1,0:T(8,128)S(1)}, u32[]{:S(2)}, u32[]{:S(2)}) %collective-permute-start.34) | collective-permute-done | bytes 196640 | tf_op jit(solution)/shard_map/send_0_7/ppermute | solution.py:33
  110.0 2.0 %collective-permute-done.37.recv_in = f32[2,64,512]{2,1,0:T(8,128)S(1)} collective-permute-done((f32[2,64,512]{2,1,0:T(8,128)S(1)}, f32[2,64,512]{2,1,0:T(8,128)S(1)}, u32[]{:S(2)}, u32[]{:S(2)}) %collective-permute-start.37) | collective-permute-done | bytes 262176 | tf_op jit(solution)/shard_map/send_2_6/ppermute | solution.py:33
  118.6 4.1 %collective-permute-done.40.recv_in = f32[2,64,512]{2,1,0:T(8,128)S(1)} collective-permute-done((f32[2,64,512]{2,1,0:T(8,128)S(1)}, f32[2,64,512]{2,1,0:T(8,128)S(1)}, u32[]{:S(2)}, u32[]{:S(2)}) %collective-permute-start.40) | collective-permute-done | bytes 262176 | tf_op jit(solution)/shard_map/send_3_6/ppermute | solution.py:33
  123.2 3.3 %collective-permute-done.41.recv_in = f32[2,64,512]{2,1,0:T(8,128)S(1)} collective-permute-done((f32[2,64,512]{2,1,0:T(8,128)S(1)}, f32[2,64,512]{2,1,0:T(8,128)S(1)}, u32[]{:S(2)}, u32[]{:S(2)}) %collective-permute-start.41) | collective-permute-done | bytes 262176 | tf_op jit(solution)/shard_map/send_2_7/ppermute | solution.py:33
  129.1 7.6 %collective-permute-done.43.recv_in = f32[2,64,512]{2,1,0:T(8,128)S(1)} collective-permute-done((f32[2,64,512]{2,1,0:T(8,128)S(1)}, f32[2,64,512]{2,1,0:T(8,128)S(1)}, u32[]{:S(2)}, u32[]{:S(2)}) %collective-permute-start.43) | collective-permute-done | bytes 262176 | tf_op jit(solution)/shard_map/send_3_7/ppermute | solution.py:33
  (145 shorter events, 68.2 us)
Async XLA Ops:
  11.5 9.6 %collective-permute-start.3 = (f32[2,64,512]{2,1,0:T(8,128)S(1)}, f32[2,64,512]{2,1,0:T(8,128)S(1)}, u32[]{:S(2)}, u32[]{:S(2)}) collective-permute-start(f32[2,64,512]{2,1,0:T(8,128)S(1)} %get-tuple-element.193), channel_id=1, source_target_pairs={{0,16},{8,24},{16,0},{24,8},{1,17},{9,25},{17,1},{25,9},{2,18},{10... | collective-permute-start | bytes 786440 | tf_op jit(solution)/shard_map/send_2_0/ppermute | solution.py:33
  13.9 12.8 %collective-permute-start.6 = (f32[2,64,512]{2,1,0:T(8,128)S(1)}, f32[2,64,512]{2,1,0:T(8,128)S(1)}, u32[]{:S(2)}, u32[]{:S(2)}) collective-permute-start(f32[2,64,512]{2,1,0:T(8,128)S(1)} %get-tuple-element.203), channel_id=1, source_target_pairs={{0,16},{8,24},{16,0},{24,8},{1,17},{9,25},{17,1},{25,9},{2,18},{10... | collective-permute-start | bytes 786440 | tf_op jit(solution)/shard_map/send_3_0/ppermute | solution.py:33
  14.0 20.3 %collective-permute-start.10 = (f32[2,64,256]{2,1,0:T(8,128)S(1)}, f32[2,64,256]{2,1,0:T(8,128)S(1)}, u32[]{:S(2)}, u32[]{:S(2)}) collective-permute-start(f32[2,64,256]{2,1,0:T(8,128)S(1)} %get-tuple-element.217), channel_id=1, source_target_pairs={{0,16},{8,24},{16,0},{24,8},{1,17},{9,25},{17,1},{25,9},{2,18},{10... | collective-permute-start | bytes 393224 | tf_op jit(solution)/shard_map/send_4_0/ppermute | solution.py:33
  31.7 10.1 %collective-permute-start.14 = (f32[2,40,384]{2,1,0:T(8,128)S(1)}, f32[2,40,384]{2,1,0:T(8,128)S(1)}, u32[]{:S(2)}, u32[]{:S(2)}) collective-permute-start(f32[2,40,384]{2,1,0:T(8,128)S(1)} %get-tuple-element.228), channel_id=1, source_target_pairs={{0,4},{1,5},{2,6},{3,7},{4,0},{5,1},{6,2},{7,3},{8,12},{9,13},{10,... | collective-permute-start | bytes 368648 | tf_op jit(solution)/shard_map/send_0_4/ppermute | solution.py:33
  37.1 11.3 %collective-permute-start.17 = (f32[2,64,512]{2,1,0:T(8,128)S(1)}, f32[2,64,512]{2,1,0:T(8,128)S(1)}, u32[]{:S(2)}, u32[]{:S(2)}) collective-permute-start(f32[2,64,512]{2,1,0:T(8,128)S(1)} %get-tuple-element.237), channel_id=1, source_target_pairs={{0,2},{1,3},{2,0},{3,1},{4,6},{5,7},{6,4},{7,5},{8,10},{9,11},{10,... | collective-permute-start | bytes 786440 | tf_op jit(solution)/shard_map/send_2_3/ppermute | solution.py:33
  39.6 11.1 %collective-permute-start.18 = (f32[2,32,384]{2,1,0:T(8,128)S(1)}, f32[2,32,384]{2,1,0:T(8,128)S(1)}, u32[]{:S(2)}, u32[]{:S(2)}) collective-permute-start(f32[2,32,384]{2,1,0:T(8,128)S(1)} %get-tuple-element.239), channel_id=1, source_target_pairs={{0,4},{1,5},{2,6},{3,7},{4,0},{5,1},{6,2},{7,3},{8,12},{9,13},{10,... | collective-permute-start | bytes 294920 | tf_op jit(solution)/shard_map/send_1_4/ppermute | solution.py:33
  44.5 12.3 %collective-permute-start.20 = (f32[2,64,512]{2,1,0:T(8,128)S(1)}, f32[2,64,512]{2,1,0:T(8,128)S(1)}, u32[]{:S(2)}, u32[]{:S(2)}) collective-permute-start(f32[2,64,512]{2,1,0:T(8,128)S(1)} %get-tuple-element.245), channel_id=1, source_target_pairs={{0,2},{1,3},{2,0},{3,1},{4,6},{5,7},{6,4},{7,5},{8,10},{9,11},{10,... | collective-permute-start | bytes 786440 | tf_op jit(solution)/shard_map/send_3_3/ppermute | solution.py:33
  57.2 12.1 %collective-permute-start.23 = (f32[2,32,512]{2,1,0:T(8,128)S(1)}, f32[2,32,512]{2,1,0:T(8,128)S(1)}, u32[]{:S(2)}, u32[]{:S(2)}) collective-permute-start(f32[2,32,512]{2,1,0:T(8,128)S(1)} %get-tuple-element.258), channel_id=1, source_target_pairs={{0,4},{1,5},{2,6},{3,7},{4,0},{5,1},{6,2},{7,3},{8,12},{9,13},{10,... | collective-permute-start | bytes 393224 | tf_op jit(solution)/shard_map/send_3_4/ppermute | solution.py:33
  59.4 12.4 %collective-permute-start.24 = (f32[2,32,256]{2,1,0:T(8,128)S(1)}, f32[2,32,256]{2,1,0:T(8,128)S(1)}, u32[]{:S(2)}, u32[]{:S(2)}) collective-permute-start(f32[2,32,256]{2,1,0:T(8,128)S(1)} %get-tuple-element.261), channel_id=1, source_target_pairs={{0,4},{1,5},{2,6},{3,7},{4,0},{5,1},{6,2},{7,3},{8,12},{9,13},{10,... | collective-permute-start | bytes 196616 | tf_op jit(solution)/shard_map/send_4_4/ppermute | solution.py:33
  63.6 10.1 %collective-permute-start.25 = (f32[2,32,384]{2,1,0:T(8,128)S(1)}, f32[2,32,384]{2,1,0:T(8,128)S(1)}, u32[]{:S(2)}, u32[]{:S(2)}) collective-permute-start(f32[2,32,384]{2,1,0:T(8,128)S(1)} %get-tuple-element.274), channel_id=1, source_target_pairs={{0,4},{1,5},{2,6},{3,7},{4,0},{5,1},{6,2},{7,3},{8,12},{9,13},{10,... | collective-permute-start | bytes 294920 | tf_op jit(solution)/shard_map/send_0_late/ppermute | solution.py:33
  76.1 10.7 %collective-permute-start.28 = (f32[2,32,512]{2,1,0:T(8,128)S(1)}, f32[2,32,512]{2,1,0:T(8,128)S(1)}, u32[]{:S(2)}, u32[]{:S(2)}) collective-permute-start(f32[2,32,512]{2,1,0:T(8,128)S(1)} %get-tuple-element.290), channel_id=1, source_target_pairs={{0,4},{1,5},{2,6},{3,7},{4,0},{5,1},{6,2},{7,3},{8,12},{9,13},{10,... | collective-permute-start | bytes 393224 | tf_op jit(solution)/shard_map/send_2_late/ppermute | solution.py:33
  84.5 11.8 %collective-permute-start.31 = (f32[2,32,512]{2,1,0:T(8,128)S(1)}, f32[2,32,512]{2,1,0:T(8,128)S(1)}, u32[]{:S(2)}, u32[]{:S(2)}) collective-permute-start(f32[2,32,512]{2,1,0:T(8,128)S(1)} %get-tuple-element.303), channel_id=1, source_target_pairs={{0,4},{1,5},{2,6},{3,7},{4,0},{5,1},{6,2},{7,3},{8,12},{9,13},{10,... | collective-permute-start | bytes 393224 | tf_op jit(solution)/shard_map/send_3_late/ppermute | solution.py:33
  87.2 11.8 %collective-permute-start.32 = (f32[2,64,512]{2,1,0:T(8,128)S(1)}, f32[2,64,512]{2,1,0:T(8,128)S(1)}, u32[]{:S(2)}, u32[]{:S(2)}) collective-permute-start(f32[2,64,512]{2,1,0:T(8,128)S(1)} %get-tuple-element.306), channel_id=1, source_target_pairs={{0,1},{1,0},{2,3},{3,2},{4,5},{5,4},{6,7},{7,6},{8,9},{9,8},{10,11... | collective-permute-start | bytes 786440 | tf_op jit(solution)/shard_map/send_2_5/ppermute | solution.py:33
  88.2 11.3 %collective-permute-start.33 = (f32[2,64,384]{2,1,0:T(8,128)S(1)}, f32[2,64,384]{2,1,0:T(8,128)S(1)}, u32[]{:S(2)}, u32[]{:S(2)}) collective-permute-start(f32[2,64,384]{2,1,0:T(8,128)S(1)} %get-tuple-element.309), channel_id=1, source_target_pairs={{0,2},{1,3},{2,0},{3,1},{4,6},{5,7},{6,4},{7,5},{8,10},{9,11},{10,... | collective-permute-start | bytes 589832 | tf_op jit(solution)/shard_map/send_1_6/ppermute | solution.py:33
  93.3 13.5 %collective-permute-start.34 = (f32[2,64,384]{2,1,0:T(8,128)S(1)}, f32[2,64,384]{2,1,0:T(8,128)S(1)}, u32[]{:S(2)}, u32[]{:S(2)}) collective-permute-start(f32[2,64,384]{2,1,0:T(8,128)S(1)} %get-tuple-element.314), channel_id=1, source_target_pairs={{0,4},{1,5},{2,6},{3,7},{4,0},{5,1},{6,2},{7,3},{8,12},{9,13},{10,... | collective-permute-start | bytes 589832 | tf_op jit(solution)/shard_map/send_0_7/ppermute | solution.py:33
  94.4 13.8 %collective-permute-start.35 = (f32[2,32,256]{2,1,0:T(8,128)S(1)}, f32[2,32,256]{2,1,0:T(8,128)S(1)}, u32[]{:S(2)}, u32[]{:S(2)}) collective-permute-start(f32[2,32,256]{2,1,0:T(8,128)S(1)} %get-tuple-element.318), channel_id=1, source_target_pairs={{0,4},{1,5},{2,6},{3,7},{4,0},{5,1},{6,2},{7,3},{8,12},{9,13},{10,... | collective-permute-start | bytes 196616 | tf_op jit(solution)/shard_map/send_4_late/ppermute | solution.py:33
  96.7 12.9 %collective-permute-start.36 = (f32[2,64,512]{2,1,0:T(8,128)S(1)}, f32[2,64,512]{2,1,0:T(8,128)S(1)}, u32[]{:S(2)}, u32[]{:S(2)}) collective-permute-start(f32[2,64,512]{2,1,0:T(8,128)S(1)} %get-tuple-element.321), channel_id=1, source_target_pairs={{0,1},{1,0},{2,3},{3,2},{4,5},{5,4},{6,7},{7,6},{8,9},{9,8},{10,11... | collective-permute-start | bytes 786440 | tf_op jit(solution)/shard_map/send_3_5/ppermute | solution.py:33
  99.4 12.7 %collective-permute-start.37 = (f32[2,64,512]{2,1,0:T(8,128)S(1)}, f32[2,64,512]{2,1,0:T(8,128)S(1)}, u32[]{:S(2)}, u32[]{:S(2)}) collective-permute-start(f32[2,64,512]{2,1,0:T(8,128)S(1)} %get-tuple-element.324), channel_id=1, source_target_pairs={{0,2},{1,3},{2,0},{3,1},{4,6},{5,7},{6,4},{7,5},{8,10},{9,11},{10,... | collective-permute-start | bytes 786440 | tf_op jit(solution)/shard_map/send_2_6/ppermute | solution.py:33
  99.9 15.8 %collective-permute-start.38 = (f32[2,64,384]{2,1,0:T(8,128)S(1)}, f32[2,64,384]{2,1,0:T(8,128)S(1)}, u32[]{:S(2)}, u32[]{:S(2)}) collective-permute-start(f32[2,64,384]{2,1,0:T(8,128)S(1)} %get-tuple-element.327), channel_id=1, source_target_pairs={{0,4},{1,5},{2,6},{3,7},{4,0},{5,1},{6,2},{7,3},{8,12},{9,13},{10,... | collective-permute-start | bytes 589832 | tf_op jit(solution)/shard_map/send_1_7/ppermute | solution.py:33
  110.0 12.7 %collective-permute-start.40 = (f32[2,64,512]{2,1,0:T(8,128)S(1)}, f32[2,64,512]{2,1,0:T(8,128)S(1)}, u32[]{:S(2)}, u32[]{:S(2)}) collective-permute-start(f32[2,64,512]{2,1,0:T(8,128)S(1)} %get-tuple-element.334), channel_id=1, source_target_pairs={{0,2},{1,3},{2,0},{3,1},{4,6},{5,7},{6,4},{7,5},{8,10},{9,11},{10,... | collective-permute-start | bytes 786440 | tf_op jit(solution)/shard_map/send_3_6/ppermute | solution.py:33
  112.4 14.1 %collective-permute-start.41 = (f32[2,64,512]{2,1,0:T(8,128)S(1)}, f32[2,64,512]{2,1,0:T(8,128)S(1)}, u32[]{:S(2)}, u32[]{:S(2)}) collective-permute-start(f32[2,64,512]{2,1,0:T(8,128)S(1)} %get-tuple-element.337), channel_id=1, source_target_pairs={{0,4},{1,5},{2,6},{3,7},{4,0},{5,1},{6,2},{7,3},{8,12},{9,13},{10,... | collective-permute-start | bytes 786440 | tf_op jit(solution)/shard_map/send_2_7/ppermute | solution.py:33
  117.5 10.7 %collective-permute-start.42 = (f32[2,64,256]{2,1,0:T(8,128)S(1)}, f32[2,64,256]{2,1,0:T(8,128)S(1)}, u32[]{:S(2)}, u32[]{:S(2)}) collective-permute-start(f32[2,64,256]{2,1,0:T(8,128)S(1)} %get-tuple-element.341), channel_id=1, source_target_pairs={{0,2},{1,3},{2,0},{3,1},{4,6},{5,7},{6,4},{7,5},{8,10},{9,11},{10,... | collective-permute-start | bytes 393224 | tf_op jit(solution)/shard_map/send_4_6/ppermute | solution.py:33
  123.1 13.6 %collective-permute-start.43 = (f32[2,64,512]{2,1,0:T(8,128)S(1)}, f32[2,64,512]{2,1,0:T(8,128)S(1)}, u32[]{:S(2)}, u32[]{:S(2)}) collective-permute-start(f32[2,64,512]{2,1,0:T(8,128)S(1)} %get-tuple-element.344), channel_id=1, source_target_pairs={{0,4},{1,5},{2,6},{3,7},{4,0},{5,1},{6,2},{7,3},{8,12},{9,13},{10,... | collective-permute-start | bytes 786440 | tf_op jit(solution)/shard_map/send_3_7/ppermute | solution.py:33
  128.4 10.0 %collective-permute-start.44 = (f32[2,64,256]{2,1,0:T(8,128)S(1)}, f32[2,64,256]{2,1,0:T(8,128)S(1)}, u32[]{:S(2)}, u32[]{:S(2)}) collective-permute-start(f32[2,64,256]{2,1,0:T(8,128)S(1)} %get-tuple-element.348), channel_id=1, source_target_pairs={{0,4},{1,5},{2,6},{3,7},{4,0},{5,1},{6,2},{7,3},{8,12},{9,13},{10,... | collective-permute-start | bytes 393224 | tf_op jit(solution)/shard_map/send_4_7/ppermute | solution.py:33
  (30 other events, 204.5 us)

commit v5 on v4

--- a/solution.py
+++ b/solution.py
@@ -16,6 +16,7 @@
 LATE_ROWS = 32
 ORDER_ROWS = 8
 TILE = 512
+LEAVING = 256
 
 
 def levels_of(level_count, dev_size):
@@ -79,8 +80,8 @@
     return dot(w[0], z[0]) + (dot(w[0], z[1]) + dot(w[1], z[0]))
 
 
-def tiles(width):
-    step = min(TILE, width)
+def tiles(width, limit=TILE):
+    step = min(limit, width)
     return [slice(at, min(at + step, width)) for at in range(0, width, step)]
 
 
@@ -273,7 +274,7 @@
 def last_kernel(at, turn, w, c, measured_ref, keep_in, recv_in, *rest):
     out_ref, _, tile_ref, left = rest[-4:]
     copies = []
-    for n, cols in enumerate(tiles(keep_in.shape[2])):
+    for n, cols in enumerate(tiles(keep_in.shape[2], LEAVING)):
         z = split(stacked(keep_in[:, :, cols], recv_in[:, :, cols]))
         image = product(c, split(product(w, z)))
         half = image.shape[0] // 2
@@ -410,7 +411,7 @@
             functools.partial(last_kernel, at), ins, args,
             [jax.ShapeDtypeStruct((1, 2, cells, boxes), F32)],
             outs=[pl.BlockSpec(memory_space=pltpu.HBM)], input_output_aliases=aliases,
-            scratch_shapes=[pltpu.VMEM((2, cells, width), F32), pltpu.SemaphoreType.DMA((len(tiles(width)),))],
+            scratch_shapes=[pltpu.VMEM((2, cells, width), F32), pltpu.SemaphoreType.DMA((len(tiles(width, LEAVING)),))],
         )[0]
 
     own, away = {}, {}

time: 142 us -> 142 us (level)
  no operation moved by 1% of the time
where the time goes in v5:
time: 142 us; the launch traced here: 140 us
  starting transfers between devices  56.6 us (40%)
  waiting for transfers between devices  48.7 us (34%)
  Pallas kernels  33 us (23%)
    ppermute x45, starting transfers between devices, swapped(): return lax.ppermute(block, axis, [(i, i ^ 1 << bit) for i in range(count)])  56.6 us
    ppermute x45, waiting for transfers between devices, swapped(): return lax.ppermute(block, axis, [(i, i ^ 1 << bit) for i in range(count)])  48.7 us
    pallas_call x56, Pallas kernels, call(): pl.pallas_call(kernel, in_specs=[anywhere(), *ins], out_specs=[*more.pop(...  28.8 us
    pallas_call x2, Pallas kernels, leaf(): pl.pallas_call(kernel, in_specs=ins, out_specs=[*[whole()] * (2 * len(par...  4.21 us
  transfers between devices with their start and end apart: 45, of which 22 were waited for; matrix products, arithmetic and copies ran while one was open for 0% of the time, Pallas kernels for 21%

profile of v5, /device:TPU:0, one launch (start us, length us, event | category | flops | bytes accessed | tf_op | source)
XLA Modules:
  0.0 139.9 jit_solution(9409443607909112158)
XLA Ops:
  0.0 2.3 %leaf.2 = (f32[2,64,384]{2,1,0:T(8,128)}, f32[2,64,384]{2,1,0:T(8,128)}, f32[8,128]{1,0:T(8,128)}) custom-call(f32[1,2,128,2048]{3,2,1,0:T(8,128)} %refs_0_.1, f32[1,2,128,128]{3,2,1,0:T(8,128)} %refs_1_.1), custom_call_target="tpu_custom_call" | custom-call | flops 1000000000 | bytes 2500000 | tf_op jit(solution)/shard_map/leaf/pallas_call | solution.py:341
  2.4 3.0 %collective-permute-start = (f32[2,64,384]{2,1,0:T(8,128)}, f32[2,64,384]{2,1,0:T(8,128)S(1)}, u32[]{:S(2)}, u32[]{:S(2)}) collective-permute-start(f32[2,64,384]{2,1,0:T(8,128)} %get-tuple-element.183), channel_id=1, source_target_pairs={{0,16},{8,24},{16,0},{24,8},{1,17},{9,25},{17,1},{25,9},{2,18},{10... | collective-permute-start | bytes 589832 | tf_op jit(solution)/shard_map/send_0_0/ppermute | solution.py:34
  6.1 1.9 %leaf.3 = (f32[2,64,384]{2,1,0:T(8,128)S(1)}, f32[2,64,384]{2,1,0:T(8,128)S(1)}, f32[2,64,512]{2,1,0:T(8,128)S(1)}, f32[2,64,512]{2,1,0:T(8,128)S(1)}, f32[2,64,...) custom-call(f32[8,128]{1,0:T(8,128)S(1)} %copy-done.7, ...), custom_call_target="tpu_custom_call" | custom-call | flops 1000000000 | bytes 2500000 | tf_op jit(solution)/shard_map/leaf/pallas_call | solution.py:341
  11.5 2.4 %collective-permute-start.3 = (f32[2,64,512]{2,1,0:T(8,128)S(1)}, f32[2,64,512]{2,1,0:T(8,128)S(1)}, u32[]{:S(2)}, u32[]{:S(2)}) collective-permute-start(f32[2,64,512]{2,1,0:T(8,128)S(1)} %get-tuple-element.193), channel_id=1, source_target_pairs={{0,16},{8,24},{16,0},{24,8},{1,17},{9,25},{17,1},{25,9},{2,18},{10... | collective-permute-start | bytes 786440 | tf_op jit(solution)/shard_map/send_2_0/ppermute | solution.py:34
  14.0 1.9 %collective-permute-start.10 = (f32[2,64,256]{2,1,0:T(8,128)S(1)}, f32[2,64,256]{2,1,0:T(8,128)S(1)}, u32[]{:S(2)}, u32[]{:S(2)}) collective-permute-start(f32[2,64,256]{2,1,0:T(8,128)S(1)} %get-tuple-element.217), channel_id=1, source_target_pairs={{0,16},{8,24},{16,0},{24,8},{1,17},{9,25},{17,1},{25,9},{2,18},{10... | collective-permute-start | bytes 393224 | tf_op jit(solution)/shard_map/send_4_0/ppermute | solution.py:34
  18.4 2.7 %collective-permute-done.3.recv_in = f32[2,64,512]{2,1,0:T(8,128)S(1)} collective-permute-done((f32[2,64,512]{2,1,0:T(8,128)S(1)}, f32[2,64,512]{2,1,0:T(8,128)S(1)}, u32[]{:S(2)}, u32[]{:S(2)}) %collective-permute-start.3) | collective-permute-done | bytes 262176 | tf_op jit(solution)/shard_map/send_2_0/ppermute | solution.py:34
  31.7 2.7 %collective-permute-start.14 = (f32[2,40,384]{2,1,0:T(8,128)S(1)}, f32[2,40,384]{2,1,0:T(8,128)S(1)}, u32[]{:S(2)}, u32[]{:S(2)}) collective-permute-start(f32[2,40,384]{2,1,0:T(8,128)S(1)} %get-tuple-element.228), channel_id=1, source_target_pairs={{0,4},{1,5},{2,6},{3,7},{4,0},{5,1},{6,2},{7,3},{8,12},{9,13},{10,... | collective-permute-start | bytes 368648 | tf_op jit(solution)/shard_map/send_0_4/ppermute | solution.py:34
  39.6 2.2 %collective-permute-start.18 = (f32[2,32,384]{2,1,0:T(8,128)S(1)}, f32[2,32,384]{2,1,0:T(8,128)S(1)}, u32[]{:S(2)}, u32[]{:S(2)}) collective-permute-start(f32[2,32,384]{2,1,0:T(8,128)S(1)} %get-tuple-element.239), channel_id=1, source_target_pairs={{0,4},{1,5},{2,6},{3,7},{4,0},{5,1},{6,2},{7,3},{8,12},{9,13},{10,... | collective-permute-start | bytes 294920 | tf_op jit(solution)/shard_map/send_1_4/ppermute | solution.py:34
  45.7 2.7 %collective-permute-done.17.recv_in = f32[2,64,512]{2,1,0:T(8,128)S(1)} collective-permute-done((f32[2,64,512]{2,1,0:T(8,128)S(1)}, f32[2,64,512]{2,1,0:T(8,128)S(1)}, u32[]{:S(2)}, u32[]{:S(2)}) %collective-permute-start.17) | collective-permute-done | bytes 262176 | tf_op jit(solution)/shard_map/send_2_3/ppermute | solution.py:34
  48.8 1.9 %collective-permute-start.21 = (f32[2,32,512]{2,1,0:T(8,128)S(1)}, f32[2,32,512]{2,1,0:T(8,128)S(1)}, u32[]{:S(2)}, u32[]{:S(2)}) collective-permute-start(f32[2,32,512]{2,1,0:T(8,128)S(1)} %get-tuple-element.247), channel_id=1, source_target_pairs={{0,4},{1,5},{2,6},{3,7},{4,0},{5,1},{6,2},{7,3},{8,12},{9,13},{10,... | collective-permute-start | bytes 393224 | tf_op jit(solution)/shard_map/send_2_4/ppermute | solution.py:34
  51.0 2.6 %collective-permute-start.22 = (f32[2,64,256]{2,1,0:T(8,128)S(1)}, f32[2,64,256]{2,1,0:T(8,128)S(1)}, u32[]{:S(2)}, u32[]{:S(2)}) collective-permute-start(f32[2,64,256]{2,1,0:T(8,128)S(1)} %get-tuple-element.250), channel_id=1, source_target_pairs={{0,2},{1,3},{2,0},{3,1},{4,6},{5,7},{6,4},{7,5},{8,10},{9,11},{10,... | collective-permute-start | bytes 393224 | tf_op jit(solution)/shard_map/send_4_3/ppermute | solution.py:34
  53.6 3.3 %collective-permute-done.20.recv_in = f32[2,64,512]{2,1,0:T(8,128)S(1)} collective-permute-done((f32[2,64,512]{2,1,0:T(8,128)S(1)}, f32[2,64,512]{2,1,0:T(8,128)S(1)}, u32[]{:S(2)}, u32[]{:S(2)}) %collective-permute-start.20) | collective-permute-done | bytes 262176 | tf_op jit(solution)/shard_map/send_3_3/ppermute | solution.py:34
  59.4 3.2 %collective-permute-start.24 = (f32[2,32,256]{2,1,0:T(8,128)S(1)}, f32[2,32,256]{2,1,0:T(8,128)S(1)}, u32[]{:S(2)}, u32[]{:S(2)}) collective-permute-start(f32[2,32,256]{2,1,0:T(8,128)S(1)} %get-tuple-element.261), channel_id=1, source_target_pairs={{0,4},{1,5},{2,6},{3,7},{4,0},{5,1},{6,2},{7,3},{8,12},{9,13},{10,... | collective-permute-start | bytes 196616 | tf_op jit(solution)/shard_map/send_4_4/ppermute | solution.py:34
  63.7 5.6 %collective-permute-done.23.part_ref = f32[2,32,512]{2,1,0:T(8,128)S(1)} collective-permute-done((f32[2,32,512]{2,1,0:T(8,128)S(1)}, f32[2,32,512]{2,1,0:T(8,128)S(1)}, u32[]{:S(2)}, u32[]{:S(2)}) %collective-permute-start.23) | collective-permute-done | bytes 131104 | tf_op jit(solution)/shard_map/send_3_4/ppermute | solution.py:34
  78.2 1.9 %collective-permute-start.29 = (f32[2,64,384]{2,1,0:T(8,128)S(1)}, f32[2,64,384]{2,1,0:T(8,128)S(1)}, u32[]{:S(2)}, u32[]{:S(2)}) collective-permute-start(f32[2,64,384]{2,1,0:T(8,128)S(1)} %get-tuple-element.293), channel_id=1, source_target_pairs={{0,1},{1,0},{2,3},{3,2},{4,5},{5,4},{6,7},{7,6},{8,9},{9,8},{10,11... | collective-permute-start | bytes 589832 | tf_op jit(solution)/shard_map/send_1_5/ppermute | solution.py:34
  84.5 2.3 %collective-permute-start.31 = (f32[2,32,512]{2,1,0:T(8,128)S(1)}, f32[2,32,512]{2,1,0:T(8,128)S(1)}, u32[]{:S(2)}, u32[]{:S(2)}) collective-permute-start(f32[2,32,512]{2,1,0:T(8,128)S(1)} %get-tuple-element.303), channel_id=1, source_target_pairs={{0,4},{1,5},{2,6},{3,7},{4,0},{5,1},{6,2},{7,3},{8,12},{9,13},{10,... | collective-permute-start | bytes 393224 | tf_op jit(solution)/shard_map/send_3_late/ppermute | solution.py:34
  89.9 2.1 %collective-permute-done.30.recv_in = f32[2,64,384]{2,1,0:T(8,128)S(1)} collective-permute-done((f32[2,64,384]{2,1,0:T(8,128)S(1)}, f32[2,64,384]{2,1,0:T(8,128)S(1)}, u32[]{:S(2)}, u32[]{:S(2)}) %collective-permute-start.30) | collective-permute-done | bytes 196640 | tf_op jit(solution)/shard_map/send_0_6/ppermute | solution.py:34
  94.4 1.9 %collective-permute-start.35 = (f32[2,32,256]{2,1,0:T(8,128)S(1)}, f32[2,32,256]{2,1,0:T(8,128)S(1)}, u32[]{:S(2)}, u32[]{:S(2)}) collective-permute-start(f32[2,32,256]{2,1,0:T(8,128)S(1)} %get-tuple-element.318), channel_id=1, source_target_pairs={{0,4},{1,5},{2,6},{3,7},{4,0},{5,1},{6,2},{7,3},{8,12},{9,13},{10,... | collective-permute-start | bytes 196616 | tf_op jit(solution)/shard_map/send_4_late/ppermute | solution.py:34
  96.7 2.3 %collective-permute-start.36 = (f32[2,64,512]{2,1,0:T(8,128)S(1)}, f32[2,64,512]{2,1,0:T(8,128)S(1)}, u32[]{:S(2)}, u32[]{:S(2)}) collective-permute-start(f32[2,64,512]{2,1,0:T(8,128)S(1)} %get-tuple-element.321), channel_id=1, source_target_pairs={{0,1},{1,0},{2,3},{3,2},{4,5},{5,4},{6,7},{7,6},{8,9},{9,8},{10,11... | collective-permute-start | bytes 786440 | tf_op jit(solution)/shard_map/send_3_5/ppermute | solution.py:34
  99.9 1.9 %collective-permute-start.38 = (f32[2,64,384]{2,1,0:T(8,128)S(1)}, f32[2,64,384]{2,1,0:T(8,128)S(1)}, u32[]{:S(2)}, u32[]{:S(2)}) collective-permute-start(f32[2,64,384]{2,1,0:T(8,128)S(1)} %get-tuple-element.327), channel_id=1, source_target_pairs={{0,4},{1,5},{2,6},{3,7},{4,0},{5,1},{6,2},{7,3},{8,12},{9,13},{10,... | collective-permute-start | bytes 589832 | tf_op jit(solution)/shard_map/send_1_7/ppermute | solution.py:34
  101.8 5.0 %collective-permute-done.34.recv_in = f32[2,64,384]{2,1,0:T(8,128)S(1)} collective-permute-done((f32[2,64,384]{2,1,0:T(8,128)S(1)}, f32[2,64,384]{2,1,0:T(8,128)S(1)}, u32[]{:S(2)}, u32[]{:S(2)}) %collective-permute-start.34) | collective-permute-done | bytes 196640 | tf_op jit(solution)/shard_map/send_0_7/ppermute | solution.py:34
  118.8 3.9 %collective-permute-done.40.recv_in = f32[2,64,512]{2,1,0:T(8,128)S(1)} collective-permute-done((f32[2,64,512]{2,1,0:T(8,128)S(1)}, f32[2,64,512]{2,1,0:T(8,128)S(1)}, u32[]{:S(2)}, u32[]{:S(2)}) %collective-permute-start.40) | collective-permute-done | bytes 262176 | tf_op jit(solution)/shard_map/send_3_6/ppermute | solution.py:34
  123.2 4.3 %collective-permute-done.41.recv_in = f32[2,64,512]{2,1,0:T(8,128)S(1)} collective-permute-done((f32[2,64,512]{2,1,0:T(8,128)S(1)}, f32[2,64,512]{2,1,0:T(8,128)S(1)}, u32[]{:S(2)}, u32[]{:S(2)}) %collective-permute-start.41) | collective-permute-done | bytes 262176 | tf_op jit(solution)/shard_map/send_2_7/ppermute | solution.py:34
  129.5 7.2 %collective-permute-done.43.recv_in = f32[2,64,512]{2,1,0:T(8,128)S(1)} collective-permute-done((f32[2,64,512]{2,1,0:T(8,128)S(1)}, f32[2,64,512]{2,1,0:T(8,128)S(1)}, u32[]{:S(2)}, u32[]{:S(2)}) %collective-permute-start.43) | collective-permute-done | bytes 262176 | tf_op jit(solution)/shard_map/send_3_7/ppermute | solution.py:34
  (145 shorter events, 67.9 us)
Async XLA Ops:
  11.5 9.6 %collective-permute-start.3 = (f32[2,64,512]{2,1,0:T(8,128)S(1)}, f32[2,64,512]{2,1,0:T(8,128)S(1)}, u32[]{:S(2)}, u32[]{:S(2)}) collective-permute-start(f32[2,64,512]{2,1,0:T(8,128)S(1)} %get-tuple-element.193), channel_id=1, source_target_pairs={{0,16},{8,24},{16,0},{24,8},{1,17},{9,25},{17,1},{25,9},{2,18},{10... | collective-permute-start | bytes 786440 | tf_op jit(solution)/shard_map/send_2_0/ppermute | solution.py:34
  13.9 12.8 %collective-permute-start.6 = (f32[2,64,512]{2,1,0:T(8,128)S(1)}, f32[2,64,512]{2,1,0:T(8,128)S(1)}, u32[]{:S(2)}, u32[]{:S(2)}) collective-permute-start(f32[2,64,512]{2,1,0:T(8,128)S(1)} %get-tuple-element.203), channel_id=1, source_target_pairs={{0,16},{8,24},{16,0},{24,8},{1,17},{9,25},{17,1},{25,9},{2,18},{10... | collective-permute-start | bytes 786440 | tf_op jit(solution)/shard_map/send_3_0/ppermute | solution.py:34
  14.0 20.3 %collective-permute-start.10 = (f32[2,64,256]{2,1,0:T(8,128)S(1)}, f32[2,64,256]{2,1,0:T(8,128)S(1)}, u32[]{:S(2)}, u32[]{:S(2)}) collective-permute-start(f32[2,64,256]{2,1,0:T(8,128)S(1)} %get-tuple-element.217), channel_id=1, source_target_pairs={{0,16},{8,24},{16,0},{24,8},{1,17},{9,25},{17,1},{25,9},{2,18},{10... | collective-permute-start | bytes 393224 | tf_op jit(solution)/shard_map/send_4_0/ppermute | solution.py:34
  31.7 10.1 %collective-permute-start.14 = (f32[2,40,384]{2,1,0:T(8,128)S(1)}, f32[2,40,384]{2,1,0:T(8,128)S(1)}, u32[]{:S(2)}, u32[]{:S(2)}) collective-permute-start(f32[2,40,384]{2,1,0:T(8,128)S(1)} %get-tuple-element.228), channel_id=1, source_target_pairs={{0,4},{1,5},{2,6},{3,7},{4,0},{5,1},{6,2},{7,3},{8,12},{9,13},{10,... | collective-permute-start | bytes 368648 | tf_op jit(solution)/shard_map/send_0_4/ppermute | solution.py:34
  37.1 11.3 %collective-permute-start.17 = (f32[2,64,512]{2,1,0:T(8,128)S(1)}, f32[2,64,512]{2,1,0:T(8,128)S(1)}, u32[]{:S(2)}, u32[]{:S(2)}) collective-permute-start(f32[2,64,512]{2,1,0:T(8,128)S(1)} %get-tuple-element.237), channel_id=1, source_target_pairs={{0,2},{1,3},{2,0},{3,1},{4,6},{5,7},{6,4},{7,5},{8,10},{9,11},{10,... | collective-permute-start | bytes 786440 | tf_op jit(solution)/shard_map/send_2_3/ppermute | solution.py:34
  39.6 11.1 %collective-permute-start.18 = (f32[2,32,384]{2,1,0:T(8,128)S(1)}, f32[2,32,384]{2,1,0:T(8,128)S(1)}, u32[]{:S(2)}, u32[]{:S(2)}) collective-permute-start(f32[2,32,384]{2,1,0:T(8,128)S(1)} %get-tuple-element.239), channel_id=1, source_target_pairs={{0,4},{1,5},{2,6},{3,7},{4,0},{5,1},{6,2},{7,3},{8,12},{9,13},{10,... | collective-permute-start | bytes 294920 | tf_op jit(solution)/shard_map/send_1_4/ppermute | solution.py:34
  44.5 12.3 %collective-permute-start.20 = (f32[2,64,512]{2,1,0:T(8,128)S(1)}, f32[2,64,512]{2,1,0:T(8,128)S(1)}, u32[]{:S(2)}, u32[]{:S(2)}) collective-permute-start(f32[2,64,512]{2,1,0:T(8,128)S(1)} %get-tuple-element.245), channel_id=1, source_target_pairs={{0,2},{1,3},{2,0},{3,1},{4,6},{5,7},{6,4},{7,5},{8,10},{9,11},{10,... | collective-permute-start | bytes 786440 | tf_op jit(solution)/shard_map/send_3_3/ppermute | solution.py:34
  57.2 12.1 %collective-permute-start.23 = (f32[2,32,512]{2,1,0:T(8,128)S(1)}, f32[2,32,512]{2,1,0:T(8,128)S(1)}, u32[]{:S(2)}, u32[]{:S(2)}) collective-permute-start(f32[2,32,512]{2,1,0:T(8,128)S(1)} %get-tuple-element.258), channel_id=1, source_target_pairs={{0,4},{1,5},{2,6},{3,7},{4,0},{5,1},{6,2},{7,3},{8,12},{9,13},{10,... | collective-permute-start | bytes 393224 | tf_op jit(solution)/shard_map/send_3_4/ppermute | solution.py:34
  59.4 12.4 %collective-permute-start.24 = (f32[2,32,256]{2,1,0:T(8,128)S(1)}, f32[2,32,256]{2,1,0:T(8,128)S(1)}, u32[]{:S(2)}, u32[]{:S(2)}) collective-permute-start(f32[2,32,256]{2,1,0:T(8,128)S(1)} %get-tuple-element.261), channel_id=1, source_target_pairs={{0,4},{1,5},{2,6},{3,7},{4,0},{5,1},{6,2},{7,3},{8,12},{9,13},{10,... | collective-permute-start | bytes 196616 | tf_op jit(solution)/shard_map/send_4_4/ppermute | solution.py:34
  63.6 10.1 %collective-permute-start.25 = (f32[2,32,384]{2,1,0:T(8,128)S(1)}, f32[2,32,384]{2,1,0:T(8,128)S(1)}, u32[]{:S(2)}, u32[]{:S(2)}) collective-permute-start(f32[2,32,384]{2,1,0:T(8,128)S(1)} %get-tuple-element.274), channel_id=1, source_target_pairs={{0,4},{1,5},{2,6},{3,7},{4,0},{5,1},{6,2},{7,3},{8,12},{9,13},{10,... | collective-permute-start | bytes 294920 | tf_op jit(solution)/shard_map/send_0_late/ppermute | solution.py:34
  76.1 10.7 %collective-permute-start.28 = (f32[2,32,512]{2,1,0:T(8,128)S(1)}, f32[2,32,512]{2,1,0:T(8,128)S(1)}, u32[]{:S(2)}, u32[]{:S(2)}) collective-permute-start(f32[2,32,512]{2,1,0:T(8,128)S(1)} %get-tuple-element.290), channel_id=1, source_target_pairs={{0,4},{1,5},{2,6},{3,7},{4,0},{5,1},{6,2},{7,3},{8,12},{9,13},{10,... | collective-permute-start | bytes 393224 | tf_op jit(solution)/shard_map/send_2_late/ppermute | solution.py:34
  78.2 9.6 %collective-permute-start.29 = (f32[2,64,384]{2,1,0:T(8,128)S(1)}, f32[2,64,384]{2,1,0:T(8,128)S(1)}, u32[]{:S(2)}, u32[]{:S(2)}) collective-permute-start(f32[2,64,384]{2,1,0:T(8,128)S(1)} %get-tuple-element.293), channel_id=1, source_target_pairs={{0,1},{1,0},{2,3},{3,2},{4,5},{5,4},{6,7},{7,6},{8,9},{9,8},{10,11... | collective-permute-start | bytes 589832 | tf_op jit(solution)/shard_map/send_1_5/ppermute | solution.py:34
  84.5 11.8 %collective-permute-start.31 = (f32[2,32,512]{2,1,0:T(8,128)S(1)}, f32[2,32,512]{2,1,0:T(8,128)S(1)}, u32[]{:S(2)}, u32[]{:S(2)}) collective-permute-start(f32[2,32,512]{2,1,0:T(8,128)S(1)} %get-tuple-element.303), channel_id=1, source_target_pairs={{0,4},{1,5},{2,6},{3,7},{4,0},{5,1},{6,2},{7,3},{8,12},{9,13},{10,... | collective-permute-start | bytes 393224 | tf_op jit(solution)/shard_map/send_3_late/ppermute | solution.py:34
  87.2 11.8 %collective-permute-start.32 = (f32[2,64,512]{2,1,0:T(8,128)S(1)}, f32[2,64,512]{2,1,0:T(8,128)S(1)}, u32[]{:S(2)}, u32[]{:S(2)}) collective-permute-start(f32[2,64,512]{2,1,0:T(8,128)S(1)} %get-tuple-element.306), channel_id=1, source_target_pairs={{0,1},{1,0},{2,3},{3,2},{4,5},{5,4},{6,7},{7,6},{8,9},{9,8},{10,11... | collective-permute-start | bytes 786440 | tf_op jit(solution)/shard_map/send_2_5/ppermute | solution.py:34
  88.2 11.3 %collective-permute-start.33 = (f32[2,64,384]{2,1,0:T(8,128)S(1)}, f32[2,64,384]{2,1,0:T(8,128)S(1)}, u32[]{:S(2)}, u32[]{:S(2)}) collective-permute-start(f32[2,64,384]{2,1,0:T(8,128)S(1)} %get-tuple-element.309), channel_id=1, source_target_pairs={{0,2},{1,3},{2,0},{3,1},{4,6},{5,7},{6,4},{7,5},{8,10},{9,11},{10,... | collective-permute-start | bytes 589832 | tf_op jit(solution)/shard_map/send_1_6/ppermute | solution.py:34
  93.3 13.5 %collective-permute-start.34 = (f32[2,64,384]{2,1,0:T(8,128)S(1)}, f32[2,64,384]{2,1,0:T(8,128)S(1)}, u32[]{:S(2)}, u32[]{:S(2)}) collective-permute-start(f32[2,64,384]{2,1,0:T(8,128)S(1)} %get-tuple-element.314), channel_id=1, source_target_pairs={{0,4},{1,5},{2,6},{3,7},{4,0},{5,1},{6,2},{7,3},{8,12},{9,13},{10,... | collective-permute-start | bytes 589832 | tf_op jit(solution)/shard_map/send_0_7/ppermute | solution.py:34
  94.4 14.1 %collective-permute-start.35 = (f32[2,32,256]{2,1,0:T(8,128)S(1)}, f32[2,32,256]{2,1,0:T(8,128)S(1)}, u32[]{:S(2)}, u32[]{:S(2)}) collective-permute-start(f32[2,32,256]{2,1,0:T(8,128)S(1)} %get-tuple-element.318), channel_id=1, source_target_pairs={{0,4},{1,5},{2,6},{3,7},{4,0},{5,1},{6,2},{7,3},{8,12},{9,13},{10,... | collective-permute-start | bytes 196616 | tf_op jit(solution)/shard_map/send_4_late/ppermute | solution.py:34
  96.7 13.1 %collective-permute-start.36 = (f32[2,64,512]{2,1,0:T(8,128)S(1)}, f32[2,64,512]{2,1,0:T(8,128)S(1)}, u32[]{:S(2)}, u32[]{:S(2)}) collective-permute-start(f32[2,64,512]{2,1,0:T(8,128)S(1)} %get-tuple-element.321), channel_id=1, source_target_pairs={{0,1},{1,0},{2,3},{3,2},{4,5},{5,4},{6,7},{7,6},{8,9},{9,8},{10,11... | collective-permute-start | bytes 786440 | tf_op jit(solution)/shard_map/send_3_5/ppermute | solution.py:34
  99.4 12.7 %collective-permute-start.37 = (f32[2,64,512]{2,1,0:T(8,128)S(1)}, f32[2,64,512]{2,1,0:T(8,128)S(1)}, u32[]{:S(2)}, u32[]{:S(2)}) collective-permute-start(f32[2,64,512]{2,1,0:T(8,128)S(1)} %get-tuple-element.324), channel_id=1, source_target_pairs={{0,2},{1,3},{2,0},{3,1},{4,6},{5,7},{6,4},{7,5},{8,10},{9,11},{10,... | collective-permute-start | bytes 786440 | tf_op jit(solution)/shard_map/send_2_6/ppermute | solution.py:34
  99.9 15.8 %collective-permute-start.38 = (f32[2,64,384]{2,1,0:T(8,128)S(1)}, f32[2,64,384]{2,1,0:T(8,128)S(1)}, u32[]{:S(2)}, u32[]{:S(2)}) collective-permute-start(f32[2,64,384]{2,1,0:T(8,128)S(1)} %get-tuple-element.327), channel_id=1, source_target_pairs={{0,4},{1,5},{2,6},{3,7},{4,0},{5,1},{6,2},{7,3},{8,12},{9,13},{10,... | collective-permute-start | bytes 589832 | tf_op jit(solution)/shard_map/send_1_7/ppermute | solution.py:34
  110.2 12.5 %collective-permute-start.40 = (f32[2,64,512]{2,1,0:T(8,128)S(1)}, f32[2,64,512]{2,1,0:T(8,128)S(1)}, u32[]{:S(2)}, u32[]{:S(2)}) collective-permute-start(f32[2,64,512]{2,1,0:T(8,128)S(1)} %get-tuple-element.334), channel_id=1, source_target_pairs={{0,2},{1,3},{2,0},{3,1},{4,6},{5,7},{6,4},{7,5},{8,10},{9,11},{10,... | collective-permute-start | bytes 786440 | tf_op jit(solution)/shard_map/send_3_6/ppermute | solution.py:34
  112.4 15.0 %collective-permute-start.41 = (f32[2,64,512]{2,1,0:T(8,128)S(1)}, f32[2,64,512]{2,1,0:T(8,128)S(1)}, u32[]{:S(2)}, u32[]{:S(2)}) collective-permute-start(f32[2,64,512]{2,1,0:T(8,128)S(1)} %get-tuple-element.337), channel_id=1, source_target_pairs={{0,4},{1,5},{2,6},{3,7},{4,0},{5,1},{6,2},{7,3},{8,12},{9,13},{10,... | collective-permute-start | bytes 786440 | tf_op jit(solution)/shard_map/send_2_7/ppermute | solution.py:34
  117.7 11.4 %collective-permute-start.42 = (f32[2,64,256]{2,1,0:T(8,128)S(1)}, f32[2,64,256]{2,1,0:T(8,128)S(1)}, u32[]{:S(2)}, u32[]{:S(2)}) collective-permute-start(f32[2,64,256]{2,1,0:T(8,128)S(1)} %get-tuple-element.341), channel_id=1, source_target_pairs={{0,2},{1,3},{2,0},{3,1},{4,6},{5,7},{6,4},{7,5},{8,10},{9,11},{10,... | collective-permute-start | bytes 393224 | tf_op jit(solution)/shard_map/send_4_6/ppermute | solution.py:34
  123.1 13.6 %collective-permute-start.43 = (f32[2,64,512]{2,1,0:T(8,128)S(1)}, f32[2,64,512]{2,1,0:T(8,128)S(1)}, u32[]{:S(2)}, u32[]{:S(2)}) collective-permute-start(f32[2,64,512]{2,1,0:T(8,128)S(1)} %get-tuple-element.344), channel_id=1, source_target_pairs={{0,4},{1,5},{2,6},{3,7},{4,0},{5,1},{6,2},{7,3},{8,12},{9,13},{10,... | collective-permute-start | bytes 786440 | tf_op jit(solution)/shard_map/send_3_7/ppermute | solution.py:34
  (30 other events, 203.8 us)
